TPU v7x, 32 devices: a whole 2x2x4 slice. The times are simulated.
32 devices in a mesh: space: 16 (over z, x, core), chan: 2 (over y).
Axes of the slice: x: 2, y: 2, z: 4, core: 2. Of those that a mesh axis runs over, the one named last changes fastest.
Arguments:
- volume: bfloat16 [64, 16, 48, 128], P('chan', 'space'), may hold values from -6 to 6
- weight: bfloat16 [64, 64, 3, 3, 3], P('chan'), may hold values from -0.15625 to 0.15625
- bias: float32 [64], P('chan'), may hold values from -3 to 3
- upstream: bfloat16 [64, 16, 48, 128], P('chan', 'space'), may hold values from -6 to 6
Outputs:
- activated: bfloat16 [64, 16, 48, 128], P('chan', 'space')
- input_grad: bfloat16 [64, 16, 48, 128], P('chan', 'space')
- weight_grad: float32 [64, 64, 3, 3, 3], P('chan')
- bias_grad: float32 [64], P('chan')
All inputs are finite; a program needn't handle non-finite values.
Results may differ from a plain program's by a relative error of at most 0.008.
Values may be sent and summed in bfloat16 or wider, within the bound.
No kernel may reach another device: no remote copies, remote signals or barrier semaphores. Data moves between devices by JAX's collectives and lax.ppermute only.
A program may use at most 64 MiB of HBM per device.

v0:
```python
import functools
import math

import jax
import jax.numpy as jnp
from jax import lax
from jax.experimental import pallas as pl
from jax.experimental.pallas import tpu as pltpu
from jax.sharding import PartitionSpec as P

leakage = 0.1
bf16 = jnp.bfloat16
f32 = jnp.float32
LIMIT = 48 * 1024 * 1024


def call(body, out_shape, scratch, flops, nbytes, trans=0, name=None):
    return pl.pallas_call(
        body,
        out_shape=out_shape,
        scratch_shapes=scratch,
        compiler_params=pltpu.CompilerParams(vmem_limit_bytes=LIMIT),
        cost_estimate=pl.CostEstimate(
            flops=flops, bytes_accessed=nbytes, transcendentals=trans
        ),
        name=name,
    )


def shape(*dims, dtype=bf16):
    return jax.ShapeDtypeStruct(dims, dtype)


def tap(a, b, c):
    return (a * 3 + b) * 3 + c


def pack_body(nchan, rows, height, *refs):
    vol, up, w, bias, v_own, u_own = refs[:6]
    v_out = refs[6 : 6 + nchan - 1]
    u_out = refs[6 + nchan - 1 : 6 + 2 * (nchan - 1)]
    flat, vt, ut = refs[6 + 2 * (nchan - 1) :]
    share = vol.shape[0]
    part = lax.axis_index("chan")
    zero = jnp.zeros((2, share, 128), bf16)
    for src, dst, rim in ((vol, vt, 2), (up, ut, 1)):
        flat[...] = src[...].astype(f32).reshape(share * height, 128)
        dst[0:rim] = zero[:rim]
        dst[height + rim : height + 2 * rim] = zero[:rim]
        for h in range(height):
            dst[h + rim] = flat[pl.ds(h, share, stride=height)].astype(bf16)
    lane = lax.broadcasted_iota(jnp.int32, (share, 64), 1)
    b = bias[...]
    b0 = b.astype(bf16).astype(f32)
    b1 = (b - b0).astype(bf16).astype(f32)
    b2 = b - b0 - b1
    pieces = jnp.where(
        lane == 0, b0, jnp.where(lane == 1, b1, jnp.where(lane == 2, b2, 0.0))
    )
    none = jnp.zeros((share, 64), f32)
    packed = []
    for c in range(3):
        for j in range(5):
            halves = []
            for t in (2 * j, 2 * j + 1):
                if t < 9:
                    halves.append(w[tap(t % 3, t // 3, c)].astype(f32))
                else:
                    halves.append(pieces if c == 1 else none)
            packed.append(jnp.concatenate(halves, axis=1).astype(bf16))
    v_own[...] = vt[pl.ds(part * rows, rows + 4)]
    u_own[0 : rows + 2] = ut[pl.ds(part * rows, rows + 2)]
    for n, value in enumerate(packed):
        u_own[rows + 2 + n] = value
    for k in range(1, nchan):
        other = lax.rem(part + k, nchan)
        v_out[k - 1][...] = vt[pl.ds(other * rows, rows + 4)]
        u_out[k - 1][0 : rows + 2] = ut[pl.ds(other * rows, rows + 2)]
        for n, value in enumerate(packed):
            u_out[k - 1][rows + 2 + n] = value


def filters_body(nchan, rows, *refs):
    own = refs[0]
    got = refs[1:nchan]
    forward, backward = refs[nchan : nchan + 2]
    wall, turned = refs[nchan + 2 :]
    share = own.shape[1]
    part = lax.axis_index("chan")
    wall[part] = own[rows + 2 :]
    for k in range(1, nchan):
        wall[lax.rem(part + nchan - k, nchan)] = got[k - 1][rows + 2 :]
    full = nchan * share
    for c in range(3):
        for j in range(5):
            block = wall[:, c * 5 + j].reshape(full, 128)
            forward[c * full : (c + 1) * full, j * 128 : (j + 1) * 128] = block
    turned[...] = jnp.zeros_like(turned)
    for b in range(3):
        for a in range(3):
            s = b * 3 + a
            t = (2 - b) * 3 + (2 - a)
            for c in range(3):
                block = wall[:, (2 - c) * 5 + t // 2].reshape(full, 128).astype(f32)
                half = block[:, (t % 2) * 64 : (t % 2) * 64 + 64]
                turned[s * 64 : (s + 1) * 64, c * 64 : (c + 1) * 64] = half
    backward[...] = turned[...].T[: 3 * 64].astype(bf16)


def gather_planes(nchan, planes, own, mine, sib, pair):
    part = lax.axis_index("chan")
    even = lax.rem(lax.axis_index("space"), 2) == 0
    at_sib = jnp.where(even, 2, 0)
    at_pair = jnp.where(even, 0, 2)
    for place, blocks in ((1, own), (at_sib, sib), (at_pair, pair)):
        for k in range(nchan):
            planes[:, place, lax.rem(part + nchan - k, nchan)] = blocks[k][...]


def ones_rows(width):
    row = lax.broadcasted_iota(jnp.int32, (64, width), 0)
    return jnp.where(row < 3, 1.0, 0.0).astype(bf16)


def taps_of(planes, r, extra):
    block = planes[r : r + 3].reshape(-1, 128)
    return jnp.concatenate([block, extra], axis=0)


def shift_sum(y, full):
    lane = lax.broadcasted_iota(jnp.int32, (full, 128), 1)
    left = jnp.where(lane == 0, 0.0, pltpu.roll(y[:full], 1, 1))
    right = jnp.where(lane == 127, 0.0, pltpu.roll(y[2 * full :], 127, 1))
    return y[full : 2 * full] + left + right


def forward_body(nchan, rows, *refs):
    own, sib, pair = refs[:nchan], refs[nchan : 2 * nchan], refs[2 * nchan : 3 * nchan]
    ups = refs[3 * nchan : 4 * nchan]
    filters = refs[4 * nchan]
    outs = refs[4 * nchan + 1 : 5 * nchan + 1]
    delta = refs[5 * nchan + 1]
    planes, upstream, activated = refs[5 * nchan + 2 :]
    part = lax.axis_index("chan")
    share = own[0].shape[1]
    full = nchan * share
    gather_planes(nchan, planes, own, None, sib, pair)
    for k in range(nchan):
        upstream[:, lax.rem(part + nchan - k, nchan)] = ups[k][0 : rows + 2]
    extra = ones_rows(128)
    w = filters[...]
    for g in range((rows + 2) // 2):
        rhs = jnp.concatenate(
            [taps_of(planes, 2 * g, extra), taps_of(planes, 2 * g + 1, extra)], axis=1
        )
        y = jnp.dot(w, rhs, preferred_element_type=f32)
        for n in range(2):
            r = 2 * g + n
            v = shift_sum(y[:, n * 128 : (n + 1) * 128], full)
            e = jnp.exp(-jnp.abs(v))
            inv = 1.0 / (1.0 + e)
            sig = jnp.where(v >= 0, 1.0, e) * inv
            u = upstream[r].reshape(full, 128).astype(f32)
            delta[r] = (u * (leakage + (1.0 - leakage) * sig)).astype(bf16)
            if 1 <= r <= rows:
                soft = jnp.maximum(v, 0.0) + jnp.log(1.0 + e)
                act = (leakage * v + (1.0 - leakage) * soft).astype(bf16)
                activated[r - 1] = act.reshape(nchan, share, 128)
    for k in range(nchan):
        outs[k][...] = activated[:, lax.rem(part + k, nchan)]


def wgrad_body(nchan, rows, step, *refs):
    own, sib, pair = refs[:nchan], refs[nchan : 2 * nchan], refs[2 * nchan : 3 * nchan]
    delta = refs[3 * nchan]
    outs = refs[3 * nchan + 1 : 4 * nchan + 1]
    planes, acc = refs[4 * nchan + 1 :]
    part = lax.axis_index("chan")
    share = own[0].shape[1]
    full = nchan * share
    gather_planes(nchan, planes, own, None, sib, pair)
    extra = ones_rows(128)
    lane = lax.broadcasted_iota(jnp.int32, (full, 128), 1)
    total = None
    for g in range(rows // step):
        lhs, rhs = [], []
        for r in range(g * step + 1, (g + 1) * step + 1):
            d = delta[r].astype(f32)
            before = jnp.where(lane == 127, 0.0, pltpu.roll(d, 127, 1))
            after = jnp.where(lane == 0, 0.0, pltpu.roll(d, 1, 1))
            lhs.append(
                jnp.concatenate([before.astype(bf16), delta[r], after.astype(bf16)], axis=0)
            )
            rhs.append(taps_of(planes, r, extra))
        term = lax.dot_general(
            jnp.concatenate(lhs, axis=1),
            jnp.concatenate(rhs, axis=1),
            (((1,), (1,)), ((), ())),
            preferred_element_type=f32,
        )
        total = term if total is None else total + term
    acc[...] = total
    for k in range(nchan):
        q = lax.rem(part + k, nchan)
        for c in range(3):
            outs[k][c * share : (c + 1) * share] = acc[
                pl.ds(pl.multiple_of(c * full + q * share, 8), share)
            ].astype(outs[k].dtype)


def backward_body(nchan, rows, *refs):
    own, sib, pair, filters = refs[:4]
    outs = refs[4 : 4 + nchan]
    planes, result = refs[4 + nchan :]
    part = lax.axis_index("chan")
    share = outs[0].shape[1]
    full = nchan * share
    even = lax.rem(lax.axis_index("space"), 2) == 0
    planes[:, 1] = own[...]
    planes[:, jnp.where(even, 2, 0)] = sib[...]
    planes[:, jnp.where(even, 0, 2)] = pair[...]
    extra = jnp.zeros((64, 128), bf16)
    w = filters[...]
    for g in range(rows // 2):
        rhs = jnp.concatenate(
            [taps_of(planes, 2 * g, extra), taps_of(planes, 2 * g + 1, extra)], axis=1
        )
        y = jnp.dot(w, rhs, preferred_element_type=f32)
        for n in range(2):
            v = shift_sum(y[:, n * 128 : (n + 1) * 128], full)
            result[2 * g + n] = v.astype(bf16).reshape(nchan, share, 128)
    for k in range(nchan):
        outs[k][...] = result[:, lax.rem(part + k, nchan)]


def unpack_body(nchan, rows, height, *refs):
    blocks = refs[:nchan]
    out, flat = refs[nchan:]
    share = out.shape[0]
    part = lax.axis_index("chan")
    size = rows * share
    for k in range(nchan):
        q = lax.rem(part + nchan - k, nchan)
        flat[pl.ds(pl.multiple_of(q * size, 8), size)] = (
            blocks[k][...].astype(f32).reshape(size, 128)
        )
    for ch in range(share):
        out[ch] = flat[pl.ds(ch, height, stride=share)].astype(bf16)


def finish_body(share, factor, a_ref, b_ref, out, bias):
    total = (a_ref[...].astype(f32) + b_ref[...].astype(f32)) * factor
    for a in range(3):
        for b in range(3):
            for c in range(3):
                t = b * 3 + a
                out[tap(a, b, c)] = total[c * share : (c + 1) * share, t * 64 : t * 64 + 64]
    col = total[share : 2 * share, 576:577]
    eye = lax.broadcasted_iota(jnp.int32, (share, share), 0) == lax.broadcasted_iota(
        jnp.int32, (share, share), 1
    )
    bias[...] = jnp.sum(jnp.where(eye, col, 0.0), axis=0, keepdims=True)


def shards(volume, weight, bias, upstream):
    nchan, nspace = lax.axis_size("chan"), lax.axis_size("space")
    share, depth, height, width = volume.shape
    assert depth == 1 and width == 128 and height % nchan == 0
    full = nchan * share
    rows = height // nchan
    factor = 1.0 / math.sqrt(nspace * depth * height * width)
    sib_perm = [(i, i ^ 1) for i in range(nspace)]
    pair_perm = [(i, i + 1) for i in range(1, nspace - 1, 2)]
    pair_perm += [(j, i) for i, j in pair_perm]

    def over_chan(blocks):
        got = []
        for k in range(1, nchan):
            perm = [(i, (i + k) % nchan) for i in range(nchan)]
            got.append(lax.ppermute(blocks[k - 1], "chan", perm))
        return got

    def to_sib(x):
        return lax.ppermute(x, "space", sib_perm)

    def to_pair(x):
        return lax.ppermute(x, "space", pair_perm)

    slabs = jnp.transpose(weight, (2, 3, 4, 0, 1)).reshape(27, share, full)
    block = share * height * width * 2
    v_shape = shape(rows + 4, share, 128)
    u_shape = shape(rows + 17, share, 128)
    packed = call(
        functools.partial(pack_body, nchan, rows, height),
        [v_shape, u_shape] + [v_shape] * (nchan - 1) + [u_shape] * (nchan - 1),
        [
            pltpu.VMEM((share * height, 128), f32),
            pltpu.VMEM((height + 4, share, 128), bf16),
            pltpu.VMEM((height + 2, share, 128), bf16),
        ],
        0,
        4 * block,
        name="pack",
    )(
        volume.reshape(share, height, width),
        upstream.reshape(share, height, width),
        slabs,
        bias.reshape(share, 1),
    )
    v_own, u_own = packed[:2]
    v_out, u_out = packed[2 : 1 + nchan], packed[1 + nchan :]
    v_got = over_chan(v_out)
    u_got = over_chan(u_out)
    mine = [v_own] + v_got
    sib = [to_sib(x) for x in mine]
    pair = [to_pair(x) for x in mine]
    w_forward, w_backward = call(
        functools.partial(filters_body, nchan, rows),
        [shape(3 * full, 640), shape(3 * full, 640)],
        [pltpu.VMEM((nchan, 15, share, 128), bf16), pltpu.VMEM((640, 256), f32)],
        0,
        1 << 20,
        name="filters",
    )(u_own, *u_got)
    planes = pltpu.VMEM((rows + 4, 3, nchan, share, 128), bf16)
    cells = rows * width
    a_shape = shape(rows, share, 128)
    *act, delta = call(
        functools.partial(forward_body, nchan, rows),
        [a_shape] * nchan + [shape(rows + 2, full, 128)],
        [
            planes,
            pltpu.VMEM((rows + 2, nchan, share, 128), bf16),
            pltpu.VMEM((rows, nchan, share, 128), bf16),
        ],
        2 * 27 * full * full * cells,
        6 * block,
        2 * full * cells,
        name="forward",
    )(*mine, *sib, *pair, u_own, *u_got, w_forward)
    d_sib, d_pair = to_sib(delta), to_pair(delta)
    step = 4 if rows % 4 == 0 else 1
    partial = call(
        functools.partial(wgrad_body, nchan, rows, step),
        [shape(3 * share, 640, dtype=f32)] + [shape(3 * share, 640)] * (nchan - 1),
        [planes, pltpu.VMEM((3 * full, 640), f32)],
        2 * 27 * full * full * cells,
        6 * block,
        name="wgrad",
    )(*mine, *sib, *pair, delta)
    act_got = over_chan(act[1:])
    total = partial[0]
    for term in over_chan(partial[1:]):
        total = total + term.astype(f32)
    hop = 1
    while True:
        sent = total.astype(bf16)
        came = lax.ppermute(sent, "space", [(i, i ^ hop) for i in range(nspace)])
        hop *= 2
        if hop >= nspace:
            break
        total = sent.astype(f32) + came.astype(f32)
    ig = call(
        functools.partial(backward_body, nchan, rows),
        [a_shape] * nchan,
        [
            pltpu.VMEM((rows + 2, 3, full, 128), bf16),
            pltpu.VMEM((rows, nchan, share, 128), bf16),
        ],
        2 * 27 * full * full * cells,
        6 * block,
        name="backward",
    )(delta, d_sib, d_pair, w_backward)
    ig_got = over_chan(ig[1:])

    def unpack(blocks, name):
        out = call(
            functools.partial(unpack_body, nchan, rows, height),
            shape(share, height, width),
            [pltpu.VMEM((height * share, 128), f32)],
            0,
            2 * block,
            name=name,
        )(*blocks)
        return out.reshape(share, 1, height, width)

    activated = unpack([act[0]] + act_got, "unpack_activated")
    input_grad = unpack([ig[0]] + ig_got, "unpack_input_grad")
    w_grad, b_grad = call(
        functools.partial(finish_body, share, factor),
        [shape(27, share, full, dtype=f32), shape(1, share, dtype=f32)],
        [],
        0,
        1 << 20,
        name="finish",
    )(sent, came)
    w_grad = jnp.transpose(w_grad.reshape(3, 3, 3, share, full), (3, 4, 0, 1, 2))
    return activated, input_grad, w_grad, b_grad.reshape(share)


def solution(mesh):
    placed = (
        P("chan", "space", None, None),
        P("chan", None, None, None, None),
        P("chan"),
        P("chan", "space", None, None),
    )
    return jax.shard_map(
        shards,
        mesh=mesh,
        in_specs=placed,
        out_specs=(
            P("chan", "space", None, None),
            P("chan", "space", None, None),
            P("chan", None, None, None, None),
            P("chan"),
        ),
        check_vma=False,
    )
```

profile of v0, /device:TPU:0, one launch (start us, length us, event | category | flops | bytes accessed | tf_op | source)
XLA Modules:
  0.0 64.3 jit_solution(4712765355910146754)
XLA Ops:
  1.4 1.0 %copy-done = bf16[32,1,48,128]{3,2,1,0:T(8,128)(2,1)S(1)} copy-done((bf16[32,1,48,128]{3,2,1,0:T(8,128)(2,1)S(1)}, bf16[32,1,48,128]{3,2,1,0:T(8,128)(2,1)}, u32[]{:S(2)}) %copy-start) | copy-done | bytes 393240
  2.4 1.0 %copy-done.1 = bf16[32,1,48,128]{3,2,1,0:T(8,128)(2,1)S(1)} copy-done((bf16[32,1,48,128]{3,2,1,0:T(8,128)(2,1)S(1)}, bf16[32,1,48,128]{3,2,1,0:T(8,128)(2,1)}, u32[]{:S(2)}) %copy-start.1) | copy-done | bytes 393240
  3.4 0.9 %copy-done.2 = bf16[32,64,3,3,3]{1,0,4,3,2:T(8,128)(2,1)S(1)} copy-done((bf16[32,64,3,3,3]{1,0,4,3,2:T(8,128)(2,1)S(1)}, bf16[32,64,3,3,3]{1,0,4,3,2:T(8,128)(2,1)}, u32[]{:S(2)}) %copy-start.2) | copy-done | bytes 110616
  5.0 3.0 %collective-permute-start = (bf16[28,32,128]{2,1,0:T(8,128)(2,1)S(1)}, bf16[28,32,128]{2,1,0:T(8,128)(2,1)S(1)}, u32[]{:S(2)}, u32[]{:S(2)}) collective-permute-start(bf16[28,32,128]{2,1,0:T(8,128)(2,1)S(1)} %get-tuple-element.20), channel_id=1, source_target_pairs={{0,1},{1,0},{2,3},{3,2},{4,5},{5,4},{6,7},{7,6},{8,9},{9,8},{10,11... | collective-permute-start | bytes 688136 | tf_op jit(solution)/shard_map/ppermute | solution.py:280
  8.8 3.3 %collective-permute-start.1 = (bf16[28,32,128]{2,1,0:T(8,128)(2,1)S(1)}, bf16[28,32,128]{2,1,0:T(8,128)(2,1)S(1)}, u32[]{:S(2)}, u32[]{:S(2)}) collective-permute-start(bf16[28,32,128]{2,1,0:T(8,128)(2,1)S(1)} %get-tuple-element.19.refs_0_), channel_id=1, source_target_pairs={{0,2},{2,0},{4,6},{6,4},{8,10},{10,8},{12,14},{14,12},{16,18},{18,... | collective-permute-start | bytes 688136 | tf_op jit(solution)/shard_map/ppermute | solution.py:284
  12.1 2.3 %collective-permute-done.refs_1_ = bf16[28,32,128]{2,1,0:T(8,128)(2,1)S(1)} collective-permute-done((bf16[28,32,128]{2,1,0:T(8,128)(2,1)S(1)}, bf16[28,32,128]{2,1,0:T(8,128)(2,1)S(1)}, u32[]{:S(2)}, u32[]{:S(2)}) %collective-permute-start) | collective-permute-done | bytes 229408 | tf_op jit(solution)/shard_map/ppermute | solution.py:280
  15.1 3.4 %collective-permute-start.2 = (bf16[28,32,128]{2,1,0:T(8,128)(2,1)S(1)}, bf16[28,32,128]{2,1,0:T(8,128)(2,1)S(1)}, u32[]{:S(2)}, u32[]{:S(2)}) collective-permute-start(bf16[28,32,128]{2,1,0:T(8,128)(2,1)S(1)} %collective-permute-done.refs_1_), channel_id=1, source_target_pairs={{0,2},{2,0},{4,6},{6,4},{8,10},{10,8},{12,14},{14,12},{16,18},{18,... | collective-permute-start | bytes 688136 | tf_op jit(solution)/shard_map/ppermute | solution.py:284
  18.6 2.3 %collective-permute-done.5.refs_1_.refs_7_ = bf16[41,32,128]{2,1,0:T(8,128)(2,1)S(1)} collective-permute-done((bf16[41,32,128]{2,1,0:T(8,128)(2,1)S(1)}, bf16[41,32,128]{2,1,0:T(8,128)(2,1)S(1)}, u32[]{:S(2)}, u32[]{:S(2)}) %collective-permute-start.5) | collective-permute-done | bytes 335904 | tf_op jit(solution)/shard_map/ppermute | solution.py:280
  21.2 1.5 %forward.1 = (bf16[24,32,128]{2,1,0:T(8,128)(2,1)S(1)}, bf16[24,32,128]{2,1,0:T(8,128)(2,1)S(1)}, bf16[26,64,128]{2,1,0:T(8,128)(2,1)S(1)}) custom-call(bf16[28,32,128]{2,1,0:T(8,128)(2,1)S(1)} %get-tuple-element.19.refs_0_, bf16[28,32,128]{2,1,0:T(8,128)(2,1)S(1)} %collective-permute-done.refs_1_, bf16[28,32,128]{2,1,0:T(8,128)(2,1)S(1)} %collective-permute-done.1.refs_2_, ...), custom_call_target="tpu_custom_call" | custom-call | flops 679477248 | bytes 2359296 | tf_op jit(solution)/shard_map/forward/pallas_call | solution.py:328
  22.7 1.6 %wgrad.1 = (f32[96,640]{1,0:T(8,128)S(1)}, bf16[96,640]{1,0:T(8,128)(2,1)S(1)}) custom-call(bf16[28,32,128]{2,1,0:T(8,128)(2,1)S(1)} %get-tuple-element.19.refs_0_, bf16[28,32,128]{2,1,0:T(8,128)(2,1)S(1)} %collective-permute-done.refs_1_, bf16[28,32,128]{2,1,0:T(8,128)(2,1)S(1)} %collective-permute-done.1.refs_2_, ...), custom_call_target="tpu_custom_call" | custom-call | flops 679477248 | bytes 2359296 | tf_op jit(solution)/shard_map/wgrad/pallas_call | solution.py:343
  24.3 1.8 %collective-permute-start.10 = (bf16[96,640]{1,0:T(8,128)(2,1)S(1)}, bf16[96,640]{1,0:T(8,128)(2,1)S(1)}, u32[]{:S(2)}, u32[]{:S(2)}) collective-permute-start(bf16[96,640]{1,0:T(8,128)(2,1)S(1)} %get-tuple-element.31), channel_id=1, source_target_pairs={{0,1},{1,0},{2,3},{3,2},{4,5},{5,4},{6,7},{7,6},{8,9},{9,8},{10,11... | collective-permute-start | bytes 368648 | tf_op jit(solution)/shard_map/ppermute | solution.py:280
  26.2 3.1 %collective-permute-done.10 = bf16[96,640]{1,0:T(8,128)(2,1)S(1)} collective-permute-done((bf16[96,640]{1,0:T(8,128)(2,1)S(1)}, bf16[96,640]{1,0:T(8,128)(2,1)S(1)}, u32[]{:S(2)}, u32[]{:S(2)}) %collective-permute-start.10) | collective-permute-done | bytes 122912 | tf_op jit(solution)/shard_map/ppermute | solution.py:280
  29.3 1.6 %collective-permute-start.11 = (bf16[96,640]{1,0:T(8,128)(2,1)S(1)}, bf16[96,640]{1,0:T(8,128)(2,1)S(1)}, u32[]{:S(2)}, u32[]{:S(2)}) collective-permute-start(bf16[96,640]{1,0:T(8,128)(2,1)S(1)} %add_convert_fusion.3), channel_id=1, source_target_pairs={{0,2},{2,0},{4,6},{6,4},{8,10},{10,8},{12,14},{14,12},{16,18},{18,... | collective-permute-start | bytes 368648 | tf_op jit(solution)/shard_map/ppermute | solution.py:358
  31.6 4.9 %collective-permute-start.7 = (bf16[26,64,128]{2,1,0:T(8,128)(2,1)S(1)}, bf16[26,64,128]{2,1,0:T(8,128)(2,1)S(1)}, u32[]{:S(2)}, u32[]{:S(2)}) collective-permute-start(bf16[26,64,128]{2,1,0:T(8,128)(2,1)S(1)} %get-tuple-element.26.refs_0_.refs_6_), channel_id=1, source_target_pairs={{0,2},{2,0},{4,6},{6,4},{8,10},{10,8},{12,14},{14,12},{16,18},{18,... | collective-permute-start | bytes 1277960 | tf_op jit(solution)/shard_map/ppermute | solution.py:284
  36.6 1.3 %collective-permute-start.12 = (bf16[96,640]{1,0:T(8,128)(2,1)S(1)}, bf16[96,640]{1,0:T(8,128)(2,1)S(1)}, u32[]{:S(2)}, u32[]{:S(2)}) collective-permute-start(bf16[96,640]{1,0:T(8,128)(2,1)S(1)} %add_convert_fusion.2), channel_id=1, source_target_pairs={{0,4},{2,6},{4,0},{6,2},{8,12},{10,14},{12,8},{14,10},{16,20},{18,... | collective-permute-start | bytes 368648 | tf_op jit(solution)/shard_map/ppermute | solution.py:358
  37.9 7.9 %collective-permute-done.12 = bf16[96,640]{1,0:T(8,128)(2,1)S(1)} collective-permute-done((bf16[96,640]{1,0:T(8,128)(2,1)S(1)}, bf16[96,640]{1,0:T(8,128)(2,1)S(1)}, u32[]{:S(2)}, u32[]{:S(2)}) %collective-permute-start.12) | collective-permute-done | bytes 122912 | tf_op jit(solution)/shard_map/ppermute | solution.py:358
  45.8 5.7 %collective-permute-start.13 = (bf16[96,640]{1,0:T(8,128)(2,1)S(1)}, bf16[96,640]{1,0:T(8,128)(2,1)S(1)}, u32[]{:S(2)}, u32[]{:S(2)}) collective-permute-start(bf16[96,640]{1,0:T(8,128)(2,1)S(1)} %add_convert_fusion.1), channel_id=1, source_target_pairs={{0,8},{2,10},{4,12},{6,14},{8,0},{10,2},{12,4},{14,6},{16,24},{18,... | collective-permute-start | bytes 368648 | tf_op jit(solution)/shard_map/ppermute | solution.py:358
  51.5 1.6 %collective-permute-start.6 = (bf16[24,32,128]{2,1,0:T(8,128)(2,1)S(1)}, bf16[24,32,128]{2,1,0:T(8,128)(2,1)S(1)}, u32[]{:S(2)}, u32[]{:S(2)}) collective-permute-start(bf16[24,32,128]{2,1,0:T(8,128)(2,1)S(1)} %get-tuple-element.25), channel_id=1, source_target_pairs={{0,1},{1,0},{2,3},{3,2},{4,5},{5,4},{6,7},{7,6},{8,9},{9,8},{10,11... | collective-permute-start | bytes 589832 | tf_op jit(solution)/shard_map/ppermute | solution.py:280
  53.1 1.3 %backward.1 = (bf16[24,32,128]{2,1,0:T(8,128)(2,1)S(1)}, bf16[24,32,128]{2,1,0:T(8,128)(2,1)S(1)}) custom-call(bf16[26,64,128]{2,1,0:T(8,128)(2,1)S(1)} %get-tuple-element.26.refs_0_.refs_6_, bf16[26,64,128]{2,1,0:T(8,128)(2,1)S(1)} %collective-permute-done.7.refs_1_, bf16[26,64,128]{2,1,0:T(8,128)(2,1)S(1)} %collective-permute-done.8.refs_2_, ...), custom_call_target="tpu_custom_call" | custom-call | flops 679477248 | bytes 2359296 | tf_op jit(solution)/shard_map/backward/pallas_call | solution.py:363
  55.0 2.7 %collective-permute-start.14 = (bf16[96,640]{1,0:T(8,128)(2,1)S(1)}, bf16[96,640]{1,0:T(8,128)(2,1)S(1)}, u32[]{:S(2)}, u32[]{:S(2)}) collective-permute-start(bf16[96,640]{1,0:T(8,128)(2,1)S(1)} %add_convert_fusion.a_ref), channel_id=1, source_target_pairs={{0,16},{2,18},{4,20},{6,22},{8,24},{10,26},{12,28},{14,30},{16,0},... | collective-permute-start | bytes 368648 | tf_op jit(solution)/shard_map/ppermute | solution.py:358
  57.6 1.4 %collective-permute-done.6.refs_1_ = bf16[24,32,128]{2,1,0:T(8,128)(2,1)S(1)} collective-permute-done((bf16[24,32,128]{2,1,0:T(8,128)(2,1)S(1)}, bf16[24,32,128]{2,1,0:T(8,128)(2,1)S(1)}, u32[]{:S(2)}, u32[]{:S(2)}) %collective-permute-start.6) | collective-permute-done | bytes 196640 | tf_op jit(solution)/shard_map/ppermute | solution.py:280
  59.0 1.2 %unpack_activated.1 = bf16[32,48,128]{2,1,0:T(8,128)(2,1)} custom-call(bf16[24,32,128]{2,1,0:T(8,128)(2,1)S(1)} %get-tuple-element.24.refs_0_, bf16[24,32,128]{2,1,0:T(8,128)(2,1)S(1)} %collective-permute-done.6.refs_1_), custom_call_target="tpu_custom_call" | custom-call | bytes 786432 | tf_op jit(solution)/shard_map/unpack_activated/pallas_call | solution.py:377
  60.3 1.9 %collective-permute-done.14.b_ref = bf16[96,640]{1,0:T(8,128)(2,1)S(1)} collective-permute-done((bf16[96,640]{1,0:T(8,128)(2,1)S(1)}, bf16[96,640]{1,0:T(8,128)(2,1)S(1)}, u32[]{:S(2)}, u32[]{:S(2)}) %collective-permute-start.14) | collective-permute-done | bytes 122912 | tf_op jit(solution)/shard_map/ppermute | solution.py:358
  63.0 1.2 %unpack_input_grad.1 = bf16[32,48,128]{2,1,0:T(8,128)(2,1)} custom-call(bf16[24,32,128]{2,1,0:T(8,128)(2,1)S(1)} %get-tuple-element.28.refs_0_, bf16[24,32,128]{2,1,0:T(8,128)(2,1)S(1)} %collective-permute-done.9.refs_1_), custom_call_target="tpu_custom_call" | custom-call | bytes 786432 | tf_op jit(solution)/shard_map/unpack_input_grad/pallas_call | solution.py:377
  (27 shorter events, 5.4 us)
Async XLA Ops:
  0.6 0.7 %copy-start.3 = (f32[32]{0:T(128)S(1)}, f32[32]{0:T(128)}, u32[]{:S(2)}) copy-start(f32[32]{0:T(128)} %param.6) | copy-start | bytes 388
  1.4 1.0 %copy-start = (bf16[32,1,48,128]{3,2,1,0:T(8,128)(2,1)S(1)}, bf16[32,1,48,128]{3,2,1,0:T(8,128)(2,1)}, u32[]{:S(2)}) copy-start(bf16[32,1,48,128]{3,2,1,0:T(8,128)(2,1)} %param.4) | copy-start | bytes 1179652
  2.4 1.0 %copy-start.1 = (bf16[32,1,48,128]{3,2,1,0:T(8,128)(2,1)S(1)}, bf16[32,1,48,128]{3,2,1,0:T(8,128)(2,1)}, u32[]{:S(2)}) copy-start(bf16[32,1,48,128]{3,2,1,0:T(8,128)(2,1)} %param.7) | copy-start | bytes 1179652
  3.4 0.9 %copy-start.2 = (bf16[32,64,3,3,3]{1,0,4,3,2:T(8,128)(2,1)S(1)}, bf16[32,64,3,3,3]{1,0,4,3,2:T(8,128)(2,1)}, u32[]{:S(2)}) copy-start(bf16[32,64,3,3,3]{1,0,4,3,2:T(8,128)(2,1)} %param.5) | copy-start | bytes 331780
  5.0 9.5 %collective-permute-start = (bf16[28,32,128]{2,1,0:T(8,128)(2,1)S(1)}, bf16[28,32,128]{2,1,0:T(8,128)(2,1)S(1)}, u32[]{:S(2)}, u32[]{:S(2)}) collective-permute-start(bf16[28,32,128]{2,1,0:T(8,128)(2,1)S(1)} %get-tuple-element.20), channel_id=1, source_target_pairs={{0,1},{1,0},{2,3},{3,2},{4,5},{5,4},{6,7},{7,6},{8,9},{9,8},{10,11... | collective-permute-start | bytes 688136 | tf_op jit(solution)/shard_map/ppermute | solution.py:280
  8.0 12.8 %collective-permute-start.5 = (bf16[41,32,128]{2,1,0:T(8,128)(2,1)S(1)}, bf16[41,32,128]{2,1,0:T(8,128)(2,1)S(1)}, u32[]{:S(2)}, u32[]{:S(2)}) collective-permute-start(bf16[41,32,128]{2,1,0:T(8,128)(2,1)S(1)} %get-tuple-element.22), channel_id=1, source_target_pairs={{0,1},{1,0},{2,3},{3,2},{4,5},{5,4},{6,7},{7,6},{8,9},{9,8},{10,11... | collective-permute-start | bytes 1007624 | tf_op jit(solution)/shard_map/ppermute | solution.py:280
  8.1 13.1 %collective-permute-start.3 = (bf16[28,32,128]{2,1,0:T(8,128)(2,1)S(1)}, bf16[28,32,128]{2,1,0:T(8,128)(2,1)S(1)}, u32[]{:S(2)}, u32[]{:S(2)}) collective-permute-start(bf16[28,32,128]{2,1,0:T(8,128)(2,1)S(1)} %get-tuple-element.19.refs_0_), channel_id=1, source_target_pairs={{2,4},{6,8},{10,12},{14,16},{18,20},{22,24},{26,28},{4,2},{8,6},{1... | collective-permute-start | bytes 688136 | tf_op jit(solution)/shard_map/ppermute | solution.py:287
  8.8 12.4 %collective-permute-start.1 = (bf16[28,32,128]{2,1,0:T(8,128)(2,1)S(1)}, bf16[28,32,128]{2,1,0:T(8,128)(2,1)S(1)}, u32[]{:S(2)}, u32[]{:S(2)}) collective-permute-start(bf16[28,32,128]{2,1,0:T(8,128)(2,1)S(1)} %get-tuple-element.19.refs_0_), channel_id=1, source_target_pairs={{0,2},{2,0},{4,6},{6,4},{8,10},{10,8},{12,14},{14,12},{16,18},{18,... | collective-permute-start | bytes 688136 | tf_op jit(solution)/shard_map/ppermute | solution.py:284
  14.4 6.7 %collective-permute-start.4 = (bf16[28,32,128]{2,1,0:T(8,128)(2,1)S(1)}, bf16[28,32,128]{2,1,0:T(8,128)(2,1)S(1)}, u32[]{:S(2)}, u32[]{:S(2)}) collective-permute-start(bf16[28,32,128]{2,1,0:T(8,128)(2,1)S(1)} %collective-permute-done.refs_1_), channel_id=1, source_target_pairs={{2,4},{6,8},{10,12},{14,16},{18,20},{22,24},{26,28},{4,2},{8,6},{1... | collective-permute-start | bytes 688136 | tf_op jit(solution)/shard_map/ppermute | solution.py:287
  15.1 6.1 %collective-permute-start.2 = (bf16[28,32,128]{2,1,0:T(8,128)(2,1)S(1)}, bf16[28,32,128]{2,1,0:T(8,128)(2,1)S(1)}, u32[]{:S(2)}, u32[]{:S(2)}) collective-permute-start(bf16[28,32,128]{2,1,0:T(8,128)(2,1)S(1)} %collective-permute-done.refs_1_), channel_id=1, source_target_pairs={{0,2},{2,0},{4,6},{6,4},{8,10},{10,8},{12,14},{14,12},{16,18},{18,... | collective-permute-start | bytes 688136 | tf_op jit(solution)/shard_map/ppermute | solution.py:284
  24.3 4.9 %collective-permute-start.10 = (bf16[96,640]{1,0:T(8,128)(2,1)S(1)}, bf16[96,640]{1,0:T(8,128)(2,1)S(1)}, u32[]{:S(2)}, u32[]{:S(2)}) collective-permute-start(bf16[96,640]{1,0:T(8,128)(2,1)S(1)} %get-tuple-element.31), channel_id=1, source_target_pairs={{0,1},{1,0},{2,3},{3,2},{4,5},{5,4},{6,7},{7,6},{8,9},{9,8},{10,11... | collective-permute-start | bytes 368648 | tf_op jit(solution)/shard_map/ppermute | solution.py:280
  29.3 7.2 %collective-permute-start.11 = (bf16[96,640]{1,0:T(8,128)(2,1)S(1)}, bf16[96,640]{1,0:T(8,128)(2,1)S(1)}, u32[]{:S(2)}, u32[]{:S(2)}) collective-permute-start(bf16[96,640]{1,0:T(8,128)(2,1)S(1)} %add_convert_fusion.3), channel_id=1, source_target_pairs={{0,2},{2,0},{4,6},{6,4},{8,10},{10,8},{12,14},{14,12},{16,18},{18,... | collective-permute-start | bytes 368648 | tf_op jit(solution)/shard_map/ppermute | solution.py:358
  30.9 22.2 %collective-permute-start.8 = (bf16[26,64,128]{2,1,0:T(8,128)(2,1)S(1)}, bf16[26,64,128]{2,1,0:T(8,128)(2,1)S(1)}, u32[]{:S(2)}, u32[]{:S(2)}) collective-permute-start(bf16[26,64,128]{2,1,0:T(8,128)(2,1)S(1)} %get-tuple-element.26.refs_0_.refs_6_), channel_id=1, source_target_pairs={{2,4},{6,8},{10,12},{14,16},{18,20},{22,24},{26,28},{4,2},{8,6},{1... | collective-permute-start | bytes 1277960 | tf_op jit(solution)/shard_map/ppermute | solution.py:287
  31.6 21.5 %collective-permute-start.7 = (bf16[26,64,128]{2,1,0:T(8,128)(2,1)S(1)}, bf16[26,64,128]{2,1,0:T(8,128)(2,1)S(1)}, u32[]{:S(2)}, u32[]{:S(2)}) collective-permute-start(bf16[26,64,128]{2,1,0:T(8,128)(2,1)S(1)} %get-tuple-element.26.refs_0_.refs_6_), channel_id=1, source_target_pairs={{0,2},{2,0},{4,6},{6,4},{8,10},{10,8},{12,14},{14,12},{16,18},{18,... | collective-permute-start | bytes 1277960 | tf_op jit(solution)/shard_map/ppermute | solution.py:284
  36.6 9.2 %collective-permute-start.12 = (bf16[96,640]{1,0:T(8,128)(2,1)S(1)}, bf16[96,640]{1,0:T(8,128)(2,1)S(1)}, u32[]{:S(2)}, u32[]{:S(2)}) collective-permute-start(bf16[96,640]{1,0:T(8,128)(2,1)S(1)} %add_convert_fusion.2), channel_id=1, source_target_pairs={{0,4},{2,6},{4,0},{6,2},{8,12},{10,14},{12,8},{14,10},{16,20},{18,... | collective-permute-start | bytes 368648 | tf_op jit(solution)/shard_map/ppermute | solution.py:358
  45.8 9.2 %collective-permute-start.13 = (bf16[96,640]{1,0:T(8,128)(2,1)S(1)}, bf16[96,640]{1,0:T(8,128)(2,1)S(1)}, u32[]{:S(2)}, u32[]{:S(2)}) collective-permute-start(bf16[96,640]{1,0:T(8,128)(2,1)S(1)} %add_convert_fusion.1), channel_id=1, source_target_pairs={{0,8},{2,10},{4,12},{6,14},{8,0},{10,2},{12,4},{14,6},{16,24},{18,... | collective-permute-start | bytes 368648 | tf_op jit(solution)/shard_map/ppermute | solution.py:358
  51.5 7.5 %collective-permute-start.6 = (bf16[24,32,128]{2,1,0:T(8,128)(2,1)S(1)}, bf16[24,32,128]{2,1,0:T(8,128)(2,1)S(1)}, u32[]{:S(2)}, u32[]{:S(2)}) collective-permute-start(bf16[24,32,128]{2,1,0:T(8,128)(2,1)S(1)} %get-tuple-element.25), channel_id=1, source_target_pairs={{0,1},{1,0},{2,3},{3,2},{4,5},{5,4},{6,7},{7,6},{8,9},{9,8},{10,11... | collective-permute-start | bytes 589832 | tf_op jit(solution)/shard_map/ppermute | solution.py:280
  54.4 8.6 %collective-permute-start.9 = (bf16[24,32,128]{2,1,0:T(8,128)(2,1)S(1)}, bf16[24,32,128]{2,1,0:T(8,128)(2,1)S(1)}, u32[]{:S(2)}, u32[]{:S(2)}) collective-permute-start(bf16[24,32,128]{2,1,0:T(8,128)(2,1)S(1)} %get-tuple-element.29), channel_id=1, source_target_pairs={{0,1},{1,0},{2,3},{3,2},{4,5},{5,4},{6,7},{7,6},{8,9},{9,8},{10,11... | collective-permute-start | bytes 589832 | tf_op jit(solution)/shard_map/ppermute | solution.py:280
  55.0 7.2 %collective-permute-start.14 = (bf16[96,640]{1,0:T(8,128)(2,1)S(1)}, bf16[96,640]{1,0:T(8,128)(2,1)S(1)}, u32[]{:S(2)}, u32[]{:S(2)}) collective-permute-start(bf16[96,640]{1,0:T(8,128)(2,1)S(1)} %add_convert_fusion.a_ref), channel_id=1, source_target_pairs={{0,16},{2,18},{4,20},{6,22},{8,24},{10,26},{12,28},{14,30},{16,0},... | collective-permute-start | bytes 368648 | tf_op jit(solution)/shard_map/ppermute | solution.py:358
where the time goes:
time: 64.5 us; the launch traced here: 64.3 us
  starting transfers between devices  32.1 us (50%)
  waiting for transfers between devices  18.9 us (29%)
  Pallas kernels  8.82 us (14%)
  local copies, waits for them, and re-layouts  3.66 us (6%)
  between operations  0.74 us (1%)
    ppermute x3, starting transfers between devices, to_sib(): return lax.ppermute(x, 'space', sib_perm)  11.7 us
    ppermute x4, starting transfers between devices, shards(): came = lax.ppermute(sent, 'space', [(i, i ^ hop) for i in range(nspace)])  11.3 us
    ppermute x4, waiting for transfers between devices, shards(): came = lax.ppermute(sent, 'space', [(i, i ^ hop) for i in range(nspace)])  9.75 us
    ppermute x5, waiting for transfers between devices, over_chan(): got.append(lax.ppermute(blocks[k - 1], 'chan', perm))  9.11 us
    ppermute x5, starting transfers between devices, over_chan(): got.append(lax.ppermute(blocks[k - 1], 'chan', perm))  7.05 us
    unnamed x8, local copies, waits for them, and re-layouts  3.57 us
    pallas_call x2, Pallas kernels, unpack(): call(functools.partial(unpack_body, nchan, rows, height), shape(share, he...  2.49 us
    ppermute x3, starting transfers between devices, to_pair(): return lax.ppermute(x, 'space', pair_perm)  2 us
  transfers between devices with their start and end apart: 15, of which 6 were waited for; matrix products, arithmetic and copies ran while one was open for 0% of the time, Pallas kernels for 6%

commit v1 on v0

--- a/solution.py
+++ b/solution.py
@@ -11,6 +11,15 @@
 leakage = 0.1
 bf16 = jnp.bfloat16
 f32 = jnp.float32
+DBAR = 0
+IBAR = 9
+ABAR = 9
+UBAR = False
+ZHOP = 2
+GBAR = 9
+VWRAP = True
+VWRAP2 = True
+DWRAP = False
 LIMIT = 48 * 1024 * 1024
 
 
@@ -35,22 +44,41 @@
     return (a * 3 + b) * 3 + c
 
 
-def pack_body(nchan, rows, height, *refs):
-    vol, up, w, bias, v_own, u_own = refs[:6]
-    v_out = refs[6 : 6 + nchan - 1]
-    u_out = refs[6 + nchan - 1 : 6 + 2 * (nchan - 1)]
-    flat, vt, ut = refs[6 + 2 * (nchan - 1) :]
-    share = vol.shape[0]
-    part = lax.axis_index("chan")
-    zero = jnp.zeros((2, share, 128), bf16)
-    for src, dst, rim in ((vol, vt, 2), (up, ut, 1)):
-        flat[...] = src[...].astype(f32).reshape(share * height, 128)
-        dst[0:rim] = zero[:rim]
-        dst[height + rim : height + 2 * rim] = zero[:rim]
-        for h in range(height):
-            dst[h + rim] = flat[pl.ds(h, share, stride=height)].astype(bf16)
+def rows_first(src, flat, dst, rim):
+    share, height, _ = src.shape
+    zero = jnp.zeros((rim, share, 128), bf16)
+    flat[...] = src[...].astype(f32).reshape(share * height, 128)
+    dst[0:rim] = zero
+    dst[height + rim : height + 2 * rim] = zero
+    for h in range(height):
+        dst[h + rim] = flat[pl.ds(h, share, stride=height)].astype(bf16)
+
+
+def pack_volume_body(nchan, rows, *refs):
+    vol = refs[0]
+    outs = refs[1 : 1 + nchan]
+    flat, vt = refs[1 + nchan :]
+    part = lax.axis_index("chan")
+    rows_first(vol, flat, vt, 2)
+    for k in range(nchan):
+        outs[k][...] = vt[pl.ds(lax.rem(part + k, nchan) * rows, rows + 4)]
+
+
+def core():
+    return lax.rem(lax.axis_index("space"), 2)
+
+
+def pack_rest_body(nchan, rows, *refs):
+    up, w, bias = refs[:3]
+    outs = refs[3 : 3 + nchan]
+    flat, ut = refs[3 + nchan :]
+    share = up.shape[0]
+    part = lax.axis_index("chan")
+    rows_first(up, flat, ut, 1)
     lane = lax.broadcasted_iota(jnp.int32, (share, 64), 1)
-    b = bias[...]
+    row = lax.broadcasted_iota(jnp.int32, (share, share), 0)
+    col = lax.broadcasted_iota(jnp.int32, (share, share), 1)
+    b = jnp.sum(jnp.where(row == col, bias[...], 0.0), axis=1, keepdims=True)
     b0 = b.astype(bf16).astype(f32)
     b1 = (b - b0).astype(bf16).astype(f32)
     b2 = b - b0 - b1
@@ -58,7 +86,6 @@
         lane == 0, b0, jnp.where(lane == 1, b1, jnp.where(lane == 2, b2, 0.0))
     )
     none = jnp.zeros((share, 64), f32)
-    packed = []
     for c in range(3):
         for j in range(5):
             halves = []
@@ -67,29 +94,20 @@
                     halves.append(w[tap(t % 3, t // 3, c)].astype(f32))
                 else:
                     halves.append(pieces if c == 1 else none)
-            packed.append(jnp.concatenate(halves, axis=1).astype(bf16))
-    v_own[...] = vt[pl.ds(part * rows, rows + 4)]
-    u_own[0 : rows + 2] = ut[pl.ds(part * rows, rows + 2)]
-    for n, value in enumerate(packed):
-        u_own[rows + 2 + n] = value
-    for k in range(1, nchan):
-        other = lax.rem(part + k, nchan)
-        v_out[k - 1][...] = vt[pl.ds(other * rows, rows + 4)]
-        u_out[k - 1][0 : rows + 2] = ut[pl.ds(other * rows, rows + 2)]
-        for n, value in enumerate(packed):
-            u_out[k - 1][rows + 2 + n] = value
+            value = jnp.concatenate(halves, axis=1).astype(bf16)
+            for k in range(nchan):
+                outs[k][rows + 2 + c * 5 + j] = value
+    for k in range(nchan):
+        outs[k][0 : rows + 2] = ut[pl.ds(lax.rem(part + k, nchan) * rows, rows + 2)]
 
 
 def filters_body(nchan, rows, *refs):
-    own = refs[0]
-    got = refs[1:nchan]
-    forward, backward = refs[nchan : nchan + 2]
-    wall, turned = refs[nchan + 2 :]
-    share = own.shape[1]
-    part = lax.axis_index("chan")
-    wall[part] = own[rows + 2 :]
-    for k in range(1, nchan):
-        wall[lax.rem(part + nchan - k, nchan)] = got[k - 1][rows + 2 :]
+    blocks = refs[:nchan]
+    forward, backward, wall, turned = refs[nchan:]
+    share = blocks[0].shape[1]
+    part = lax.axis_index("chan")
+    for k in range(nchan):
+        wall[lax.rem(part + nchan - k, nchan)] = blocks[k][rows + 2 :]
     full = nchan * share
     for c in range(3):
         for j in range(5):
@@ -107,6 +125,11 @@
     backward[...] = turned[...].T[: 3 * 64].astype(bf16)
 
 
+def outermost():
+    at = lax.axis_index("space")
+    return (at == 0) | (at == lax.axis_size("space") - 1)
+
+
 def gather_planes(nchan, planes, own, mine, sib, pair):
     part = lax.axis_index("chan")
     even = lax.rem(lax.axis_index("space"), 2) == 0
@@ -115,6 +138,10 @@
     for place, blocks in ((1, own), (at_sib, sib), (at_pair, pair)):
         for k in range(nchan):
             planes[:, place, lax.rem(part + nchan - k, nchan)] = blocks[k][...]
+
+    @pl.when(outermost())
+    def _():
+        planes[:, at_pair] = jnp.zeros(planes[:, at_pair].shape, bf16)
 
 
 def ones_rows(width):
@@ -173,8 +200,7 @@
 def wgrad_body(nchan, rows, step, *refs):
     own, sib, pair = refs[:nchan], refs[nchan : 2 * nchan], refs[2 * nchan : 3 * nchan]
     delta = refs[3 * nchan]
-    outs = refs[3 * nchan + 1 : 4 * nchan + 1]
-    planes, acc = refs[4 * nchan + 1 :]
+    kept, sent, planes, acc = refs[3 * nchan + 1 :]
     part = lax.axis_index("chan")
     share = own[0].shape[1]
     full = nchan * share
@@ -199,13 +225,15 @@
             preferred_element_type=f32,
         )
         total = term if total is None else total + term
-    acc[...] = total
-    for k in range(nchan):
-        q = lax.rem(part + k, nchan)
-        for c in range(3):
-            outs[k][c * share : (c + 1) * share] = acc[
-                pl.ds(pl.multiple_of(c * full + q * share, 8), share)
-            ].astype(outs[k].dtype)
+    for c in range(3):
+        for q in range(nchan):
+            at = (q * 3 + c) * share
+            acc[at : at + share] = total[c * full + q * share : c * full + (q + 1) * share]
+    half = 3 * share // 2
+    for k in range(nchan):
+        at = lax.rem(part + k, nchan) * 3 * share
+        kept[k] = acc[pl.ds(pl.multiple_of(at + core() * half, 8), half)]
+        sent[k] = acc[pl.ds(pl.multiple_of(at + (1 - core()) * half, 8), half)].astype(bf16)
 
 
 def backward_body(nchan, rows, *refs):
@@ -218,7 +246,13 @@
     even = lax.rem(lax.axis_index("space"), 2) == 0
     planes[:, 1] = own[...]
     planes[:, jnp.where(even, 2, 0)] = sib[...]
-    planes[:, jnp.where(even, 0, 2)] = pair[...]
+    at_pair = jnp.where(even, 0, 2)
+    planes[:, at_pair] = pair[...]
+
+    @pl.when(outermost())
+    def _():
+        planes[:, at_pair] = jnp.zeros(pair.shape, bf16)
+
     extra = jnp.zeros((64, 128), bf16)
     w = filters[...]
     for g in range(rows // 2):
@@ -248,8 +282,11 @@
         out[ch] = flat[pl.ds(ch, height, stride=share)].astype(bf16)
 
 
-def finish_body(share, factor, a_ref, b_ref, out, bias):
-    total = (a_ref[...].astype(f32) + b_ref[...].astype(f32)) * factor
+def finish_body(share, factor, mine, other, out, bias, both):
+    half = 3 * share // 2
+    both[pl.ds(pl.multiple_of(core() * half, 8), half)] = mine[...]
+    both[pl.ds(pl.multiple_of((1 - core()) * half, 8), half)] = other[...]
+    total = both[...] * factor
     for a in range(3):
         for b in range(3):
             for c in range(3):
@@ -262,6 +299,13 @@
     bias[...] = jnp.sum(jnp.where(eye, col, 0.0), axis=0, keepdims=True)
 
 
+def kept_sum(first, others):
+    total = first.astype(f32)
+    for term in others:
+        total = total + term.astype(f32)
+    return total
+
+
 def shards(volume, weight, bias, upstream):
     nchan, nspace = lax.axis_size("chan"), lax.axis_size("space")
     share, depth, height, width = volume.shape
@@ -270,8 +314,16 @@
     rows = height // nchan
     factor = 1.0 / math.sqrt(nspace * depth * height * width)
     sib_perm = [(i, i ^ 1) for i in range(nspace)]
-    pair_perm = [(i, i + 1) for i in range(1, nspace - 1, 2)]
-    pair_perm += [(j, i) for i, j in pair_perm]
+    pairs = [(i, i + 1) for i in range(1, nspace - 1, 2)]
+    pairs += [(j, i) for i, j in pairs]
+    pair_perm = [(i * nchan + c, j * nchan + c) for i, j in pairs for c in range(nchan)]
+    ends = (0, nspace - 1)
+    turn_perm = [
+        (i * nchan + c, i * nchan + (c + 1) % nchan) for i in ends for c in range(nchan)
+    ]
+    wrap_perm = [
+        (i * nchan + c, (nspace - 1 - i) * nchan + c) for i in ends for c in range(nchan)
+    ]
 
     def over_chan(blocks):
         got = []
@@ -283,37 +335,45 @@
     def to_sib(x):
         return lax.ppermute(x, "space", sib_perm)
 
-    def to_pair(x):
-        return lax.ppermute(x, "space", pair_perm)
+    def to_pair(x, wrap):
+        perm = pair_perm + (wrap_perm if wrap else turn_perm)
+        return lax.ppermute(x, ("space", "chan"), perm)
 
     slabs = jnp.transpose(weight, (2, 3, 4, 0, 1)).reshape(27, share, full)
     block = share * height * width * 2
     v_shape = shape(rows + 4, share, 128)
     u_shape = shape(rows + 17, share, 128)
-    packed = call(
-        functools.partial(pack_body, nchan, rows, height),
-        [v_shape, u_shape] + [v_shape] * (nchan - 1) + [u_shape] * (nchan - 1),
+    v_own, *v_out = call(
+        functools.partial(pack_volume_body, nchan, rows),
+        [v_shape] * nchan,
         [
-            pltpu.VMEM((share * height, 128), f32),
-            pltpu.VMEM((height + 4, share, 128), bf16),
-            pltpu.VMEM((height + 2, share, 128), bf16),
+            pltpu.VMEM((share * height, width), f32),
+            pltpu.VMEM((height + 4, share, width), bf16),
         ],
         0,
-        4 * block,
-        name="pack",
-    )(
-        volume.reshape(share, height, width),
-        upstream.reshape(share, height, width),
-        slabs,
-        bias.reshape(share, 1),
-    )
-    v_own, u_own = packed[:2]
-    v_out, u_out = packed[2 : 1 + nchan], packed[1 + nchan :]
+        2 * block,
+        name="pack_volume",
+    )(volume.reshape(share, height, width))
     v_got = over_chan(v_out)
+    own_sib, own_pair = to_sib(v_own), to_pair(v_own, VWRAP)
+    u_own, *u_out = call(
+        functools.partial(pack_rest_body, nchan, rows),
+        [u_shape] * nchan,
+        [
+            pltpu.VMEM((share * height, width), f32),
+            pltpu.VMEM((height + 2, share, width), bf16),
+        ],
+        0,
+        3 * block,
+        name="pack_rest",
+    )(upstream.reshape(share, height, width), slabs, bias.reshape(1, share))
+    if UBAR:
+        u_out, v_got = lax.optimization_barrier((u_out, v_got))
+    v_got, own_sib, own_pair = lax.optimization_barrier((v_got, own_sib, own_pair))
+    mine = [v_own] + v_got
+    sib = [own_sib] + [to_sib(x) for x in v_got]
+    pair = [own_pair] + [to_pair(x, VWRAP2) for x in v_got]
     u_got = over_chan(u_out)
-    mine = [v_own] + v_got
-    sib = [to_sib(x) for x in mine]
-    pair = [to_pair(x) for x in mine]
     w_forward, w_backward = call(
         functools.partial(filters_body, nchan, rows),
         [shape(3 * full, 640), shape(3 * full, 640)],
@@ -338,28 +398,45 @@
         2 * full * cells,
         name="forward",
     )(*mine, *sib, *pair, u_own, *u_got, w_forward)
-    d_sib, d_pair = to_sib(delta), to_pair(delta)
+    d_sib, d_pair = to_sib(delta), to_pair(delta, DWRAP)
     step = 4 if rows % 4 == 0 else 1
-    partial = call(
+    h_shape = (nchan, 3 * share // 2, 640)
+    kept, sent = call(
         functools.partial(wgrad_body, nchan, rows, step),
-        [shape(3 * share, 640, dtype=f32)] + [shape(3 * share, 640)] * (nchan - 1),
+        [shape(*h_shape, dtype=f32), shape(*h_shape)],
         [planes, pltpu.VMEM((3 * full, 640), f32)],
         2 * 27 * full * full * cells,
         6 * block,
         name="wgrad",
     )(*mine, *sib, *pair, delta)
-    act_got = over_chan(act[1:])
-    total = partial[0]
-    for term in over_chan(partial[1:]):
-        total = total + term.astype(f32)
-    hop = 1
-    while True:
-        sent = total.astype(bf16)
-        came = lax.ppermute(sent, "space", [(i, i ^ hop) for i in range(nspace)])
-        hop *= 2
-        if hop >= nspace:
-            break
-        total = sent.astype(f32) + came.astype(f32)
+    kept = kept + to_sib(sent).astype(f32)
+    sent = [kept[k].astype(bf16) for k in range(nchan)]
+    near = kept_sum(sent[0], over_chan(sent[1:]))
+    far = [
+        lax.ppermute(
+            sent[k],
+            ("space", "chan"),
+            [
+                (i * nchan + c, (i ^ 2 * ZHOP) * nchan + (c + k) % nchan)
+                for i in range(nspace)
+                for c in range(nchan)
+            ],
+        )
+        for k in range(nchan)
+    ]
+    total = near + kept_sum(far[0], far[1:])
+    def unpack(blocks, name):
+        out = call(
+            functools.partial(unpack_body, nchan, rows, height),
+            shape(share, height, width),
+            [pltpu.VMEM((height * share, 128), f32)],
+            0,
+            2 * block,
+            name=name,
+        )(*blocks)
+        return out.reshape(share, 1, height, width)
+
+    activated = unpack([act[0]] + over_chan(act[1:]), "unpack_activated")
     ig = call(
         functools.partial(backward_body, nchan, rows),
         [a_shape] * nchan,
@@ -372,28 +449,31 @@
         name="backward",
     )(delta, d_sib, d_pair, w_backward)
     ig_got = over_chan(ig[1:])
-
-    def unpack(blocks, name):
-        out = call(
-            functools.partial(unpack_body, nchan, rows, height),
-            shape(share, height, width),
-            [pltpu.VMEM((height * share, 128), f32)],
-            0,
-            2 * block,
-            name=name,
-        )(*blocks)
-        return out.reshape(share, 1, height, width)
-
-    activated = unpack([act[0]] + act_got, "unpack_activated")
+    hops = [1 << n for n in range(1, nspace.bit_length() - 1)]
+    hops.remove(2 * ZHOP)
+    for n, hop in enumerate(hops[1:] + hops[:1]):
+        if n == DBAR:
+            total, d_sib, d_pair = lax.optimization_barrier((total, d_sib, d_pair))
+        if n == IBAR:
+            total, ig = lax.optimization_barrier((total, ig))
+        if n == GBAR:
+            total, ig_got = lax.optimization_barrier((total, ig_got))
+        if n == ABAR:
+            total, activated = lax.optimization_barrier((total, activated))
+        sent = total.astype(bf16)
+        came = lax.ppermute(sent, "space", [(i, i ^ hop) for i in range(nspace)])
+        total = sent.astype(f32) + came.astype(f32)
+    summed = to_sib(total)
+
     input_grad = unpack([ig[0]] + ig_got, "unpack_input_grad")
     w_grad, b_grad = call(
         functools.partial(finish_body, share, factor),
         [shape(27, share, full, dtype=f32), shape(1, share, dtype=f32)],
-        [],
+        [pltpu.VMEM((3 * share, 640), f32)],
         0,
         1 << 20,
         name="finish",
-    )(sent, came)
+    )(total, summed)
     w_grad = jnp.transpose(w_grad.reshape(3, 3, 3, share, full), (3, 4, 0, 1, 2))
     return activated, input_grad, w_grad, b_grad.reshape(share)
 

time: 64.5 us -> 51.7 us (0.80)
  starting transfers between devices: 32.1 us -> 20.6 us
  local copies, waits for them, and re-layouts: 3.66 us -> 2.59 us
    ppermute x3 -> x5, starting transfers between devices: 11.7 us -> 0.15 us  [to_sib(): return lax.ppermute(x, 'space', sib_perm)]
    ppermute x3 -> x5, starting transfers between devices: 2 us -> 10.3 us  [the longest x3 8.01 us: to_pair(): return lax.ppermute(x, ('space', 'chan'), perm)]
    ppermute x3 -> x5, waiting for transfers between devices: 0.01 us -> 7.84 us  [the longest x2 5.89 us: shards(): lax.ppermute(sent[k], ('space', 'chan'), [(i * nchan + c, (i ^ 2 * ZHOP)...]
    ppermute x4 -> x2, starting transfers between devices: 11.3 us -> 3.49 us  [shards(): came = lax.ppermute(sent, 'space', [(i, i ^ hop) for i in range(nspace)])]
    ppermute x4 -> x2, waiting for transfers between devices: 9.75 us -> 3.52 us  [shards(): came = lax.ppermute(sent, 'space', [(i, i ^ hop) for i in range(nspace)])]
    ppermute x5, waiting for transfers between devices: 9.11 us -> 6.53 us  [over_chan(): got.append(lax.ppermute(blocks[k - 1], 'chan', perm))]
    unnamed x8, local copies, waits for them, and re-layouts: 3.57 us -> 2.58 us
    ppermute x3 -> x5, waiting for transfers between devices: 0.01 us -> 0.72 us  [to_sib(): return lax.ppermute(x, 'space', sib_perm)]
  transfers between devices with their start and end apart: 15 -> 17, of which waited for: 6 -> 8; matrix products, arithmetic and copies ran while one was open for 0% -> 0% of each run, Pallas kernels for 6% -> 9%
where the time goes in v1:
time: 51.7 us; the launch traced here: 51.5 us
  starting transfers between devices  20.6 us (40%)
  waiting for transfers between devices  18.6 us (36%)
  Pallas kernels  8.82 us (17%)
  local copies, waits for them, and re-layouts  2.59 us (5%)
  between operations  0.76 us (1%)
    ppermute x3, starting transfers between devices, to_pair(): return lax.ppermute(x, ('space', 'chan'), perm)  8.01 us
    ppermute x5, starting transfers between devices, over_chan(): got.append(lax.ppermute(blocks[k - 1], 'chan', perm))  6.63 us
    ppermute x5, waiting for transfers between devices, over_chan(): got.append(lax.ppermute(blocks[k - 1], 'chan', perm))  6.53 us
    ppermute x2, waiting for transfers between devices, shards(): lax.ppermute(sent[k], ('space', 'chan'), [(i * nchan + c, (i ^ 2 * ZHOP)...  5.89 us
    ppermute x2, waiting for transfers between devices, shards(): came = lax.ppermute(sent, 'space', [(i, i ^ hop) for i in range(nspace)])  3.52 us
    ppermute x2, starting transfers between devices, shards(): came = lax.ppermute(sent, 'space', [(i, i ^ hop) for i in range(nspace)])  3.49 us
    unnamed x8, local copies, waits for them, and re-layouts  2.58 us
    pallas_call x2, Pallas kernels, unpack(): call(functools.partial(unpack_body, nchan, rows, height), shape(share, he...  2.5 us
  transfers between devices with their start and end apart: 17, of which 8 were waited for; matrix products, arithmetic and copies ran while one was open for 0% of the time, Pallas kernels for 9%

profile of v1, /device:TPU:0, one launch (start us, length us, event | category | flops | bytes accessed | tf_op | source)
XLA Modules:
  0.0 51.5 jit_solution(18320326173303985929)
XLA Ops:
  0.6 1.0 %copy-done = bf16[32,1,48,128]{3,2,1,0:T(8,128)(2,1)S(1)} copy-done((bf16[32,1,48,128]{3,2,1,0:T(8,128)(2,1)S(1)}, bf16[32,1,48,128]{3,2,1,0:T(8,128)(2,1)}, u32[]{:S(2)}) %copy-start) | copy-done | bytes 393240
  1.9 3.0 %collective-permute-start = (bf16[28,32,128]{2,1,0:T(8,128)(2,1)S(1)}, bf16[28,32,128]{2,1,0:T(8,128)(2,1)S(1)}, u32[]{:S(2)}, u32[]{:S(2)}) collective-permute-start(bf16[28,32,128]{2,1,0:T(8,128)(2,1)S(1)} %get-tuple-element.24), channel_id=1, source_target_pairs={{0,1},{1,0},{2,3},{3,2},{4,5},{5,4},{6,7},{7,6},{8,9},{9,8},{10,11... | collective-permute-start | bytes 688136 | tf_op jit(solution)/shard_map/ppermute | solution.py:332
  5.0 3.7 %collective-permute-start.2 = (bf16[28,32,128]{2,1,0:T(8,128)(2,1)S(1)}, bf16[28,32,128]{2,1,0:T(8,128)(2,1)S(1)}, u32[]{:S(2)}, u32[]{:S(2)}) collective-permute-start(bf16[28,32,128]{2,1,0:T(8,128)(2,1)S(1)} %get-tuple-element.23.refs_0_), channel_id=1, source_target_pairs={{2,4},{3,5},{6,8},{7,9},{10,12},{11,13},{14,16},{15,17},{18,20},{1... | collective-permute-start | bytes 688136 | tf_op jit(solution)/shard_map/ppermute | solution.py:340
  9.3 0.9 %copy-done.2 = bf16[32,64,3,3,3]{1,0,4,3,2:T(8,128)(2,1)S(1)} copy-done((bf16[32,64,3,3,3]{1,0,4,3,2:T(8,128)(2,1)S(1)}, bf16[32,64,3,3,3]{1,0,4,3,2:T(8,128)(2,1)}, u32[]{:S(2)}) %copy-start.2) | copy-done | bytes 110616
  11.2 1.9 %collective-permute-done.2.refs_4_ = bf16[28,32,128]{2,1,0:T(8,128)(2,1)S(1)} collective-permute-done((bf16[28,32,128]{2,1,0:T(8,128)(2,1)S(1)}, bf16[28,32,128]{2,1,0:T(8,128)(2,1)S(1)}, u32[]{:S(2)}, u32[]{:S(2)}) %collective-permute-start.2) | collective-permute-done | bytes 229408 | tf_op jit(solution)/shard_map/ppermute | solution.py:340
  13.1 3.7 %collective-permute-start.4 = (bf16[28,32,128]{2,1,0:T(8,128)(2,1)S(1)}, bf16[28,32,128]{2,1,0:T(8,128)(2,1)S(1)}, u32[]{:S(2)}, u32[]{:S(2)}) collective-permute-start(bf16[28,32,128]{2,1,0:T(8,128)(2,1)S(1)} %collective-permute-done.refs_1_), channel_id=1, source_target_pairs={{2,4},{3,5},{6,8},{7,9},{10,12},{11,13},{14,16},{15,17},{18,20},{1... | collective-permute-start | bytes 688136 | tf_op jit(solution)/shard_map/ppermute | solution.py:340
  16.8 4.1 %collective-permute-done.5.refs_1_.refs_7_ = bf16[41,32,128]{2,1,0:T(8,128)(2,1)S(1)} collective-permute-done((bf16[41,32,128]{2,1,0:T(8,128)(2,1)S(1)}, bf16[41,32,128]{2,1,0:T(8,128)(2,1)S(1)}, u32[]{:S(2)}, u32[]{:S(2)}) %collective-permute-start.5) | collective-permute-done | bytes 335904 | tf_op jit(solution)/shard_map/ppermute | solution.py:332
  21.3 1.5 %forward.1 = (bf16[24,32,128]{2,1,0:T(8,128)(2,1)S(1)}, bf16[24,32,128]{2,1,0:T(8,128)(2,1)S(1)}, bf16[26,64,128]{2,1,0:T(8,128)(2,1)S(1)}) custom-call(bf16[28,32,128]{2,1,0:T(8,128)(2,1)S(1)} %get-tuple-element.23.refs_0_, bf16[28,32,128]{2,1,0:T(8,128)(2,1)S(1)} %collective-permute-done.refs_1_, bf16[28,32,128]{2,1,0:T(8,128)(2,1)S(1)} %collective-permute-done.1.refs_2_, ...), custom_call_target="tpu_custom_call" | custom-call | flops 679477248 | bytes 2359296 | tf_op jit(solution)/shard_map/forward/pallas_call | solution.py:388
  22.8 1.6 %wgrad.1 = (f32[2,48,640]{2,1,0:T(8,128)S(1)}, bf16[2,48,640]{2,1,0:T(8,128)(2,1)S(1)}) custom-call(bf16[28,32,128]{2,1,0:T(8,128)(2,1)S(1)} %get-tuple-element.23.refs_0_, bf16[28,32,128]{2,1,0:T(8,128)(2,1)S(1)} %collective-permute-done.refs_1_, bf16[28,32,128]{2,1,0:T(8,128)(2,1)S(1)} %collective-permute-done.1.refs_2_, ...), custom_call_target="tpu_custom_call" | custom-call | flops 679477248 | bytes 2359296 | tf_op jit(solution)/shard_map/wgrad/pallas_call | solution.py:404
  25.1 0.7 %collective-permute-done.10 = bf16[2,48,640]{2,1,0:T(8,128)(2,1)S(1)} collective-permute-done((bf16[2,48,640]{2,1,0:T(8,128)(2,1)S(1)}, bf16[2,48,640]{2,1,0:T(8,128)(2,1)S(1)}, u32[]{:S(2)}, u32[]{:S(2)}) %collective-permute-start.10) | collective-permute-done | bytes 122912 | tf_op jit(solution)/shard_map/ppermute | solution.py:336
  26.4 1.8 %collective-permute-start.13 = (bf16[48,640]{1,0:T(8,128)(2,1)S(1)}, bf16[48,640]{1,0:T(8,128)(2,1)S(1)}, u32[]{:S(2)}, u32[]{:S(2)}) collective-permute-start(bf16[48,640]{1,0:T(8,128)(2,1)S(1)} %get-tuple-element.47), channel_id=1, source_target_pairs={{0,9},{1,8},{2,11},{3,10},{4,13},{5,12},{6,15},{7,14},{8,1},{9,0},... | collective-permute-start | bytes 184328 | tf_op jit(solution)/shard_map/ppermute | solution.py:416
  28.2 1.3 %collective-permute-start.11 = (bf16[48,640]{1,0:T(8,128)(2,1)S(1)}, bf16[48,640]{1,0:T(8,128)(2,1)S(1)}, u32[]{:S(2)}, u32[]{:S(2)}) collective-permute-start(bf16[48,640]{1,0:T(8,128)(2,1)S(1)} %get-tuple-element.47), channel_id=1, source_target_pairs={{0,1},{1,0},{2,3},{3,2},{4,5},{5,4},{6,7},{7,6},{8,9},{9,8},{10,11... | collective-permute-start | bytes 184328 | tf_op jit(solution)/shard_map/ppermute | solution.py:332
  29.4 4.8 %collective-permute-done.12 = bf16[48,640]{1,0:T(8,128)(2,1)S(1)} collective-permute-done((bf16[48,640]{1,0:T(8,128)(2,1)S(1)}, bf16[48,640]{1,0:T(8,128)(2,1)S(1)}, u32[]{:S(2)}, u32[]{:S(2)}) %collective-permute-start.12) | collective-permute-done | bytes 61472 | tf_op jit(solution)/shard_map/ppermute | solution.py:416
  34.2 1.1 %collective-permute-done.13 = bf16[48,640]{1,0:T(8,128)(2,1)S(1)} collective-permute-done((bf16[48,640]{1,0:T(8,128)(2,1)S(1)}, bf16[48,640]{1,0:T(8,128)(2,1)S(1)}, u32[]{:S(2)}, u32[]{:S(2)}) %collective-permute-start.13) | collective-permute-done | bytes 61472 | tf_op jit(solution)/shard_map/ppermute | solution.py:416
  35.4 2.5 %collective-permute-start.14 = (bf16[48,640]{1,0:T(8,128)(2,1)S(1)}, bf16[48,640]{1,0:T(8,128)(2,1)S(1)}, u32[]{:S(2)}, u32[]{:S(2)}) collective-permute-start(bf16[48,640]{1,0:T(8,128)(2,1)S(1)} %add_add_fusion), channel_id=1, source_target_pairs={{0,16},{2,18},{4,20},{6,22},{8,24},{10,26},{12,28},{14,30},{16,0},... | collective-permute-start | bytes 184328 | tf_op jit(solution)/shard_map/ppermute | solution.py:464
  37.9 1.1 %collective-permute-start.6 = (bf16[24,32,128]{2,1,0:T(8,128)(2,1)S(1)}, bf16[24,32,128]{2,1,0:T(8,128)(2,1)S(1)}, u32[]{:S(2)}, u32[]{:S(2)}) collective-permute-start(bf16[24,32,128]{2,1,0:T(8,128)(2,1)S(1)} %get-tuple-element.32), channel_id=1, source_target_pairs={{0,1},{1,0},{2,3},{3,2},{4,5},{5,4},{6,7},{7,6},{8,9},{9,8},{10,11... | collective-permute-start | bytes 589832 | tf_op jit(solution)/shard_map/ppermute | solution.py:332
  39.0 2.2 %collective-permute-done.14 = bf16[48,640]{1,0:T(8,128)(2,1)S(1)} collective-permute-done((bf16[48,640]{1,0:T(8,128)(2,1)S(1)}, bf16[48,640]{1,0:T(8,128)(2,1)S(1)}, u32[]{:S(2)}, u32[]{:S(2)}) %collective-permute-start.14) | collective-permute-done | bytes 61472 | tf_op jit(solution)/shard_map/ppermute | solution.py:464
  41.3 1.0 %collective-permute-start.15 = (bf16[48,640]{1,0:T(8,128)(2,1)S(1)}, bf16[48,640]{1,0:T(8,128)(2,1)S(1)}, u32[]{:S(2)}, u32[]{:S(2)}) collective-permute-start(bf16[48,640]{1,0:T(8,128)(2,1)S(1)} %add_convert_fusion.1), channel_id=1, source_target_pairs={{0,4},{2,6},{4,0},{6,2},{8,12},{10,14},{12,8},{14,10},{16,20},{18,... | collective-permute-start | bytes 184328 | tf_op jit(solution)/shard_map/ppermute | solution.py:464
  42.2 1.3 %backward.1 = (bf16[24,32,128]{2,1,0:T(8,128)(2,1)S(1)}, bf16[24,32,128]{2,1,0:T(8,128)(2,1)S(1)}) custom-call(bf16[26,64,128]{2,1,0:T(8,128)(2,1)S(1)} %get-tuple-element.33.refs_0_.refs_6_, bf16[26,64,128]{2,1,0:T(8,128)(2,1)S(1)} %collective-permute-done.7.refs_1_, bf16[26,64,128]{2,1,0:T(8,128)(2,1)S(1)} %collective-permute-done.8.refs_2_, ...), custom_call_target="tpu_custom_call" | custom-call | flops 679477248 | bytes 2359296 | tf_op jit(solution)/shard_map/backward/pallas_call | solution.py:440
  44.3 1.3 %collective-permute-done.15 = bf16[48,640]{1,0:T(8,128)(2,1)S(1)} collective-permute-done((bf16[48,640]{1,0:T(8,128)(2,1)S(1)}, bf16[48,640]{1,0:T(8,128)(2,1)S(1)}, u32[]{:S(2)}, u32[]{:S(2)}) %collective-permute-start.15) | collective-permute-done | bytes 61472 | tf_op jit(solution)/shard_map/ppermute | solution.py:464
  45.6 1.2 %unpack_activated.1 = bf16[32,48,128]{2,1,0:T(8,128)(2,1)} custom-call(bf16[24,32,128]{2,1,0:T(8,128)(2,1)S(1)} %get-tuple-element.31.refs_0_, bf16[24,32,128]{2,1,0:T(8,128)(2,1)S(1)} %collective-permute-done.6.refs_1_), custom_call_target="tpu_custom_call" | custom-call | bytes 786432 | tf_op jit(solution)/shard_map/unpack_activated/pallas_call | solution.py:429
  46.9 2.4 %collective-permute-done.9.refs_1_ = bf16[24,32,128]{2,1,0:T(8,128)(2,1)S(1)} collective-permute-done((bf16[24,32,128]{2,1,0:T(8,128)(2,1)S(1)}, bf16[24,32,128]{2,1,0:T(8,128)(2,1)S(1)}, u32[]{:S(2)}, u32[]{:S(2)}) %collective-permute-start.9) | collective-permute-done | bytes 196640 | tf_op jit(solution)/shard_map/ppermute | solution.py:332
  49.3 1.2 %unpack_input_grad.1 = bf16[32,48,128]{2,1,0:T(8,128)(2,1)} custom-call(bf16[24,32,128]{2,1,0:T(8,128)(2,1)S(1)} %get-tuple-element.35.refs_0_, bf16[24,32,128]{2,1,0:T(8,128)(2,1)S(1)} %collective-permute-done.9.refs_1_), custom_call_target="tpu_custom_call" | custom-call | bytes 786432 | tf_op jit(solution)/shard_map/unpack_input_grad/pallas_call | solution.py:429
  50.5 0.9 %finish.1 = (f32[27,32,64]{2,1,0:T(8,128)}, f32[1,32]{1,0:T(1,128)}) custom-call(f32[48,640]{1,0:T(8,128)S(1)} %convert_add_fusion.mine, f32[48,640]{1,0:T(8,128)S(1)} %collective-permute-done.16.other), custom_call_target="tpu_custom_call" | custom-call | bytes 1048576 | tf_op jit(solution)/shard_map/finish/pallas_call | solution.py:469
  (32 shorter events, 4.3 us)
Async XLA Ops:
  0.6 1.0 %copy-start = (bf16[32,1,48,128]{3,2,1,0:T(8,128)(2,1)S(1)}, bf16[32,1,48,128]{3,2,1,0:T(8,128)(2,1)}, u32[]{:S(2)}) copy-start(bf16[32,1,48,128]{3,2,1,0:T(8,128)(2,1)} %param.4) | copy-start | bytes 1179652
  1.6 7.0 %copy-start.1 = (bf16[32,1,48,128]{3,2,1,0:T(8,128)(2,1)S(1)}, bf16[32,1,48,128]{3,2,1,0:T(8,128)(2,1)}, u32[]{:S(2)}) copy-start(bf16[32,1,48,128]{3,2,1,0:T(8,128)(2,1)} %param.7) | copy-start | bytes 1179652
  1.9 9.2 %collective-permute-start = (bf16[28,32,128]{2,1,0:T(8,128)(2,1)S(1)}, bf16[28,32,128]{2,1,0:T(8,128)(2,1)S(1)}, u32[]{:S(2)}, u32[]{:S(2)}) collective-permute-start(bf16[28,32,128]{2,1,0:T(8,128)(2,1)S(1)} %get-tuple-element.24), channel_id=1, source_target_pairs={{0,1},{1,0},{2,3},{3,2},{4,5},{5,4},{6,7},{7,6},{8,9},{9,8},{10,11... | collective-permute-start | bytes 688136 | tf_op jit(solution)/shard_map/ppermute | solution.py:332
  5.0 8.1 %collective-permute-start.2 = (bf16[28,32,128]{2,1,0:T(8,128)(2,1)S(1)}, bf16[28,32,128]{2,1,0:T(8,128)(2,1)S(1)}, u32[]{:S(2)}, u32[]{:S(2)}) collective-permute-start(bf16[28,32,128]{2,1,0:T(8,128)(2,1)S(1)} %get-tuple-element.23.refs_0_), channel_id=1, source_target_pairs={{2,4},{3,5},{6,8},{7,9},{10,12},{11,13},{14,16},{15,17},{18,20},{1... | collective-permute-start | bytes 688136 | tf_op jit(solution)/shard_map/ppermute | solution.py:340
  8.7 4.5 %collective-permute-start.1 = (bf16[28,32,128]{2,1,0:T(8,128)(2,1)S(1)}, bf16[28,32,128]{2,1,0:T(8,128)(2,1)S(1)}, u32[]{:S(2)}, u32[]{:S(2)}) collective-permute-start(bf16[28,32,128]{2,1,0:T(8,128)(2,1)S(1)} %get-tuple-element.23.refs_0_), channel_id=1, source_target_pairs={{0,2},{2,0},{4,6},{6,4},{8,10},{10,8},{12,14},{14,12},{16,18},{18,... | collective-permute-start | bytes 688136 | tf_op jit(solution)/shard_map/ppermute | solution.py:336
  8.7 0.7 %copy-start.3 = (f32[32]{0:T(128)S(1)}, f32[32]{0:T(128)}, u32[]{:S(2)}) copy-start(f32[32]{0:T(128)} %param.6) | copy-start | bytes 388
  9.3 0.9 %copy-start.2 = (bf16[32,64,3,3,3]{1,0,4,3,2:T(8,128)(2,1)S(1)}, bf16[32,64,3,3,3]{1,0,4,3,2:T(8,128)(2,1)}, u32[]{:S(2)}) copy-start(bf16[32,64,3,3,3]{1,0,4,3,2:T(8,128)(2,1)} %param.5) | copy-start | bytes 331780
  10.6 10.4 %collective-permute-start.5 = (bf16[41,32,128]{2,1,0:T(8,128)(2,1)S(1)}, bf16[41,32,128]{2,1,0:T(8,128)(2,1)S(1)}, u32[]{:S(2)}, u32[]{:S(2)}) collective-permute-start(bf16[41,32,128]{2,1,0:T(8,128)(2,1)S(1)} %get-tuple-element.29), channel_id=1, source_target_pairs={{0,1},{1,0},{2,3},{3,2},{4,5},{5,4},{6,7},{7,6},{8,9},{9,8},{10,11... | collective-permute-start | bytes 1007624 | tf_op jit(solution)/shard_map/ppermute | solution.py:332
  13.1 8.2 %collective-permute-start.4 = (bf16[28,32,128]{2,1,0:T(8,128)(2,1)S(1)}, bf16[28,32,128]{2,1,0:T(8,128)(2,1)S(1)}, u32[]{:S(2)}, u32[]{:S(2)}) collective-permute-start(bf16[28,32,128]{2,1,0:T(8,128)(2,1)S(1)} %collective-permute-done.refs_1_), channel_id=1, source_target_pairs={{2,4},{3,5},{6,8},{7,9},{10,12},{11,13},{14,16},{15,17},{18,20},{1... | collective-permute-start | bytes 688136 | tf_op jit(solution)/shard_map/ppermute | solution.py:340
  16.8 4.5 %collective-permute-start.3 = (bf16[28,32,128]{2,1,0:T(8,128)(2,1)S(1)}, bf16[28,32,128]{2,1,0:T(8,128)(2,1)S(1)}, u32[]{:S(2)}, u32[]{:S(2)}) collective-permute-start(bf16[28,32,128]{2,1,0:T(8,128)(2,1)S(1)} %collective-permute-done.refs_1_), channel_id=1, source_target_pairs={{0,2},{2,0},{4,6},{6,4},{8,10},{10,8},{12,14},{14,12},{16,18},{18,... | collective-permute-start | bytes 688136 | tf_op jit(solution)/shard_map/ppermute | solution.py:336
  24.4 1.4 %collective-permute-start.10 = (bf16[2,48,640]{2,1,0:T(8,128)(2,1)S(1)}, bf16[2,48,640]{2,1,0:T(8,128)(2,1)S(1)}, u32[]{:S(2)}, u32[]{:S(2)}) collective-permute-start(bf16[2,48,640]{2,1,0:T(8,128)(2,1)S(1)} %get-tuple-element.38), channel_id=1, source_target_pairs={{0,2},{2,0},{4,6},{6,4},{8,10},{10,8},{12,14},{14,12},{16,18},{18,... | collective-permute-start | bytes 368648 | tf_op jit(solution)/shard_map/ppermute | solution.py:336
  24.5 10.9 %collective-permute-start.8 = (bf16[26,64,128]{2,1,0:T(8,128)(2,1)S(1)}, bf16[26,64,128]{2,1,0:T(8,128)(2,1)S(1)}, u32[]{:S(2)}, u32[]{:S(2)}) collective-permute-start(bf16[26,64,128]{2,1,0:T(8,128)(2,1)S(1)} %get-tuple-element.33.refs_0_.refs_6_), channel_id=1, source_target_pairs={{2,4},{3,5},{6,8},{7,9},{10,12},{11,13},{14,16},{15,17},{18,20},{1... | collective-permute-start | bytes 1277960 | tf_op jit(solution)/shard_map/ppermute | solution.py:340
  25.1 10.3 %collective-permute-start.7 = (bf16[26,64,128]{2,1,0:T(8,128)(2,1)S(1)}, bf16[26,64,128]{2,1,0:T(8,128)(2,1)S(1)}, u32[]{:S(2)}, u32[]{:S(2)}) collective-permute-start(bf16[26,64,128]{2,1,0:T(8,128)(2,1)S(1)} %get-tuple-element.33.refs_0_.refs_6_), channel_id=1, source_target_pairs={{0,2},{2,0},{4,6},{6,4},{8,10},{10,8},{12,14},{14,12},{16,18},{18,... | collective-permute-start | bytes 1277960 | tf_op jit(solution)/shard_map/ppermute | solution.py:336
  25.9 8.3 %collective-permute-start.12 = (bf16[48,640]{1,0:T(8,128)(2,1)S(1)}, bf16[48,640]{1,0:T(8,128)(2,1)S(1)}, u32[]{:S(2)}, u32[]{:S(2)}) collective-permute-start(bf16[48,640]{1,0:T(8,128)(2,1)S(1)} %get-tuple-element.46), channel_id=1, source_target_pairs={{0,8},{1,9},{2,10},{3,11},{4,12},{5,13},{6,14},{7,15},{8,0},{9,1},... | collective-permute-start | bytes 184328 | tf_op jit(solution)/shard_map/ppermute | solution.py:416
  26.4 8.9 %collective-permute-start.13 = (bf16[48,640]{1,0:T(8,128)(2,1)S(1)}, bf16[48,640]{1,0:T(8,128)(2,1)S(1)}, u32[]{:S(2)}, u32[]{:S(2)}) collective-permute-start(bf16[48,640]{1,0:T(8,128)(2,1)S(1)} %get-tuple-element.47), channel_id=1, source_target_pairs={{0,9},{1,8},{2,11},{3,10},{4,13},{5,12},{6,15},{7,14},{8,1},{9,0},... | collective-permute-start | bytes 184328 | tf_op jit(solution)/shard_map/ppermute | solution.py:416
  28.2 7.1 %collective-permute-start.11 = (bf16[48,640]{1,0:T(8,128)(2,1)S(1)}, bf16[48,640]{1,0:T(8,128)(2,1)S(1)}, u32[]{:S(2)}, u32[]{:S(2)}) collective-permute-start(bf16[48,640]{1,0:T(8,128)(2,1)S(1)} %get-tuple-element.47), channel_id=1, source_target_pairs={{0,1},{1,0},{2,3},{3,2},{4,5},{5,4},{6,7},{7,6},{8,9},{9,8},{10,11... | collective-permute-start | bytes 184328 | tf_op jit(solution)/shard_map/ppermute | solution.py:332
  35.4 5.8 %collective-permute-start.14 = (bf16[48,640]{1,0:T(8,128)(2,1)S(1)}, bf16[48,640]{1,0:T(8,128)(2,1)S(1)}, u32[]{:S(2)}, u32[]{:S(2)}) collective-permute-start(bf16[48,640]{1,0:T(8,128)(2,1)S(1)} %add_add_fusion), channel_id=1, source_target_pairs={{0,16},{2,18},{4,20},{6,22},{8,24},{10,26},{12,28},{14,30},{16,0},... | collective-permute-start | bytes 184328 | tf_op jit(solution)/shard_map/ppermute | solution.py:464
  37.9 7.7 %collective-permute-start.6 = (bf16[24,32,128]{2,1,0:T(8,128)(2,1)S(1)}, bf16[24,32,128]{2,1,0:T(8,128)(2,1)S(1)}, u32[]{:S(2)}, u32[]{:S(2)}) collective-permute-start(bf16[24,32,128]{2,1,0:T(8,128)(2,1)S(1)} %get-tuple-element.32), channel_id=1, source_target_pairs={{0,1},{1,0},{2,3},{3,2},{4,5},{5,4},{6,7},{7,6},{8,9},{9,8},{10,11... | collective-permute-start | bytes 589832 | tf_op jit(solution)/shard_map/ppermute | solution.py:332
  41.3 4.3 %collective-permute-start.15 = (bf16[48,640]{1,0:T(8,128)(2,1)S(1)}, bf16[48,640]{1,0:T(8,128)(2,1)S(1)}, u32[]{:S(2)}, u32[]{:S(2)}) collective-permute-start(bf16[48,640]{1,0:T(8,128)(2,1)S(1)} %add_convert_fusion.1), channel_id=1, source_target_pairs={{0,4},{2,6},{4,0},{6,2},{8,12},{10,14},{12,8},{14,10},{16,20},{18,... | collective-permute-start | bytes 184328 | tf_op jit(solution)/shard_map/ppermute | solution.py:464
  43.6 5.7 %collective-permute-start.9 = (bf16[24,32,128]{2,1,0:T(8,128)(2,1)S(1)}, bf16[24,32,128]{2,1,0:T(8,128)(2,1)S(1)}, u32[]{:S(2)}, u32[]{:S(2)}) collective-permute-start(bf16[24,32,128]{2,1,0:T(8,128)(2,1)S(1)} %get-tuple-element.36), channel_id=1, source_target_pairs={{0,1},{1,0},{2,3},{3,2},{4,5},{5,4},{6,7},{7,6},{8,9},{9,8},{10,11... | collective-permute-start | bytes 589832 | tf_op jit(solution)/shard_map/ppermute | solution.py:332
  45.6 5.0 %collective-permute-start.16 = (f32[48,640]{1,0:T(8,128)S(1)}, f32[48,640]{1,0:T(8,128)S(1)}, u32[]{:S(2)}, u32[]{:S(2)}) collective-permute-start(f32[48,640]{1,0:T(8,128)S(1)} %convert_add_fusion.mine), channel_id=1, source_target_pairs={{0,2},{2,0},{4,6},{6,4},{8,10},{10,8},{12,14},{14,12},{16,18},{18,... | collective-permute-start | bytes 368648 | tf_op jit(solution)/shard_map/ppermute | solution.py:336

commit v2 on v1

--- a/solution.py
+++ b/solution.py
@@ -11,12 +11,14 @@
 leakage = 0.1
 bf16 = jnp.bfloat16
 f32 = jnp.float32
-DBAR = 0
+DBAR = 9
 IBAR = 9
 ABAR = 9
 UBAR = False
 ZHOP = 2
 GBAR = 9
+SBAR = False
+FLIP = True
 VWRAP = True
 VWRAP2 = True
 DWRAP = False
@@ -451,7 +453,9 @@
     ig_got = over_chan(ig[1:])
     hops = [1 << n for n in range(1, nspace.bit_length() - 1)]
     hops.remove(2 * ZHOP)
-    for n, hop in enumerate(hops[1:] + hops[:1]):
+    if FLIP:
+        hops = hops[1:] + hops[:1]
+    for n, hop in enumerate(hops):
         if n == DBAR:
             total, d_sib, d_pair = lax.optimization_barrier((total, d_sib, d_pair))
         if n == IBAR:
@@ -463,6 +467,8 @@
         sent = total.astype(bf16)
         came = lax.ppermute(sent, "space", [(i, i ^ hop) for i in range(nspace)])
         total = sent.astype(f32) + came.astype(f32)
+    if SBAR:
+        total, ig_got = lax.optimization_barrier((total, ig_got))
     summed = to_sib(total)
 
     input_grad = unpack([ig[0]] + ig_got, "unpack_input_grad")

time: 51.7 us -> 48.8 us (0.944)
  waiting for transfers between devices: 18.6 us -> 16 us
    ppermute x2, waiting for transfers between devices: 5.89 us -> 1.59 us  [shards(): lax.ppermute(sent[k], ('space', 'chan'), [(i * nchan + c, (i ^ 2 * ZHOP)...]
    ppermute x5, waiting for transfers between devices: 0.72 us -> 1.39 us  [to_sib(): return lax.ppermute(x, 'space', sib_perm)]
    ppermute x2, waiting for transfers between devices: 3.52 us -> 4.17 us  [shards(): came = lax.ppermute(sent, 'space', [(i, i ^ hop) for i in range(nspace)])]
    ppermute x5, starting transfers between devices: 6.63 us -> 7.16 us  [over_chan(): got.append(lax.ppermute(blocks[k - 1], 'chan', perm))]
  transfers between devices with their start and end apart: 17 -> 17, of which waited for: 8 -> 10; matrix products, arithmetic and copies ran while one was open for 0% -> 0% of each run, Pallas kernels for 9% -> 9%
where the time goes in v2:
time: 48.8 us; the launch traced here: 48.6 us
  starting transfers between devices  20.4 us (42%)
  waiting for transfers between devices  16 us (33%)
  Pallas kernels  8.82 us (18%)
  local copies, waits for them, and re-layouts  2.59 us (5%)
  between operations  0.75 us (2%)
    ppermute x3, starting transfers between devices, to_pair(): return lax.ppermute(x, ('space', 'chan'), perm)  7.94 us
    ppermute x5, starting transfers between devices, over_chan(): got.append(lax.ppermute(blocks[k - 1], 'chan', perm))  7.16 us
    ppermute x5, waiting for transfers between devices, over_chan(): got.append(lax.ppermute(blocks[k - 1], 'chan', perm))  6.87 us
    ppermute x2, waiting for transfers between devices, shards(): came = lax.ppermute(sent, 'space', [(i, i ^ hop) for i in range(nspace)])  4.17 us
    ppermute x2, starting transfers between devices, shards(): came = lax.ppermute(sent, 'space', [(i, i ^ hop) for i in range(nspace)])  3.07 us
    unnamed x8, local copies, waits for them, and re-layouts  2.58 us
    pallas_call x2, Pallas kernels, unpack(): call(functools.partial(unpack_body, nchan, rows, height), shape(share, he...  2.5 us
    ppermute x2, starting transfers between devices, shards(): lax.ppermute(sent[k], ('space', 'chan'), [(i * nchan + c, (i ^ 2 * ZHOP)...  2.06 us
  transfers between devices with their start and end apart: 17, of which 10 were waited for; matrix products, arithmetic and copies ran while one was open for 0% of the time, Pallas kernels for 9%

profile of v2, /device:TPU:0, one launch (start us, length us, event | category | flops | bytes accessed | tf_op | source)
XLA Modules:
  0.0 48.6 jit_solution(3047350963277010995)
XLA Ops:
  0.6 1.0 %copy-done = bf16[32,1,48,128]{3,2,1,0:T(8,128)(2,1)S(1)} copy-done((bf16[32,1,48,128]{3,2,1,0:T(8,128)(2,1)S(1)}, bf16[32,1,48,128]{3,2,1,0:T(8,128)(2,1)}, u32[]{:S(2)}) %copy-start) | copy-done | bytes 393240
  1.9 3.0 %collective-permute-start = (bf16[28,32,128]{2,1,0:T(8,128)(2,1)S(1)}, bf16[28,32,128]{2,1,0:T(8,128)(2,1)S(1)}, u32[]{:S(2)}, u32[]{:S(2)}) collective-permute-start(bf16[28,32,128]{2,1,0:T(8,128)(2,1)S(1)} %get-tuple-element.23), channel_id=1, source_target_pairs={{0,1},{1,0},{2,3},{3,2},{4,5},{5,4},{6,7},{7,6},{8,9},{9,8},{10,11... | collective-permute-start | bytes 688136 | tf_op jit(solution)/shard_map/ppermute | solution.py:334
  5.0 3.7 %collective-permute-start.2 = (bf16[28,32,128]{2,1,0:T(8,128)(2,1)S(1)}, bf16[28,32,128]{2,1,0:T(8,128)(2,1)S(1)}, u32[]{:S(2)}, u32[]{:S(2)}) collective-permute-start(bf16[28,32,128]{2,1,0:T(8,128)(2,1)S(1)} %get-tuple-element.22.refs_0_), channel_id=1, source_target_pairs={{2,4},{3,5},{6,8},{7,9},{10,12},{11,13},{14,16},{15,17},{18,20},{1... | collective-permute-start | bytes 688136 | tf_op jit(solution)/shard_map/ppermute | solution.py:342
  9.3 0.9 %copy-done.2 = bf16[32,64,3,3,3]{1,0,4,3,2:T(8,128)(2,1)S(1)} copy-done((bf16[32,64,3,3,3]{1,0,4,3,2:T(8,128)(2,1)S(1)}, bf16[32,64,3,3,3]{1,0,4,3,2:T(8,128)(2,1)}, u32[]{:S(2)}) %copy-start.2) | copy-done | bytes 110616
  11.2 1.9 %collective-permute-done.2.refs_4_ = bf16[28,32,128]{2,1,0:T(8,128)(2,1)S(1)} collective-permute-done((bf16[28,32,128]{2,1,0:T(8,128)(2,1)S(1)}, bf16[28,32,128]{2,1,0:T(8,128)(2,1)S(1)}, u32[]{:S(2)}, u32[]{:S(2)}) %collective-permute-start.2) | collective-permute-done | bytes 229408 | tf_op jit(solution)/shard_map/ppermute | solution.py:342
  13.1 3.7 %collective-permute-start.4 = (bf16[28,32,128]{2,1,0:T(8,128)(2,1)S(1)}, bf16[28,32,128]{2,1,0:T(8,128)(2,1)S(1)}, u32[]{:S(2)}, u32[]{:S(2)}) collective-permute-start(bf16[28,32,128]{2,1,0:T(8,128)(2,1)S(1)} %collective-permute-done.refs_1_), channel_id=1, source_target_pairs={{2,4},{3,5},{6,8},{7,9},{10,12},{11,13},{14,16},{15,17},{18,20},{1... | collective-permute-start | bytes 688136 | tf_op jit(solution)/shard_map/ppermute | solution.py:342
  16.8 4.1 %collective-permute-done.5.refs_1_.refs_7_ = bf16[41,32,128]{2,1,0:T(8,128)(2,1)S(1)} collective-permute-done((bf16[41,32,128]{2,1,0:T(8,128)(2,1)S(1)}, bf16[41,32,128]{2,1,0:T(8,128)(2,1)S(1)}, u32[]{:S(2)}, u32[]{:S(2)}) %collective-permute-start.5) | collective-permute-done | bytes 335904 | tf_op jit(solution)/shard_map/ppermute | solution.py:334
  21.3 1.5 %forward.1 = (bf16[24,32,128]{2,1,0:T(8,128)(2,1)S(1)}, bf16[24,32,128]{2,1,0:T(8,128)(2,1)S(1)}, bf16[26,64,128]{2,1,0:T(8,128)(2,1)S(1)}) custom-call(bf16[28,32,128]{2,1,0:T(8,128)(2,1)S(1)} %get-tuple-element.22.refs_0_, bf16[28,32,128]{2,1,0:T(8,128)(2,1)S(1)} %collective-permute-done.refs_1_, bf16[28,32,128]{2,1,0:T(8,128)(2,1)S(1)} %collective-permute-done.1.refs_2_, ...), custom_call_target="tpu_custom_call" | custom-call | flops 679477248 | bytes 2359296 | tf_op jit(solution)/shard_map/forward/pallas_call | solution.py:390
  22.8 1.6 %wgrad.1 = (f32[2,48,640]{2,1,0:T(8,128)S(1)}, bf16[2,48,640]{2,1,0:T(8,128)(2,1)S(1)}) custom-call(bf16[28,32,128]{2,1,0:T(8,128)(2,1)S(1)} %get-tuple-element.22.refs_0_, bf16[28,32,128]{2,1,0:T(8,128)(2,1)S(1)} %collective-permute-done.refs_1_, bf16[28,32,128]{2,1,0:T(8,128)(2,1)S(1)} %collective-permute-done.1.refs_2_, ...), custom_call_target="tpu_custom_call" | custom-call | flops 679477248 | bytes 2359296 | tf_op jit(solution)/shard_map/wgrad/pallas_call | solution.py:406
  24.5 1.3 %collective-permute-done.10 = bf16[2,48,640]{2,1,0:T(8,128)(2,1)S(1)} collective-permute-done((bf16[2,48,640]{2,1,0:T(8,128)(2,1)S(1)}, bf16[2,48,640]{2,1,0:T(8,128)(2,1)S(1)}, u32[]{:S(2)}, u32[]{:S(2)}) %collective-permute-start.10) | collective-permute-done | bytes 122912 | tf_op jit(solution)/shard_map/ppermute | solution.py:338
  26.0 2.0 %collective-permute-start.13 = (bf16[48,640]{1,0:T(8,128)(2,1)S(1)}, bf16[48,640]{1,0:T(8,128)(2,1)S(1)}, u32[]{:S(2)}, u32[]{:S(2)}) collective-permute-start(bf16[48,640]{1,0:T(8,128)(2,1)S(1)} %get-tuple-element.45), channel_id=1, source_target_pairs={{0,9},{1,8},{2,11},{3,10},{4,13},{5,12},{6,15},{7,14},{8,1},{9,0},... | collective-permute-start | bytes 184328 | tf_op jit(solution)/shard_map/ppermute | solution.py:418
  27.9 1.5 %collective-permute-start.11 = (bf16[48,640]{1,0:T(8,128)(2,1)S(1)}, bf16[48,640]{1,0:T(8,128)(2,1)S(1)}, u32[]{:S(2)}, u32[]{:S(2)}) collective-permute-start(bf16[48,640]{1,0:T(8,128)(2,1)S(1)} %get-tuple-element.45), channel_id=1, source_target_pairs={{0,1},{1,0},{2,3},{3,2},{4,5},{5,4},{6,7},{7,6},{8,9},{9,8},{10,11... | collective-permute-start | bytes 184328 | tf_op jit(solution)/shard_map/ppermute | solution.py:334
  30.7 0.9 %collective-permute-done.13 = bf16[48,640]{1,0:T(8,128)(2,1)S(1)} collective-permute-done((bf16[48,640]{1,0:T(8,128)(2,1)S(1)}, bf16[48,640]{1,0:T(8,128)(2,1)S(1)}, u32[]{:S(2)}, u32[]{:S(2)}) %collective-permute-start.13) | collective-permute-done | bytes 61472 | tf_op jit(solution)/shard_map/ppermute | solution.py:418
  31.6 1.0 %collective-permute-done.11 = bf16[48,640]{1,0:T(8,128)(2,1)S(1)} collective-permute-done((bf16[48,640]{1,0:T(8,128)(2,1)S(1)}, bf16[48,640]{1,0:T(8,128)(2,1)S(1)}, u32[]{:S(2)}, u32[]{:S(2)}) %collective-permute-start.11) | collective-permute-done | bytes 61472 | tf_op jit(solution)/shard_map/ppermute | solution.py:334
  32.6 2.1 %collective-permute-start.14 = (bf16[48,640]{1,0:T(8,128)(2,1)S(1)}, bf16[48,640]{1,0:T(8,128)(2,1)S(1)}, u32[]{:S(2)}, u32[]{:S(2)}) collective-permute-start(bf16[48,640]{1,0:T(8,128)(2,1)S(1)} %add_convert_fusion.2), channel_id=1, source_target_pairs={{0,16},{2,18},{4,20},{6,22},{8,24},{10,26},{12,28},{14,30},{16,0},... | collective-permute-start | bytes 184328 | tf_op jit(solution)/shard_map/ppermute | solution.py:468
  34.7 0.8 %collective-permute-start.6 = (bf16[24,32,128]{2,1,0:T(8,128)(2,1)S(1)}, bf16[24,32,128]{2,1,0:T(8,128)(2,1)S(1)}, u32[]{:S(2)}, u32[]{:S(2)}) collective-permute-start(bf16[24,32,128]{2,1,0:T(8,128)(2,1)S(1)} %get-tuple-element.31), channel_id=1, source_target_pairs={{0,1},{1,0},{2,3},{3,2},{4,5},{5,4},{6,7},{7,6},{8,9},{9,8},{10,11... | collective-permute-start | bytes 589832 | tf_op jit(solution)/shard_map/ppermute | solution.py:334
  35.4 3.5 %collective-permute-done.14 = bf16[48,640]{1,0:T(8,128)(2,1)S(1)} collective-permute-done((bf16[48,640]{1,0:T(8,128)(2,1)S(1)}, bf16[48,640]{1,0:T(8,128)(2,1)S(1)}, u32[]{:S(2)}, u32[]{:S(2)}) %collective-permute-start.14) | collective-permute-done | bytes 61472 | tf_op jit(solution)/shard_map/ppermute | solution.py:468
  39.0 1.0 %collective-permute-start.15 = (bf16[48,640]{1,0:T(8,128)(2,1)S(1)}, bf16[48,640]{1,0:T(8,128)(2,1)S(1)}, u32[]{:S(2)}, u32[]{:S(2)}) collective-permute-start(bf16[48,640]{1,0:T(8,128)(2,1)S(1)} %add_convert_fusion.1), channel_id=1, source_target_pairs={{0,4},{2,6},{4,0},{6,2},{8,12},{10,14},{12,8},{14,10},{16,20},{18,... | collective-permute-start | bytes 184328 | tf_op jit(solution)/shard_map/ppermute | solution.py:468
  39.9 1.3 %backward.1 = (bf16[24,32,128]{2,1,0:T(8,128)(2,1)S(1)}, bf16[24,32,128]{2,1,0:T(8,128)(2,1)S(1)}) custom-call(bf16[26,64,128]{2,1,0:T(8,128)(2,1)S(1)} %get-tuple-element.32.refs_0_.refs_6_, bf16[26,64,128]{2,1,0:T(8,128)(2,1)S(1)} %collective-permute-done.7.refs_1_, bf16[26,64,128]{2,1,0:T(8,128)(2,1)S(1)} %collective-permute-done.8.refs_2_, ...), custom_call_target="tpu_custom_call" | custom-call | flops 679477248 | bytes 2359296 | tf_op jit(solution)/shard_map/backward/pallas_call | solution.py:442
  41.3 1.3 %collective-permute-start.9 = (bf16[24,32,128]{2,1,0:T(8,128)(2,1)S(1)}, bf16[24,32,128]{2,1,0:T(8,128)(2,1)S(1)}, u32[]{:S(2)}, u32[]{:S(2)}) collective-permute-start(bf16[24,32,128]{2,1,0:T(8,128)(2,1)S(1)} %get-tuple-element.35), channel_id=1, source_target_pairs={{0,1},{1,0},{2,3},{3,2},{4,5},{5,4},{6,7},{7,6},{8,9},{9,8},{10,11... | collective-permute-start | bytes 589832 | tf_op jit(solution)/shard_map/ppermute | solution.py:334
  43.4 1.2 %unpack_activated.1 = bf16[32,48,128]{2,1,0:T(8,128)(2,1)} custom-call(bf16[24,32,128]{2,1,0:T(8,128)(2,1)S(1)} %get-tuple-element.30.refs_0_, bf16[24,32,128]{2,1,0:T(8,128)(2,1)S(1)} %collective-permute-done.6.refs_1_), custom_call_target="tpu_custom_call" | custom-call | bytes 786432 | tf_op jit(solution)/shard_map/unpack_activated/pallas_call | solution.py:431
  44.7 0.9 %finish.1 = (f32[27,32,64]{2,1,0:T(8,128)}, f32[1,32]{1,0:T(1,128)}) custom-call(f32[48,640]{1,0:T(8,128)S(1)} %convert_add_fusion.mine, f32[48,640]{1,0:T(8,128)S(1)} %collective-permute-done.16.other), custom_call_target="tpu_custom_call" | custom-call | bytes 1048576 | tf_op jit(solution)/shard_map/finish/pallas_call | solution.py:475
  45.6 1.8 %collective-permute-done.9.refs_1_ = bf16[24,32,128]{2,1,0:T(8,128)(2,1)S(1)} collective-permute-done((bf16[24,32,128]{2,1,0:T(8,128)(2,1)S(1)}, bf16[24,32,128]{2,1,0:T(8,128)(2,1)S(1)}, u32[]{:S(2)}, u32[]{:S(2)}) %collective-permute-start.9) | collective-permute-done | bytes 196640 | tf_op jit(solution)/shard_map/ppermute | solution.py:334
  47.4 1.2 %unpack_input_grad.1 = bf16[32,48,128]{2,1,0:T(8,128)(2,1)} custom-call(bf16[24,32,128]{2,1,0:T(8,128)(2,1)S(1)} %get-tuple-element.34.refs_0_, bf16[24,32,128]{2,1,0:T(8,128)(2,1)S(1)} %collective-permute-done.9.refs_1_), custom_call_target="tpu_custom_call" | custom-call | bytes 786432 | tf_op jit(solution)/shard_map/unpack_input_grad/pallas_call | solution.py:431
  (32 shorter events, 4.5 us)
Async XLA Ops:
  0.6 1.0 %copy-start = (bf16[32,1,48,128]{3,2,1,0:T(8,128)(2,1)S(1)}, bf16[32,1,48,128]{3,2,1,0:T(8,128)(2,1)}, u32[]{:S(2)}) copy-start(bf16[32,1,48,128]{3,2,1,0:T(8,128)(2,1)} %param.4) | copy-start | bytes 1179652
  1.6 7.0 %copy-start.1 = (bf16[32,1,48,128]{3,2,1,0:T(8,128)(2,1)S(1)}, bf16[32,1,48,128]{3,2,1,0:T(8,128)(2,1)}, u32[]{:S(2)}) copy-start(bf16[32,1,48,128]{3,2,1,0:T(8,128)(2,1)} %param.7) | copy-start | bytes 1179652
  1.9 9.2 %collective-permute-start = (bf16[28,32,128]{2,1,0:T(8,128)(2,1)S(1)}, bf16[28,32,128]{2,1,0:T(8,128)(2,1)S(1)}, u32[]{:S(2)}, u32[]{:S(2)}) collective-permute-start(bf16[28,32,128]{2,1,0:T(8,128)(2,1)S(1)} %get-tuple-element.23), channel_id=1, source_target_pairs={{0,1},{1,0},{2,3},{3,2},{4,5},{5,4},{6,7},{7,6},{8,9},{9,8},{10,11... | collective-permute-start | bytes 688136 | tf_op jit(solution)/shard_map/ppermute | solution.py:334
  5.0 8.1 %collective-permute-start.2 = (bf16[28,32,128]{2,1,0:T(8,128)(2,1)S(1)}, bf16[28,32,128]{2,1,0:T(8,128)(2,1)S(1)}, u32[]{:S(2)}, u32[]{:S(2)}) collective-permute-start(bf16[28,32,128]{2,1,0:T(8,128)(2,1)S(1)} %get-tuple-element.22.refs_0_), channel_id=1, source_target_pairs={{2,4},{3,5},{6,8},{7,9},{10,12},{11,13},{14,16},{15,17},{18,20},{1... | collective-permute-start | bytes 688136 | tf_op jit(solution)/shard_map/ppermute | solution.py:342
  8.7 4.5 %collective-permute-start.1 = (bf16[28,32,128]{2,1,0:T(8,128)(2,1)S(1)}, bf16[28,32,128]{2,1,0:T(8,128)(2,1)S(1)}, u32[]{:S(2)}, u32[]{:S(2)}) collective-permute-start(bf16[28,32,128]{2,1,0:T(8,128)(2,1)S(1)} %get-tuple-element.22.refs_0_), channel_id=1, source_target_pairs={{0,2},{2,0},{4,6},{6,4},{8,10},{10,8},{12,14},{14,12},{16,18},{18,... | collective-permute-start | bytes 688136 | tf_op jit(solution)/shard_map/ppermute | solution.py:338
  8.7 0.7 %copy-start.3 = (f32[32]{0:T(128)S(1)}, f32[32]{0:T(128)}, u32[]{:S(2)}) copy-start(f32[32]{0:T(128)} %param.6) | copy-start | bytes 388
  9.3 0.9 %copy-start.2 = (bf16[32,64,3,3,3]{1,0,4,3,2:T(8,128)(2,1)S(1)}, bf16[32,64,3,3,3]{1,0,4,3,2:T(8,128)(2,1)}, u32[]{:S(2)}) copy-start(bf16[32,64,3,3,3]{1,0,4,3,2:T(8,128)(2,1)} %param.5) | copy-start | bytes 331780
  10.6 10.4 %collective-permute-start.5 = (bf16[41,32,128]{2,1,0:T(8,128)(2,1)S(1)}, bf16[41,32,128]{2,1,0:T(8,128)(2,1)S(1)}, u32[]{:S(2)}, u32[]{:S(2)}) collective-permute-start(bf16[41,32,128]{2,1,0:T(8,128)(2,1)S(1)} %get-tuple-element.28), channel_id=1, source_target_pairs={{0,1},{1,0},{2,3},{3,2},{4,5},{5,4},{6,7},{7,6},{8,9},{9,8},{10,11... | collective-permute-start | bytes 1007624 | tf_op jit(solution)/shard_map/ppermute | solution.py:334
  13.1 8.2 %collective-permute-start.4 = (bf16[28,32,128]{2,1,0:T(8,128)(2,1)S(1)}, bf16[28,32,128]{2,1,0:T(8,128)(2,1)S(1)}, u32[]{:S(2)}, u32[]{:S(2)}) collective-permute-start(bf16[28,32,128]{2,1,0:T(8,128)(2,1)S(1)} %collective-permute-done.refs_1_), channel_id=1, source_target_pairs={{2,4},{3,5},{6,8},{7,9},{10,12},{11,13},{14,16},{15,17},{18,20},{1... | collective-permute-start | bytes 688136 | tf_op jit(solution)/shard_map/ppermute | solution.py:342
  16.8 4.5 %collective-permute-start.3 = (bf16[28,32,128]{2,1,0:T(8,128)(2,1)S(1)}, bf16[28,32,128]{2,1,0:T(8,128)(2,1)S(1)}, u32[]{:S(2)}, u32[]{:S(2)}) collective-permute-start(bf16[28,32,128]{2,1,0:T(8,128)(2,1)S(1)} %collective-permute-done.refs_1_), channel_id=1, source_target_pairs={{0,2},{2,0},{4,6},{6,4},{8,10},{10,8},{12,14},{14,12},{16,18},{18,... | collective-permute-start | bytes 688136 | tf_op jit(solution)/shard_map/ppermute | solution.py:338
  24.4 1.4 %collective-permute-start.10 = (bf16[2,48,640]{2,1,0:T(8,128)(2,1)S(1)}, bf16[2,48,640]{2,1,0:T(8,128)(2,1)S(1)}, u32[]{:S(2)}, u32[]{:S(2)}) collective-permute-start(bf16[2,48,640]{2,1,0:T(8,128)(2,1)S(1)} %get-tuple-element.37), channel_id=1, source_target_pairs={{0,2},{2,0},{4,6},{6,4},{8,10},{10,8},{12,14},{14,12},{16,18},{18,... | collective-permute-start | bytes 368648 | tf_op jit(solution)/shard_map/ppermute | solution.py:338
  25.9 4.8 %collective-permute-start.12 = (bf16[48,640]{1,0:T(8,128)(2,1)S(1)}, bf16[48,640]{1,0:T(8,128)(2,1)S(1)}, u32[]{:S(2)}, u32[]{:S(2)}) collective-permute-start(bf16[48,640]{1,0:T(8,128)(2,1)S(1)} %get-tuple-element.44), channel_id=1, source_target_pairs={{0,8},{1,9},{2,10},{3,11},{4,12},{5,13},{6,14},{7,15},{8,0},{9,1},... | collective-permute-start | bytes 184328 | tf_op jit(solution)/shard_map/ppermute | solution.py:418
  26.0 5.6 %collective-permute-start.13 = (bf16[48,640]{1,0:T(8,128)(2,1)S(1)}, bf16[48,640]{1,0:T(8,128)(2,1)S(1)}, u32[]{:S(2)}, u32[]{:S(2)}) collective-permute-start(bf16[48,640]{1,0:T(8,128)(2,1)S(1)} %get-tuple-element.45), channel_id=1, source_target_pairs={{0,9},{1,8},{2,11},{3,10},{4,13},{5,12},{6,15},{7,14},{8,1},{9,0},... | collective-permute-start | bytes 184328 | tf_op jit(solution)/shard_map/ppermute | solution.py:418
  27.9 4.6 %collective-permute-start.11 = (bf16[48,640]{1,0:T(8,128)(2,1)S(1)}, bf16[48,640]{1,0:T(8,128)(2,1)S(1)}, u32[]{:S(2)}, u32[]{:S(2)}) collective-permute-start(bf16[48,640]{1,0:T(8,128)(2,1)S(1)} %get-tuple-element.45), channel_id=1, source_target_pairs={{0,1},{1,0},{2,3},{3,2},{4,5},{5,4},{6,7},{7,6},{8,9},{9,8},{10,11... | collective-permute-start | bytes 184328 | tf_op jit(solution)/shard_map/ppermute | solution.py:334
  29.4 10.5 %collective-permute-start.8 = (bf16[26,64,128]{2,1,0:T(8,128)(2,1)S(1)}, bf16[26,64,128]{2,1,0:T(8,128)(2,1)S(1)}, u32[]{:S(2)}, u32[]{:S(2)}) collective-permute-start(bf16[26,64,128]{2,1,0:T(8,128)(2,1)S(1)} %get-tuple-element.32.refs_0_.refs_6_), channel_id=1, source_target_pairs={{2,4},{3,5},{6,8},{7,9},{10,12},{11,13},{14,16},{15,17},{18,20},{1... | collective-permute-start | bytes 1277960 | tf_op jit(solution)/shard_map/ppermute | solution.py:342
  30.0 10.0 %collective-permute-start.7 = (bf16[26,64,128]{2,1,0:T(8,128)(2,1)S(1)}, bf16[26,64,128]{2,1,0:T(8,128)(2,1)S(1)}, u32[]{:S(2)}, u32[]{:S(2)}) collective-permute-start(bf16[26,64,128]{2,1,0:T(8,128)(2,1)S(1)} %get-tuple-element.32.refs_0_.refs_6_), channel_id=1, source_target_pairs={{0,2},{2,0},{4,6},{6,4},{8,10},{10,8},{12,14},{14,12},{16,18},{18,... | collective-permute-start | bytes 1277960 | tf_op jit(solution)/shard_map/ppermute | solution.py:338
  32.6 6.4 %collective-permute-start.14 = (bf16[48,640]{1,0:T(8,128)(2,1)S(1)}, bf16[48,640]{1,0:T(8,128)(2,1)S(1)}, u32[]{:S(2)}, u32[]{:S(2)}) collective-permute-start(bf16[48,640]{1,0:T(8,128)(2,1)S(1)} %add_convert_fusion.2), channel_id=1, source_target_pairs={{0,16},{2,18},{4,20},{6,22},{8,24},{10,26},{12,28},{14,30},{16,0},... | collective-permute-start | bytes 184328 | tf_op jit(solution)/shard_map/ppermute | solution.py:468
  34.7 8.7 %collective-permute-start.6 = (bf16[24,32,128]{2,1,0:T(8,128)(2,1)S(1)}, bf16[24,32,128]{2,1,0:T(8,128)(2,1)S(1)}, u32[]{:S(2)}, u32[]{:S(2)}) collective-permute-start(bf16[24,32,128]{2,1,0:T(8,128)(2,1)S(1)} %get-tuple-element.31), channel_id=1, source_target_pairs={{0,1},{1,0},{2,3},{3,2},{4,5},{5,4},{6,7},{7,6},{8,9},{9,8},{10,11... | collective-permute-start | bytes 589832 | tf_op jit(solution)/shard_map/ppermute | solution.py:334
  39.0 4.3 %collective-permute-start.15 = (bf16[48,640]{1,0:T(8,128)(2,1)S(1)}, bf16[48,640]{1,0:T(8,128)(2,1)S(1)}, u32[]{:S(2)}, u32[]{:S(2)}) collective-permute-start(bf16[48,640]{1,0:T(8,128)(2,1)S(1)} %add_convert_fusion.1), channel_id=1, source_target_pairs={{0,4},{2,6},{4,0},{6,2},{8,12},{10,14},{12,8},{14,10},{16,20},{18,... | collective-permute-start | bytes 184328 | tf_op jit(solution)/shard_map/ppermute | solution.py:468
  41.3 6.1 %collective-permute-start.9 = (bf16[24,32,128]{2,1,0:T(8,128)(2,1)S(1)}, bf16[24,32,128]{2,1,0:T(8,128)(2,1)S(1)}, u32[]{:S(2)}, u32[]{:S(2)}) collective-permute-start(bf16[24,32,128]{2,1,0:T(8,128)(2,1)S(1)} %get-tuple-element.35), channel_id=1, source_target_pairs={{0,1},{1,0},{2,3},{3,2},{4,5},{5,4},{6,7},{7,6},{8,9},{9,8},{10,11... | collective-permute-start | bytes 589832 | tf_op jit(solution)/shard_map/ppermute | solution.py:334
  43.3 1.4 %collective-permute-start.16 = (f32[48,640]{1,0:T(8,128)S(1)}, f32[48,640]{1,0:T(8,128)S(1)}, u32[]{:S(2)}, u32[]{:S(2)}) collective-permute-start(f32[48,640]{1,0:T(8,128)S(1)} %convert_add_fusion.mine), channel_id=1, source_target_pairs={{0,2},{2,0},{4,6},{6,4},{8,10},{10,8},{12,14},{14,12},{16,18},{18,... | collective-permute-start | bytes 368648 | tf_op jit(solution)/shard_map/ppermute | solution.py:338

commit v3 on v1

--- a/solution.py
+++ b/solution.py
@@ -11,22 +11,14 @@
 leakage = 0.1
 bf16 = jnp.bfloat16
 f32 = jnp.float32
-DBAR = 0
-IBAR = 9
-ABAR = 9
-UBAR = False
-ZHOP = 2
-GBAR = 9
-VWRAP = True
-VWRAP2 = True
-DWRAP = False
 LIMIT = 48 * 1024 * 1024
 
 
-def call(body, out_shape, scratch, flops, nbytes, trans=0, name=None):
+def call(body, out_shape, scratch, flops, nbytes, trans=0, name=None, **specs):
     return pl.pallas_call(
         body,
         out_shape=out_shape,
+        **specs,
         scratch_shapes=scratch,
         compiler_params=pltpu.CompilerParams(vmem_limit_bytes=LIMIT),
         cost_estimate=pl.CostEstimate(
@@ -161,13 +153,12 @@
     return y[full : 2 * full] + left + right
 
 
-def forward_body(nchan, rows, *refs):
+def forward_body(nchan, rows, step, *refs):
     own, sib, pair = refs[:nchan], refs[nchan : 2 * nchan], refs[2 * nchan : 3 * nchan]
     ups = refs[3 * nchan : 4 * nchan]
     filters = refs[4 * nchan]
     outs = refs[4 * nchan + 1 : 5 * nchan + 1]
-    delta = refs[5 * nchan + 1]
-    planes, upstream, activated = refs[5 * nchan + 2 :]
+    delta, kept, sent, planes, upstream, activated, acc = refs[5 * nchan + 1 :]
     part = lax.axis_index("chan")
     share = own[0].shape[1]
     full = nchan * share
@@ -195,17 +186,6 @@
                 activated[r - 1] = act.reshape(nchan, share, 128)
     for k in range(nchan):
         outs[k][...] = activated[:, lax.rem(part + k, nchan)]
-
-
-def wgrad_body(nchan, rows, step, *refs):
-    own, sib, pair = refs[:nchan], refs[nchan : 2 * nchan], refs[2 * nchan : 3 * nchan]
-    delta = refs[3 * nchan]
-    kept, sent, planes, acc = refs[3 * nchan + 1 :]
-    part = lax.axis_index("chan")
-    share = own[0].shape[1]
-    full = nchan * share
-    gather_planes(nchan, planes, own, None, sib, pair)
-    extra = ones_rows(128)
     lane = lax.broadcasted_iota(jnp.int32, (full, 128), 1)
     total = None
     for g in range(rows // step):
@@ -269,7 +249,7 @@
 
 def unpack_body(nchan, rows, height, *refs):
     blocks = refs[:nchan]
-    out, flat = refs[nchan:]
+    out, staged, flat, sems = refs[nchan:]
     share = out.shape[0]
     part = lax.axis_index("chan")
     size = rows * share
@@ -278,8 +258,15 @@
         flat[pl.ds(pl.multiple_of(q * size, 8), size)] = (
             blocks[k][...].astype(f32).reshape(size, 128)
         )
-    for ch in range(share):
-        out[ch] = flat[pl.ds(ch, height, stride=share)].astype(bf16)
+    copies = []
+    for n in range(4):
+        group = pl.ds(n * (share // 4), share // 4)
+        for ch in range(n * (share // 4), (n + 1) * (share // 4)):
+            staged[ch] = flat[pl.ds(ch, height, stride=share)].astype(bf16)
+        copies.append(pltpu.make_async_copy(staged.at[group], out.at[group], sems.at[n]))
+        copies[-1].start()
+    for copy in copies:
+        copy.wait()
 
 
 def finish_body(share, factor, mine, other, out, bias, both):
@@ -355,7 +342,7 @@
         name="pack_volume",
     )(volume.reshape(share, height, width))
     v_got = over_chan(v_out)
-    own_sib, own_pair = to_sib(v_own), to_pair(v_own, VWRAP)
+    own_sib, own_pair = to_sib(v_own), to_pair(v_own, True)
     u_own, *u_out = call(
         functools.partial(pack_rest_body, nchan, rows),
         [u_shape] * nchan,
@@ -367,12 +354,10 @@
         3 * block,
         name="pack_rest",
     )(upstream.reshape(share, height, width), slabs, bias.reshape(1, share))
-    if UBAR:
-        u_out, v_got = lax.optimization_barrier((u_out, v_got))
-    v_got, own_sib, own_pair = lax.optimization_barrier((v_got, own_sib, own_pair))
+    v_got, own_pair = lax.optimization_barrier((v_got, own_pair))
     mine = [v_own] + v_got
     sib = [own_sib] + [to_sib(x) for x in v_got]
-    pair = [own_pair] + [to_pair(x, VWRAP2) for x in v_got]
+    pair = [own_pair] + [to_pair(x, True) for x in v_got]
     u_got = over_chan(u_out)
     w_forward, w_backward = call(
         functools.partial(filters_body, nchan, rows),
@@ -385,54 +370,68 @@
     planes = pltpu.VMEM((rows + 4, 3, nchan, share, 128), bf16)
     cells = rows * width
     a_shape = shape(rows, share, 128)
-    *act, delta = call(
-        functools.partial(forward_body, nchan, rows),
-        [a_shape] * nchan + [shape(rows + 2, full, 128)],
+    step = 4 if rows % 4 == 0 else 1
+    h_shape = (nchan, 3 * share // 2, 640)
+    *act, delta, kept, sent = call(
+        functools.partial(forward_body, nchan, rows, step),
+        [a_shape] * nchan
+        + [shape(rows + 2, full, 128), shape(*h_shape, dtype=f32), shape(*h_shape)],
         [
             planes,
             pltpu.VMEM((rows + 2, nchan, share, 128), bf16),
             pltpu.VMEM((rows, nchan, share, 128), bf16),
+            pltpu.VMEM((3 * full, 640), f32),
         ],
-        2 * 27 * full * full * cells,
-        6 * block,
+        4 * 27 * full * full * cells,
+        8 * block,
         2 * full * cells,
         name="forward",
     )(*mine, *sib, *pair, u_own, *u_got, w_forward)
-    d_sib, d_pair = to_sib(delta), to_pair(delta, DWRAP)
-    step = 4 if rows % 4 == 0 else 1
-    h_shape = (nchan, 3 * share // 2, 640)
-    kept, sent = call(
-        functools.partial(wgrad_body, nchan, rows, step),
-        [shape(*h_shape, dtype=f32), shape(*h_shape)],
-        [planes, pltpu.VMEM((3 * full, 640), f32)],
-        2 * 27 * full * full * cells,
-        6 * block,
-        name="wgrad",
-    )(*mine, *sib, *pair, delta)
+    d_sib, d_pair = to_sib(delta), to_pair(delta, False)
     kept = kept + to_sib(sent).astype(f32)
     sent = [kept[k].astype(bf16) for k in range(nchan)]
-    near = kept_sum(sent[0], over_chan(sent[1:]))
-    far = [
-        lax.ppermute(
-            sent[k],
-            ("space", "chan"),
-            [
-                (i * nchan + c, (i ^ 2 * ZHOP) * nchan + (c + k) % nchan)
-                for i in range(nspace)
-                for c in range(nchan)
-            ],
-        )
-        for k in range(nchan)
-    ]
-    total = near + kept_sum(far[0], far[1:])
+
+    def from_hop(blocks, hop):
+        got = [
+            lax.ppermute(
+                blocks[k],
+                ("space", "chan"),
+                [
+                    (i * nchan + c, (i ^ hop) * nchan + (c + k) % nchan)
+                    for i in range(nspace)
+                    for c in range(nchan)
+                ],
+            )
+            for k in range(len(blocks))
+            if hop or k
+        ]
+        got = got if hop else [blocks[0]] + got
+        return kept_sum(got[0], got[1:])
+
+    def from_hops(blocks, hops):
+        reach = [0]
+        for hop in hops:
+            reach += [hop ^ other for other in reach]
+        sums = [from_hop(blocks, hop) for hop in reach]
+        while len(sums) > 1:
+            sums = [a + b for a, b in zip(sums[0::2], sums[1::2])]
+        return sums[0]
+
+    near = 4 if nspace > 4 else 2
+    total = from_hops(sent, (near,))
     def unpack(blocks, name):
         out = call(
             functools.partial(unpack_body, nchan, rows, height),
             shape(share, height, width),
-            [pltpu.VMEM((height * share, 128), f32)],
+            [
+                pltpu.VMEM((share, height, width), bf16),
+                pltpu.VMEM((height * share, 128), f32),
+                pltpu.SemaphoreType.DMA((4,)),
+            ],
             0,
             2 * block,
             name=name,
+            out_specs=pl.BlockSpec(memory_space=pl.ANY),
         )(*blocks)
         return out.reshape(share, 1, height, width)
 
@@ -449,20 +448,9 @@
         name="backward",
     )(delta, d_sib, d_pair, w_backward)
     ig_got = over_chan(ig[1:])
-    hops = [1 << n for n in range(1, nspace.bit_length() - 1)]
-    hops.remove(2 * ZHOP)
-    for n, hop in enumerate(hops[1:] + hops[:1]):
-        if n == DBAR:
-            total, d_sib, d_pair = lax.optimization_barrier((total, d_sib, d_pair))
-        if n == IBAR:
-            total, ig = lax.optimization_barrier((total, ig))
-        if n == GBAR:
-            total, ig_got = lax.optimization_barrier((total, ig_got))
-        if n == ABAR:
-            total, activated = lax.optimization_barrier((total, activated))
-        sent = total.astype(bf16)
-        came = lax.ppermute(sent, "space", [(i, i ^ hop) for i in range(nspace)])
-        total = sent.astype(f32) + came.astype(f32)
+    hops = [1 << n for n in range(1, nspace.bit_length() - 1) if 1 << n != near]
+    for hop in hops[1:] + hops[:1]:
+        total = from_hops([total.astype(bf16)], (hop,))
     summed = to_sib(total)
 
     input_grad = unpack([ig[0]] + ig_got, "unpack_input_grad")

time: 51.7 us -> 48.5 us (0.938)
  waiting for transfers between devices: 18.6 us -> 16.2 us
    ppermute x5 -> x4, waiting for transfers between devices: 6.53 us -> 3.31 us  [over_chan(): got.append(lax.ppermute(blocks[k - 1], 'chan', perm))]
    ppermute x3, waiting for transfers between devices: 1.95 us -> 4.48 us  [to_pair(): return lax.ppermute(x, ('space', 'chan'), perm)]
    ppermute x4 -> x5, waiting for transfers between devices: 9.41 us -> 6.93 us  [from_hop(): lax.ppermute(blocks[k], ('space', 'chan'), [(i * nchan + c, (i ^ hop) * n...]
    ppermute x4 -> x5, starting transfers between devices: 5.79 us -> 6.75 us  [from_hop(): lax.ppermute(blocks[k], ('space', 'chan'), [(i * nchan + c, (i ^ hop) * n...]
    ppermute x5 -> x4, starting transfers between devices: 6.63 us -> 5.75 us  [over_chan(): got.append(lax.ppermute(blocks[k - 1], 'chan', perm))]
    ppermute x5, waiting for transfers between devices: 0.72 us -> 1.45 us  [to_sib(): return lax.ppermute(x, 'space', sib_perm)]
    pallas_call x2 -> x1, Pallas kernels: 3.09 us -> 2.77 us  [shards(): call(functools.partial(forward_body, nchan, rows, step), [a_shape] * ncha...]
  transfers between devices with their start and end apart: 17 -> 17, of which waited for: 8 -> 11; matrix products, arithmetic and copies ran while one was open for 0% -> 0% of each run, Pallas kernels for 9% -> 9%
where the time goes in v3:
time: 48.5 us; the launch traced here: 48.3 us
  starting transfers between devices  20.3 us (42%)
  waiting for transfers between devices  16.2 us (33%)
  Pallas kernels  8.37 us (17%)
  local copies, waits for them, and re-layouts  2.59 us (5%)
  between operations  0.75 us (2%)
    ppermute x3, starting transfers between devices, to_pair(): return lax.ppermute(x, ('space', 'chan'), perm)  7.6 us
    ppermute x5, waiting for transfers between devices, from_hop(): lax.ppermute(blocks[k], ('space', 'chan'), [(i * nchan + c, (i ^ hop) * n...  6.93 us
    ppermute x5, starting transfers between devices, from_hop(): lax.ppermute(blocks[k], ('space', 'chan'), [(i * nchan + c, (i ^ hop) * n...  6.75 us
    ppermute x4, starting transfers between devices, over_chan(): got.append(lax.ppermute(blocks[k - 1], 'chan', perm))  5.75 us
    ppermute x3, waiting for transfers between devices, to_pair(): return lax.ppermute(x, ('space', 'chan'), perm)  4.48 us
    ppermute x4, waiting for transfers between devices, over_chan(): got.append(lax.ppermute(blocks[k - 1], 'chan', perm))  3.31 us
    pallas_call x1, Pallas kernels, shards(): call(functools.partial(forward_body, nchan, rows, step), [a_shape] * ncha...  2.77 us
    unnamed x8, local copies, waits for them, and re-layouts  2.58 us
  transfers between devices with their start and end apart: 17, of which 11 were waited for; matrix products, arithmetic and copies ran while one was open for 0% of the time, Pallas kernels for 9%

profile of v3, /device:TPU:0, one launch (start us, length us, event | category | flops | bytes accessed | tf_op | source)
XLA Modules:
  0.0 48.3 jit_solution(9731494085627518131)
XLA Ops:
  0.6 1.0 %copy-done = bf16[32,1,48,128]{3,2,1,0:T(8,128)(2,1)S(1)} copy-done((bf16[32,1,48,128]{3,2,1,0:T(8,128)(2,1)S(1)}, bf16[32,1,48,128]{3,2,1,0:T(8,128)(2,1)}, u32[]{:S(2)}) %copy-start) | copy-done | bytes 393240
  1.9 3.0 %collective-permute-start = (bf16[28,32,128]{2,1,0:T(8,128)(2,1)S(1)}, bf16[28,32,128]{2,1,0:T(8,128)(2,1)S(1)}, u32[]{:S(2)}, u32[]{:S(2)}) collective-permute-start(bf16[28,32,128]{2,1,0:T(8,128)(2,1)S(1)} %get-tuple-element.22), channel_id=1, source_target_pairs={{0,1},{1,0},{2,3},{3,2},{4,5},{5,4},{6,7},{7,6},{8,9},{9,8},{10,11... | collective-permute-start | bytes 688136 | tf_op jit(solution)/shard_map/ppermute | solution.py:319
  5.0 3.7 %collective-permute-start.1 = (bf16[28,32,128]{2,1,0:T(8,128)(2,1)S(1)}, bf16[28,32,128]{2,1,0:T(8,128)(2,1)S(1)}, u32[]{:S(2)}, u32[]{:S(2)}) collective-permute-start(bf16[28,32,128]{2,1,0:T(8,128)(2,1)S(1)} %get-tuple-element.21.refs_0_), channel_id=1, source_target_pairs={{2,4},{3,5},{6,8},{7,9},{10,12},{11,13},{14,16},{15,17},{18,20},{1... | collective-permute-start | bytes 688136 | tf_op jit(solution)/shard_map/ppermute | solution.py:327
  9.3 0.9 %copy-done.2 = bf16[32,64,3,3,3]{1,0,4,3,2:T(8,128)(2,1)S(1)} copy-done((bf16[32,64,3,3,3]{1,0,4,3,2:T(8,128)(2,1)S(1)}, bf16[32,64,3,3,3]{1,0,4,3,2:T(8,128)(2,1)}, u32[]{:S(2)}) %copy-start.2) | copy-done | bytes 110616
  11.2 1.9 %collective-permute-done.1.refs_4_ = bf16[28,32,128]{2,1,0:T(8,128)(2,1)S(1)} collective-permute-done((bf16[28,32,128]{2,1,0:T(8,128)(2,1)S(1)}, bf16[28,32,128]{2,1,0:T(8,128)(2,1)S(1)}, u32[]{:S(2)}, u32[]{:S(2)}) %collective-permute-start.1) | collective-permute-done | bytes 229408 | tf_op jit(solution)/shard_map/ppermute | solution.py:327
  13.1 3.7 %collective-permute-start.4 = (bf16[28,32,128]{2,1,0:T(8,128)(2,1)S(1)}, bf16[28,32,128]{2,1,0:T(8,128)(2,1)S(1)}, u32[]{:S(2)}, u32[]{:S(2)}) collective-permute-start(bf16[28,32,128]{2,1,0:T(8,128)(2,1)S(1)} %collective-permute-done.refs_1_), channel_id=1, source_target_pairs={{2,4},{3,5},{6,8},{7,9},{10,12},{11,13},{14,16},{15,17},{18,20},{1... | collective-permute-start | bytes 688136 | tf_op jit(solution)/shard_map/ppermute | solution.py:327
  16.8 1.5 %collective-permute-done.5.refs_1_.refs_7_ = bf16[41,32,128]{2,1,0:T(8,128)(2,1)S(1)} collective-permute-done((bf16[41,32,128]{2,1,0:T(8,128)(2,1)S(1)}, bf16[41,32,128]{2,1,0:T(8,128)(2,1)S(1)}, u32[]{:S(2)}, u32[]{:S(2)}) %collective-permute-start.5) | collective-permute-done | bytes 335904 | tf_op jit(solution)/shard_map/ppermute | solution.py:319
  18.7 2.5 %collective-permute-done.4.refs_5_ = bf16[28,32,128]{2,1,0:T(8,128)(2,1)S(1)} collective-permute-done((bf16[28,32,128]{2,1,0:T(8,128)(2,1)S(1)}, bf16[28,32,128]{2,1,0:T(8,128)(2,1)S(1)}, u32[]{:S(2)}, u32[]{:S(2)}) %collective-permute-start.4) | collective-permute-done | bytes 229408 | tf_op jit(solution)/shard_map/ppermute | solution.py:327
  21.3 2.8 %forward.1 = (bf16[24,32,128]{2,1,0:T(8,128)(2,1)S(1)}, bf16[24,32,128]{2,1,0:T(8,128)(2,1)S(1)}, bf16[26,64,128]{2,1,0:T(8,128)(2,1)S(1)}, f32[2,48,640]{2,1,0:T(8,128)S(1)}, bf16[2,48,640]{2,1,0:T(8,128)(2,1)S(1)}) custom-call(bf16[28,32,128]{2,1,0:T(8,128)(2,1)S(1)} %get-tuple-element.21.refs_0_, bf16[28,32,128]{2,1,0:T(8,128)(2,1)S(1)} %collective-permute-done.refs_1_, ...), custom_call_target="tpu_custom_call" | custom-call | flops 1358954496 | bytes 3145728 | tf_op jit(solution)/shard_map/forward/pallas_call | solution.py:375
  24.1 1.3 %collective-permute-done.10 = bf16[2,48,640]{2,1,0:T(8,128)(2,1)S(1)} collective-permute-done((bf16[2,48,640]{2,1,0:T(8,128)(2,1)S(1)}, bf16[2,48,640]{2,1,0:T(8,128)(2,1)S(1)}, u32[]{:S(2)}, u32[]{:S(2)}) %collective-permute-start.10) | collective-permute-done | bytes 122912 | tf_op jit(solution)/shard_map/ppermute | solution.py:323
  25.6 1.6 %collective-permute-start.13 = (bf16[48,640]{1,0:T(8,128)(2,1)S(1)}, bf16[48,640]{1,0:T(8,128)(2,1)S(1)}, u32[]{:S(2)}, u32[]{:S(2)}) collective-permute-start(bf16[48,640]{1,0:T(8,128)(2,1)S(1)} %get-tuple-element.43), channel_id=1, source_target_pairs={{0,9},{1,8},{2,11},{3,10},{4,13},{5,12},{6,15},{7,14},{8,1},{9,0},... | collective-permute-start | bytes 184328 | tf_op jit(solution)/shard_map/ppermute | solution.py:396
  27.2 1.8 %collective-permute-start.11 = (bf16[48,640]{1,0:T(8,128)(2,1)S(1)}, bf16[48,640]{1,0:T(8,128)(2,1)S(1)}, u32[]{:S(2)}, u32[]{:S(2)}) collective-permute-start(bf16[48,640]{1,0:T(8,128)(2,1)S(1)} %get-tuple-element.43), channel_id=1, source_target_pairs={{0,1},{1,0},{2,3},{3,2},{4,5},{5,4},{6,7},{7,6},{8,9},{9,8},{10,11... | collective-permute-start | bytes 184328 | tf_op jit(solution)/shard_map/ppermute | solution.py:396
  29.3 1.0 %collective-permute-done.12 = bf16[48,640]{1,0:T(8,128)(2,1)S(1)} collective-permute-done((bf16[48,640]{1,0:T(8,128)(2,1)S(1)}, bf16[48,640]{1,0:T(8,128)(2,1)S(1)}, u32[]{:S(2)}, u32[]{:S(2)}) %collective-permute-start.12) | collective-permute-done | bytes 61472 | tf_op jit(solution)/shard_map/ppermute | solution.py:396
  30.8 1.1 %collective-permute-done.11 = bf16[48,640]{1,0:T(8,128)(2,1)S(1)} collective-permute-done((bf16[48,640]{1,0:T(8,128)(2,1)S(1)}, bf16[48,640]{1,0:T(8,128)(2,1)S(1)}, u32[]{:S(2)}, u32[]{:S(2)}) %collective-permute-start.11) | collective-permute-done | bytes 61472 | tf_op jit(solution)/shard_map/ppermute | solution.py:396
  32.0 2.4 %collective-permute-start.14 = (bf16[48,640]{1,0:T(8,128)(2,1)S(1)}, bf16[48,640]{1,0:T(8,128)(2,1)S(1)}, u32[]{:S(2)}, u32[]{:S(2)}) collective-permute-start(bf16[48,640]{1,0:T(8,128)(2,1)S(1)} %add_convert_fusion.2), channel_id=1, source_target_pairs={{0,16},{1,17},{2,18},{3,19},{4,20},{5,21},{6,22},{7,23},{8,24},{9,... | collective-permute-start | bytes 184328 | tf_op jit(solution)/shard_map/ppermute | solution.py:396
  34.4 0.8 %collective-permute-start.6 = (bf16[24,32,128]{2,1,0:T(8,128)(2,1)S(1)}, bf16[24,32,128]{2,1,0:T(8,128)(2,1)S(1)}, u32[]{:S(2)}, u32[]{:S(2)}) collective-permute-start(bf16[24,32,128]{2,1,0:T(8,128)(2,1)S(1)} %get-tuple-element.29), channel_id=1, source_target_pairs={{0,1},{1,0},{2,3},{3,2},{4,5},{5,4},{6,7},{7,6},{8,9},{9,8},{10,11... | collective-permute-start | bytes 589832 | tf_op jit(solution)/shard_map/ppermute | solution.py:319
  35.2 3.5 %collective-permute-done.14 = bf16[48,640]{1,0:T(8,128)(2,1)S(1)} collective-permute-done((bf16[48,640]{1,0:T(8,128)(2,1)S(1)}, bf16[48,640]{1,0:T(8,128)(2,1)S(1)}, u32[]{:S(2)}, u32[]{:S(2)}) %collective-permute-start.14) | collective-permute-done | bytes 61472 | tf_op jit(solution)/shard_map/ppermute | solution.py:396
  38.7 0.8 %collective-permute-start.15 = (bf16[48,640]{1,0:T(8,128)(2,1)S(1)}, bf16[48,640]{1,0:T(8,128)(2,1)S(1)}, u32[]{:S(2)}, u32[]{:S(2)}) collective-permute-start(bf16[48,640]{1,0:T(8,128)(2,1)S(1)} %add_convert_fusion.1), channel_id=1, source_target_pairs={{0,4},{1,5},{2,6},{3,7},{4,0},{5,1},{6,2},{7,3},{8,12},{9,13},{10,... | collective-permute-start | bytes 184328 | tf_op jit(solution)/shard_map/ppermute | solution.py:396
  39.5 1.4 %backward.1 = (bf16[24,32,128]{2,1,0:T(8,128)(2,1)S(1)}, bf16[24,32,128]{2,1,0:T(8,128)(2,1)S(1)}) custom-call(bf16[26,64,128]{2,1,0:T(8,128)(2,1)S(1)} %get-tuple-element.30.refs_0_, bf16[26,64,128]{2,1,0:T(8,128)(2,1)S(1)} %collective-permute-done.7.refs_1_, bf16[26,64,128]{2,1,0:T(8,128)(2,1)S(1)} %collective-permute-done.8.refs_2_, ...), custom_call_target="tpu_custom_call" | custom-call | flops 679477248 | bytes 2359296 | tf_op jit(solution)/shard_map/backward/pallas_call | solution.py:439
  40.9 1.4 %collective-permute-start.9 = (bf16[24,32,128]{2,1,0:T(8,128)(2,1)S(1)}, bf16[24,32,128]{2,1,0:T(8,128)(2,1)S(1)}, u32[]{:S(2)}, u32[]{:S(2)}) collective-permute-start(bf16[24,32,128]{2,1,0:T(8,128)(2,1)S(1)} %get-tuple-element.33), channel_id=1, source_target_pairs={{0,1},{1,0},{2,3},{3,2},{4,5},{5,4},{6,7},{7,6},{8,9},{9,8},{10,11... | collective-permute-start | bytes 589832 | tf_op jit(solution)/shard_map/ppermute | solution.py:319
  43.1 1.2 %unpack_activated.1 = bf16[32,48,128]{2,1,0:T(8,128)(2,1)} custom-call(bf16[24,32,128]{2,1,0:T(8,128)(2,1)S(1)} %get-tuple-element.28.refs_0_, bf16[24,32,128]{2,1,0:T(8,128)(2,1)S(1)} %collective-permute-done.6.refs_1_), custom_call_target="tpu_custom_call" | custom-call | bytes 786432 | tf_op jit(solution)/shard_map/unpack_activated/pallas_call | solution.py:423
  44.4 0.9 %finish.1 = (f32[27,32,64]{2,1,0:T(8,128)}, f32[1,32]{1,0:T(1,128)}) custom-call(f32[48,640]{1,0:T(8,128)S(1)} %convert_add_fusion.mine, f32[48,640]{1,0:T(8,128)S(1)} %collective-permute-done.16.other), custom_call_target="tpu_custom_call" | custom-call | bytes 1048576 | tf_op jit(solution)/shard_map/finish/pallas_call | solution.py:457
  45.3 1.8 %collective-permute-done.9.refs_1_ = bf16[24,32,128]{2,1,0:T(8,128)(2,1)S(1)} collective-permute-done((bf16[24,32,128]{2,1,0:T(8,128)(2,1)S(1)}, bf16[24,32,128]{2,1,0:T(8,128)(2,1)S(1)}, u32[]{:S(2)}, u32[]{:S(2)}) %collective-permute-start.9) | collective-permute-done | bytes 196640 | tf_op jit(solution)/shard_map/ppermute | solution.py:319
  47.1 1.2 %unpack_input_grad.1 = bf16[32,48,128]{2,1,0:T(8,128)(2,1)} custom-call(bf16[24,32,128]{2,1,0:T(8,128)(2,1)S(1)} %get-tuple-element.32.refs_0_, bf16[24,32,128]{2,1,0:T(8,128)(2,1)S(1)} %collective-permute-done.9.refs_1_), custom_call_target="tpu_custom_call" | custom-call | bytes 786432 | tf_op jit(solution)/shard_map/unpack_input_grad/pallas_call | solution.py:423
  (31 shorter events, 4.1 us)
Async XLA Ops:
  0.6 1.0 %copy-start = (bf16[32,1,48,128]{3,2,1,0:T(8,128)(2,1)S(1)}, bf16[32,1,48,128]{3,2,1,0:T(8,128)(2,1)}, u32[]{:S(2)}) copy-start(bf16[32,1,48,128]{3,2,1,0:T(8,128)(2,1)} %param.4) | copy-start | bytes 1179652
  1.6 7.0 %copy-start.1 = (bf16[32,1,48,128]{3,2,1,0:T(8,128)(2,1)S(1)}, bf16[32,1,48,128]{3,2,1,0:T(8,128)(2,1)}, u32[]{:S(2)}) copy-start(bf16[32,1,48,128]{3,2,1,0:T(8,128)(2,1)} %param.7) | copy-start | bytes 1179652
  1.9 9.2 %collective-permute-start = (bf16[28,32,128]{2,1,0:T(8,128)(2,1)S(1)}, bf16[28,32,128]{2,1,0:T(8,128)(2,1)S(1)}, u32[]{:S(2)}, u32[]{:S(2)}) collective-permute-start(bf16[28,32,128]{2,1,0:T(8,128)(2,1)S(1)} %get-tuple-element.22), channel_id=1, source_target_pairs={{0,1},{1,0},{2,3},{3,2},{4,5},{5,4},{6,7},{7,6},{8,9},{9,8},{10,11... | collective-permute-start | bytes 688136 | tf_op jit(solution)/shard_map/ppermute | solution.py:319
  5.0 8.1 %collective-permute-start.1 = (bf16[28,32,128]{2,1,0:T(8,128)(2,1)S(1)}, bf16[28,32,128]{2,1,0:T(8,128)(2,1)S(1)}, u32[]{:S(2)}, u32[]{:S(2)}) collective-permute-start(bf16[28,32,128]{2,1,0:T(8,128)(2,1)S(1)} %get-tuple-element.21.refs_0_), channel_id=1, source_target_pairs={{2,4},{3,5},{6,8},{7,9},{10,12},{11,13},{14,16},{15,17},{18,20},{1... | collective-permute-start | bytes 688136 | tf_op jit(solution)/shard_map/ppermute | solution.py:327
  8.7 0.7 %copy-start.3 = (f32[32]{0:T(128)S(1)}, f32[32]{0:T(128)}, u32[]{:S(2)}) copy-start(f32[32]{0:T(128)} %param.6) | copy-start | bytes 388
  9.3 0.9 %copy-start.2 = (bf16[32,64,3,3,3]{1,0,4,3,2:T(8,128)(2,1)S(1)}, bf16[32,64,3,3,3]{1,0,4,3,2:T(8,128)(2,1)}, u32[]{:S(2)}) copy-start(bf16[32,64,3,3,3]{1,0,4,3,2:T(8,128)(2,1)} %param.5) | copy-start | bytes 331780
  10.6 7.8 %collective-permute-start.5 = (bf16[41,32,128]{2,1,0:T(8,128)(2,1)S(1)}, bf16[41,32,128]{2,1,0:T(8,128)(2,1)S(1)}, u32[]{:S(2)}, u32[]{:S(2)}) collective-permute-start(bf16[41,32,128]{2,1,0:T(8,128)(2,1)S(1)} %get-tuple-element.26), channel_id=1, source_target_pairs={{0,1},{1,0},{2,3},{3,2},{4,5},{5,4},{6,7},{7,6},{8,9},{9,8},{10,11... | collective-permute-start | bytes 1007624 | tf_op jit(solution)/shard_map/ppermute | solution.py:319
  11.2 7.6 %collective-permute-start.2 = (bf16[28,32,128]{2,1,0:T(8,128)(2,1)S(1)}, bf16[28,32,128]{2,1,0:T(8,128)(2,1)S(1)}, u32[]{:S(2)}, u32[]{:S(2)}) collective-permute-start(bf16[28,32,128]{2,1,0:T(8,128)(2,1)S(1)} %get-tuple-element.21.refs_0_), channel_id=1, source_target_pairs={{0,2},{2,0},{4,6},{6,4},{8,10},{10,8},{12,14},{14,12},{16,18},{18,... | collective-permute-start | bytes 688136 | tf_op jit(solution)/shard_map/ppermute | solution.py:323
  13.1 8.1 %collective-permute-start.4 = (bf16[28,32,128]{2,1,0:T(8,128)(2,1)S(1)}, bf16[28,32,128]{2,1,0:T(8,128)(2,1)S(1)}, u32[]{:S(2)}, u32[]{:S(2)}) collective-permute-start(bf16[28,32,128]{2,1,0:T(8,128)(2,1)S(1)} %collective-permute-done.refs_1_), channel_id=1, source_target_pairs={{2,4},{3,5},{6,8},{7,9},{10,12},{11,13},{14,16},{15,17},{18,20},{1... | collective-permute-start | bytes 688136 | tf_op jit(solution)/shard_map/ppermute | solution.py:327
  16.8 4.4 %collective-permute-start.3 = (bf16[28,32,128]{2,1,0:T(8,128)(2,1)S(1)}, bf16[28,32,128]{2,1,0:T(8,128)(2,1)S(1)}, u32[]{:S(2)}, u32[]{:S(2)}) collective-permute-start(bf16[28,32,128]{2,1,0:T(8,128)(2,1)S(1)} %collective-permute-done.refs_1_), channel_id=1, source_target_pairs={{0,2},{2,0},{4,6},{6,4},{8,10},{10,8},{12,14},{14,12},{16,18},{18,... | collective-permute-start | bytes 688136 | tf_op jit(solution)/shard_map/ppermute | solution.py:323
  24.0 1.4 %collective-permute-start.10 = (bf16[2,48,640]{2,1,0:T(8,128)(2,1)S(1)}, bf16[2,48,640]{2,1,0:T(8,128)(2,1)S(1)}, u32[]{:S(2)}, u32[]{:S(2)}) collective-permute-start(bf16[2,48,640]{2,1,0:T(8,128)(2,1)S(1)} %get-tuple-element.35), channel_id=1, source_target_pairs={{0,2},{2,0},{4,6},{6,4},{8,10},{10,8},{12,14},{14,12},{16,18},{18,... | collective-permute-start | bytes 368648 | tf_op jit(solution)/shard_map/ppermute | solution.py:323
  25.5 4.8 %collective-permute-start.12 = (bf16[48,640]{1,0:T(8,128)(2,1)S(1)}, bf16[48,640]{1,0:T(8,128)(2,1)S(1)}, u32[]{:S(2)}, u32[]{:S(2)}) collective-permute-start(bf16[48,640]{1,0:T(8,128)(2,1)S(1)} %get-tuple-element.42), channel_id=1, source_target_pairs={{0,8},{1,9},{2,10},{3,11},{4,12},{5,13},{6,14},{7,15},{8,0},{9,1},... | collective-permute-start | bytes 184328 | tf_op jit(solution)/shard_map/ppermute | solution.py:396
  25.6 5.3 %collective-permute-start.13 = (bf16[48,640]{1,0:T(8,128)(2,1)S(1)}, bf16[48,640]{1,0:T(8,128)(2,1)S(1)}, u32[]{:S(2)}, u32[]{:S(2)}) collective-permute-start(bf16[48,640]{1,0:T(8,128)(2,1)S(1)} %get-tuple-element.43), channel_id=1, source_target_pairs={{0,9},{1,8},{2,11},{3,10},{4,13},{5,12},{6,15},{7,14},{8,1},{9,0},... | collective-permute-start | bytes 184328 | tf_op jit(solution)/shard_map/ppermute | solution.py:396
  27.2 4.8 %collective-permute-start.11 = (bf16[48,640]{1,0:T(8,128)(2,1)S(1)}, bf16[48,640]{1,0:T(8,128)(2,1)S(1)}, u32[]{:S(2)}, u32[]{:S(2)}) collective-permute-start(bf16[48,640]{1,0:T(8,128)(2,1)S(1)} %get-tuple-element.43), channel_id=1, source_target_pairs={{0,1},{1,0},{2,3},{3,2},{4,5},{5,4},{6,7},{7,6},{8,9},{9,8},{10,11... | collective-permute-start | bytes 184328 | tf_op jit(solution)/shard_map/ppermute | solution.py:396
  29.0 10.5 %collective-permute-start.8 = (bf16[26,64,128]{2,1,0:T(8,128)(2,1)S(1)}, bf16[26,64,128]{2,1,0:T(8,128)(2,1)S(1)}, u32[]{:S(2)}, u32[]{:S(2)}) collective-permute-start(bf16[26,64,128]{2,1,0:T(8,128)(2,1)S(1)} %get-tuple-element.30.refs_0_), channel_id=1, source_target_pairs={{2,4},{3,5},{6,8},{7,9},{10,12},{11,13},{14,16},{15,17},{18,20},{1... | collective-permute-start | bytes 1277960 | tf_op jit(solution)/shard_map/ppermute | solution.py:327
  29.2 10.3 %collective-permute-start.7 = (bf16[26,64,128]{2,1,0:T(8,128)(2,1)S(1)}, bf16[26,64,128]{2,1,0:T(8,128)(2,1)S(1)}, u32[]{:S(2)}, u32[]{:S(2)}) collective-permute-start(bf16[26,64,128]{2,1,0:T(8,128)(2,1)S(1)} %get-tuple-element.30.refs_0_), channel_id=1, source_target_pairs={{0,2},{2,0},{4,6},{6,4},{8,10},{10,8},{12,14},{14,12},{16,18},{18,... | collective-permute-start | bytes 1277960 | tf_op jit(solution)/shard_map/ppermute | solution.py:323
  32.0 6.7 %collective-permute-start.14 = (bf16[48,640]{1,0:T(8,128)(2,1)S(1)}, bf16[48,640]{1,0:T(8,128)(2,1)S(1)}, u32[]{:S(2)}, u32[]{:S(2)}) collective-permute-start(bf16[48,640]{1,0:T(8,128)(2,1)S(1)} %add_convert_fusion.2), channel_id=1, source_target_pairs={{0,16},{1,17},{2,18},{3,19},{4,20},{5,21},{6,22},{7,23},{8,24},{9,... | collective-permute-start | bytes 184328 | tf_op jit(solution)/shard_map/ppermute | solution.py:396
  34.4 8.7 %collective-permute-start.6 = (bf16[24,32,128]{2,1,0:T(8,128)(2,1)S(1)}, bf16[24,32,128]{2,1,0:T(8,128)(2,1)S(1)}, u32[]{:S(2)}, u32[]{:S(2)}) collective-permute-start(bf16[24,32,128]{2,1,0:T(8,128)(2,1)S(1)} %get-tuple-element.29), channel_id=1, source_target_pairs={{0,1},{1,0},{2,3},{3,2},{4,5},{5,4},{6,7},{7,6},{8,9},{9,8},{10,11... | collective-permute-start | bytes 589832 | tf_op jit(solution)/shard_map/ppermute | solution.py:319
  38.7 4.3 %collective-permute-start.15 = (bf16[48,640]{1,0:T(8,128)(2,1)S(1)}, bf16[48,640]{1,0:T(8,128)(2,1)S(1)}, u32[]{:S(2)}, u32[]{:S(2)}) collective-permute-start(bf16[48,640]{1,0:T(8,128)(2,1)S(1)} %add_convert_fusion.1), channel_id=1, source_target_pairs={{0,4},{1,5},{2,6},{3,7},{4,0},{5,1},{6,2},{7,3},{8,12},{9,13},{10,... | collective-permute-start | bytes 184328 | tf_op jit(solution)/shard_map/ppermute | solution.py:396
  40.9 6.2 %collective-permute-start.9 = (bf16[24,32,128]{2,1,0:T(8,128)(2,1)S(1)}, bf16[24,32,128]{2,1,0:T(8,128)(2,1)S(1)}, u32[]{:S(2)}, u32[]{:S(2)}) collective-permute-start(bf16[24,32,128]{2,1,0:T(8,128)(2,1)S(1)} %get-tuple-element.33), channel_id=1, source_target_pairs={{0,1},{1,0},{2,3},{3,2},{4,5},{5,4},{6,7},{7,6},{8,9},{9,8},{10,11... | collective-permute-start | bytes 589832 | tf_op jit(solution)/shard_map/ppermute | solution.py:319
  43.0 1.4 %collective-permute-start.16 = (f32[48,640]{1,0:T(8,128)S(1)}, f32[48,640]{1,0:T(8,128)S(1)}, u32[]{:S(2)}, u32[]{:S(2)}) collective-permute-start(f32[48,640]{1,0:T(8,128)S(1)} %convert_add_fusion.mine), channel_id=1, source_target_pairs={{0,2},{2,0},{4,6},{6,4},{8,10},{10,8},{12,14},{14,12},{16,18},{18,... | collective-permute-start | bytes 368648 | tf_op jit(solution)/shard_map/ppermute | solution.py:323

commit v4 on v3

--- a/solution.py
+++ b/solution.py
@@ -93,27 +93,32 @@
         outs[k][0 : rows + 2] = ut[pl.ds(lax.rem(part + k, nchan) * rows, rows + 2)]
 
 
-def filters_body(nchan, rows, *refs):
+def gather_filters(nchan, rows, wall, blocks):
+    part = lax.axis_index("chan")
+    for k in range(nchan):
+        wall[lax.rem(part + nchan - k, nchan)] = blocks[k][rows + 2 :]
+
+
+def backward_filters_body(nchan, rows, *refs):
     blocks = refs[:nchan]
-    forward, backward, wall, turned = refs[nchan:]
-    share = blocks[0].shape[1]
-    part = lax.axis_index("chan")
-    for k in range(nchan):
-        wall[lax.rem(part + nchan - k, nchan)] = blocks[k][rows + 2 :]
-    full = nchan * share
-    for c in range(3):
-        for j in range(5):
-            block = wall[:, c * 5 + j].reshape(full, 128)
-            forward[c * full : (c + 1) * full, j * 128 : (j + 1) * 128] = block
+    backward, wall, turned = refs[nchan:]
+    full = nchan * blocks[0].shape[1]
+    gather_filters(nchan, rows, wall, blocks)
     turned[...] = jnp.zeros_like(turned)
-    for b in range(3):
-        for a in range(3):
-            s = b * 3 + a
+    for a in range(3):
+        plane = 0 if a == 1 else 2 - core() if a == 0 else 1 + core()
+        for b in range(3):
+            at = pl.ds(pl.multiple_of((plane * 3 + b) * 64, 64), 64)
             t = (2 - b) * 3 + (2 - a)
             for c in range(3):
                 block = wall[:, (2 - c) * 5 + t // 2].reshape(full, 128).astype(f32)
                 half = block[:, (t % 2) * 64 : (t % 2) * 64 + 64]
-                turned[s * 64 : (s + 1) * 64, c * 64 : (c + 1) * 64] = half
+                turned[at, c * 64 : (c + 1) * 64] = half
+
+    @pl.when(outermost())
+    def _():
+        turned[6 * 64 : 9 * 64] = jnp.zeros((3 * 64, 256), f32)
+
     backward[...] = turned[...].T[: 3 * 64].astype(bf16)
 
 
@@ -156,15 +161,19 @@
 def forward_body(nchan, rows, step, *refs):
     own, sib, pair = refs[:nchan], refs[nchan : 2 * nchan], refs[2 * nchan : 3 * nchan]
     ups = refs[3 * nchan : 4 * nchan]
-    filters = refs[4 * nchan]
-    outs = refs[4 * nchan + 1 : 5 * nchan + 1]
-    delta, kept, sent, planes, upstream, activated, acc = refs[5 * nchan + 1 :]
+    outs = refs[4 * nchan : 5 * nchan]
+    delta, kept, sent, planes, upstream, activated, acc, wall, filters = refs[5 * nchan :]
     part = lax.axis_index("chan")
     share = own[0].shape[1]
     full = nchan * share
     gather_planes(nchan, planes, own, None, sib, pair)
     for k in range(nchan):
         upstream[:, lax.rem(part + nchan - k, nchan)] = ups[k][0 : rows + 2]
+    gather_filters(nchan, rows, wall, ups)
+    for c in range(3):
+        for j in range(5):
+            block = wall[:, c * 5 + j].reshape(full, 128)
+            filters[c * full : (c + 1) * full, j * 128 : (j + 1) * 128] = block
     extra = ones_rows(128)
     w = filters[...]
     for g in range((rows + 2) // 2):
@@ -217,27 +226,22 @@
 
 
 def backward_body(nchan, rows, *refs):
-    own, sib, pair, filters = refs[:4]
+    sources, filters = refs[:3], refs[3]
     outs = refs[4 : 4 + nchan]
-    planes, result = refs[4 + nchan :]
+    result = refs[4 + nchan]
     part = lax.axis_index("chan")
     share = outs[0].shape[1]
     full = nchan * share
-    even = lax.rem(lax.axis_index("space"), 2) == 0
-    planes[:, 1] = own[...]
-    planes[:, jnp.where(even, 2, 0)] = sib[...]
-    at_pair = jnp.where(even, 0, 2)
-    planes[:, at_pair] = pair[...]
-
-    @pl.when(outermost())
-    def _():
-        planes[:, at_pair] = jnp.zeros(pair.shape, bf16)
-
     extra = jnp.zeros((64, 128), bf16)
+
+    def taps(r):
+        blocks = [source[r : r + 3].reshape(-1, 128) for source in sources]
+        return jnp.concatenate(blocks + [extra], axis=0)
+
     w = filters[...]
     for g in range(rows // 2):
         rhs = jnp.concatenate(
-            [taps_of(planes, 2 * g, extra), taps_of(planes, 2 * g + 1, extra)], axis=1
+            [taps(2 * g), taps(2 * g + 1)], axis=1
         )
         y = jnp.dot(w, rhs, preferred_element_type=f32)
         for n in range(2):
@@ -359,9 +363,9 @@
     sib = [own_sib] + [to_sib(x) for x in v_got]
     pair = [own_pair] + [to_pair(x, True) for x in v_got]
     u_got = over_chan(u_out)
-    w_forward, w_backward = call(
-        functools.partial(filters_body, nchan, rows),
-        [shape(3 * full, 640), shape(3 * full, 640)],
+    w_backward = call(
+        functools.partial(backward_filters_body, nchan, rows),
+        shape(3 * full, 640),
         [pltpu.VMEM((nchan, 15, share, 128), bf16), pltpu.VMEM((640, 256), f32)],
         0,
         1 << 20,
@@ -381,12 +385,14 @@
             pltpu.VMEM((rows + 2, nchan, share, 128), bf16),
             pltpu.VMEM((rows, nchan, share, 128), bf16),
             pltpu.VMEM((3 * full, 640), f32),
+            pltpu.VMEM((nchan, 15, share, 128), bf16),
+            pltpu.VMEM((3 * full, 640), bf16),
         ],
         4 * 27 * full * full * cells,
         8 * block,
         2 * full * cells,
         name="forward",
-    )(*mine, *sib, *pair, u_own, *u_got, w_forward)
+    )(*mine, *sib, *pair, u_own, *u_got)
     d_sib, d_pair = to_sib(delta), to_pair(delta, False)
     kept = kept + to_sib(sent).astype(f32)
     sent = [kept[k].astype(bf16) for k in range(nchan)]
@@ -419,6 +425,7 @@
 
     near = 4 if nspace > 4 else 2
     total = from_hops(sent, (near,))
+
     def unpack(blocks, name):
         out = call(
             functools.partial(unpack_body, nchan, rows, height),
@@ -439,10 +446,7 @@
     ig = call(
         functools.partial(backward_body, nchan, rows),
         [a_shape] * nchan,
-        [
-            pltpu.VMEM((rows + 2, 3, full, 128), bf16),
-            pltpu.VMEM((rows, nchan, share, 128), bf16),
-        ],
+        [pltpu.VMEM((rows, nchan, share, 128), bf16)],
         2 * 27 * full * full * cells,
         6 * block,
         name="backward",

time: 48.5 us -> 48.4 us (level)
  transfers between devices with their start and end apart: 17 -> 17, of which waited for: 11 -> 11; matrix products, arithmetic and copies ran while one was open for 0% -> 0% of each run, Pallas kernels for 9% -> 8%
where the time goes in v4:
time: 48.4 us; the launch traced here: 48.2 us
  starting transfers between devices  20.4 us (42%)
  waiting for transfers between devices  16.1 us (33%)
  Pallas kernels  8.24 us (17%)
  local copies, waits for them, and re-layouts  2.59 us (5%)
  between operations  0.74 us (2%)
    ppermute x3, starting transfers between devices, to_pair(): return lax.ppermute(x, ('space', 'chan'), perm)  7.61 us
    ppermute x5, starting transfers between devices, from_hop(): lax.ppermute(blocks[k], ('space', 'chan'), [(i * nchan + c, (i ^ hop) * n...  6.75 us
    ppermute x5, waiting for transfers between devices, from_hop(): lax.ppermute(blocks[k], ('space', 'chan'), [(i * nchan + c, (i ^ hop) * n...  6.66 us
    ppermute x4, starting transfers between devices, over_chan(): got.append(lax.ppermute(blocks[k - 1], 'chan', perm))  5.81 us
    ppermute x3, waiting for transfers between devices, to_pair(): return lax.ppermute(x, ('space', 'chan'), perm)  4.83 us
    ppermute x4, waiting for transfers between devices, over_chan(): got.append(lax.ppermute(blocks[k - 1], 'chan', perm))  3.2 us
    pallas_call x1, Pallas kernels, shards(): call(functools.partial(forward_body, nchan, rows, step), [a_shape] * ncha...  2.78 us
    unnamed x8, local copies, waits for them, and re-layouts  2.58 us
  transfers between devices with their start and end apart: 17, of which 11 were waited for; matrix products, arithmetic and copies ran while one was open for 0% of the time, Pallas kernels for 8%

profile of v4, /device:TPU:0, one launch (start us, length us, event | category | flops | bytes accessed | tf_op | source)
XLA Modules:
  0.0 48.2 jit_solution(14788652603720787648)
XLA Ops:
  0.6 1.0 %copy-done = bf16[32,1,48,128]{3,2,1,0:T(8,128)(2,1)S(1)} copy-done((bf16[32,1,48,128]{3,2,1,0:T(8,128)(2,1)S(1)}, bf16[32,1,48,128]{3,2,1,0:T(8,128)(2,1)}, u32[]{:S(2)}) %copy-start) | copy-done | bytes 393240
  1.9 3.0 %collective-permute-start = (bf16[28,32,128]{2,1,0:T(8,128)(2,1)S(1)}, bf16[28,32,128]{2,1,0:T(8,128)(2,1)S(1)}, u32[]{:S(2)}, u32[]{:S(2)}) collective-permute-start(bf16[28,32,128]{2,1,0:T(8,128)(2,1)S(1)} %get-tuple-element.20), channel_id=1, source_target_pairs={{0,1},{1,0},{2,3},{3,2},{4,5},{5,4},{6,7},{7,6},{8,9},{9,8},{10,11... | collective-permute-start | bytes 688136 | tf_op jit(solution)/shard_map/ppermute | solution.py:323
  5.0 3.7 %collective-permute-start.1 = (bf16[28,32,128]{2,1,0:T(8,128)(2,1)S(1)}, bf16[28,32,128]{2,1,0:T(8,128)(2,1)S(1)}, u32[]{:S(2)}, u32[]{:S(2)}) collective-permute-start(bf16[28,32,128]{2,1,0:T(8,128)(2,1)S(1)} %get-tuple-element.19.refs_0_), channel_id=1, source_target_pairs={{2,4},{3,5},{6,8},{7,9},{10,12},{11,13},{14,16},{15,17},{18,20},{1... | collective-permute-start | bytes 688136 | tf_op jit(solution)/shard_map/ppermute | solution.py:331
  9.3 0.9 %copy-done.2 = bf16[32,64,3,3,3]{1,0,4,3,2:T(8,128)(2,1)S(1)} copy-done((bf16[32,64,3,3,3]{1,0,4,3,2:T(8,128)(2,1)S(1)}, bf16[32,64,3,3,3]{1,0,4,3,2:T(8,128)(2,1)}, u32[]{:S(2)}) %copy-start.2) | copy-done | bytes 110616
  11.2 1.9 %collective-permute-done.1.refs_4_ = bf16[28,32,128]{2,1,0:T(8,128)(2,1)S(1)} collective-permute-done((bf16[28,32,128]{2,1,0:T(8,128)(2,1)S(1)}, bf16[28,32,128]{2,1,0:T(8,128)(2,1)S(1)}, u32[]{:S(2)}, u32[]{:S(2)}) %collective-permute-start.1) | collective-permute-done | bytes 229408 | tf_op jit(solution)/shard_map/ppermute | solution.py:331
  13.1 3.7 %collective-permute-start.4 = (bf16[28,32,128]{2,1,0:T(8,128)(2,1)S(1)}, bf16[28,32,128]{2,1,0:T(8,128)(2,1)S(1)}, u32[]{:S(2)}, u32[]{:S(2)}) collective-permute-start(bf16[28,32,128]{2,1,0:T(8,128)(2,1)S(1)} %collective-permute-done.refs_1_), channel_id=1, source_target_pairs={{2,4},{3,5},{6,8},{7,9},{10,12},{11,13},{14,16},{15,17},{18,20},{1... | collective-permute-start | bytes 688136 | tf_op jit(solution)/shard_map/ppermute | solution.py:331
  16.8 1.5 %collective-permute-done.5.refs_7_.refs_1_ = bf16[41,32,128]{2,1,0:T(8,128)(2,1)S(1)} collective-permute-done((bf16[41,32,128]{2,1,0:T(8,128)(2,1)S(1)}, bf16[41,32,128]{2,1,0:T(8,128)(2,1)S(1)}, u32[]{:S(2)}, u32[]{:S(2)}) %collective-permute-start.5) | collective-permute-done | bytes 335904 | tf_op jit(solution)/shard_map/ppermute | solution.py:323
  18.4 2.9 %collective-permute-done.4.refs_5_ = bf16[28,32,128]{2,1,0:T(8,128)(2,1)S(1)} collective-permute-done((bf16[28,32,128]{2,1,0:T(8,128)(2,1)S(1)}, bf16[28,32,128]{2,1,0:T(8,128)(2,1)S(1)}, u32[]{:S(2)}, u32[]{:S(2)}) %collective-permute-start.4) | collective-permute-done | bytes 229408 | tf_op jit(solution)/shard_map/ppermute | solution.py:331
  21.3 2.8 %forward.1 = (bf16[24,32,128]{2,1,0:T(8,128)(2,1)S(1)}, bf16[24,32,128]{2,1,0:T(8,128)(2,1)S(1)}, bf16[26,64,128]{2,1,0:T(8,128)(2,1)S(1)}, f32[2,48,640]{2,1,0:T(8,128)S(1)}, bf16[2,48,640]{2,1,0:T(8,128)(2,1)S(1)}) custom-call(bf16[28,32,128]{2,1,0:T(8,128)(2,1)S(1)} %get-tuple-element.19.refs_0_, bf16[28,32,128]{2,1,0:T(8,128)(2,1)S(1)} %collective-permute-done.refs_1_, ...), custom_call_target="tpu_custom_call" | custom-call | flops 1358954496 | bytes 3145728 | tf_op jit(solution)/shard_map/forward/pallas_call | solution.py:379
  24.1 1.3 %collective-permute-done.10 = bf16[2,48,640]{2,1,0:T(8,128)(2,1)S(1)} collective-permute-done((bf16[2,48,640]{2,1,0:T(8,128)(2,1)S(1)}, bf16[2,48,640]{2,1,0:T(8,128)(2,1)S(1)}, u32[]{:S(2)}, u32[]{:S(2)}) %collective-permute-start.10) | collective-permute-done | bytes 122912 | tf_op jit(solution)/shard_map/ppermute | solution.py:327
  25.6 1.7 %collective-permute-start.13 = (bf16[48,640]{1,0:T(8,128)(2,1)S(1)}, bf16[48,640]{1,0:T(8,128)(2,1)S(1)}, u32[]{:S(2)}, u32[]{:S(2)}) collective-permute-start(bf16[48,640]{1,0:T(8,128)(2,1)S(1)} %get-tuple-element.39), channel_id=1, source_target_pairs={{0,9},{1,8},{2,11},{3,10},{4,13},{5,12},{6,15},{7,14},{8,1},{9,0},... | collective-permute-start | bytes 184328 | tf_op jit(solution)/shard_map/ppermute | solution.py:402
  27.2 1.8 %collective-permute-start.11 = (bf16[48,640]{1,0:T(8,128)(2,1)S(1)}, bf16[48,640]{1,0:T(8,128)(2,1)S(1)}, u32[]{:S(2)}, u32[]{:S(2)}) collective-permute-start(bf16[48,640]{1,0:T(8,128)(2,1)S(1)} %get-tuple-element.39), channel_id=1, source_target_pairs={{0,1},{1,0},{2,3},{3,2},{4,5},{5,4},{6,7},{7,6},{8,9},{9,8},{10,11... | collective-permute-start | bytes 184328 | tf_op jit(solution)/shard_map/ppermute | solution.py:402
  29.3 1.0 %collective-permute-done.12 = bf16[48,640]{1,0:T(8,128)(2,1)S(1)} collective-permute-done((bf16[48,640]{1,0:T(8,128)(2,1)S(1)}, bf16[48,640]{1,0:T(8,128)(2,1)S(1)}, u32[]{:S(2)}, u32[]{:S(2)}) %collective-permute-start.12) | collective-permute-done | bytes 61472 | tf_op jit(solution)/shard_map/ppermute | solution.py:402
  30.8 1.1 %collective-permute-done.11 = bf16[48,640]{1,0:T(8,128)(2,1)S(1)} collective-permute-done((bf16[48,640]{1,0:T(8,128)(2,1)S(1)}, bf16[48,640]{1,0:T(8,128)(2,1)S(1)}, u32[]{:S(2)}, u32[]{:S(2)}) %collective-permute-start.11) | collective-permute-done | bytes 61472 | tf_op jit(solution)/shard_map/ppermute | solution.py:402
  32.0 2.4 %collective-permute-start.14 = (bf16[48,640]{1,0:T(8,128)(2,1)S(1)}, bf16[48,640]{1,0:T(8,128)(2,1)S(1)}, u32[]{:S(2)}, u32[]{:S(2)}) collective-permute-start(bf16[48,640]{1,0:T(8,128)(2,1)S(1)} %add_convert_fusion.2), channel_id=1, source_target_pairs={{0,16},{1,17},{2,18},{3,19},{4,20},{5,21},{6,22},{7,23},{8,24},{9,... | collective-permute-start | bytes 184328 | tf_op jit(solution)/shard_map/ppermute | solution.py:402
  35.6 3.1 %collective-permute-done.14 = bf16[48,640]{1,0:T(8,128)(2,1)S(1)} collective-permute-done((bf16[48,640]{1,0:T(8,128)(2,1)S(1)}, bf16[48,640]{1,0:T(8,128)(2,1)S(1)}, u32[]{:S(2)}, u32[]{:S(2)}) %collective-permute-start.14) | collective-permute-done | bytes 61472 | tf_op jit(solution)/shard_map/ppermute | solution.py:402
  38.7 0.8 %collective-permute-start.15 = (bf16[48,640]{1,0:T(8,128)(2,1)S(1)}, bf16[48,640]{1,0:T(8,128)(2,1)S(1)}, u32[]{:S(2)}, u32[]{:S(2)}) collective-permute-start(bf16[48,640]{1,0:T(8,128)(2,1)S(1)} %add_convert_fusion.1), channel_id=1, source_target_pairs={{0,4},{1,5},{2,6},{3,7},{4,0},{5,1},{6,2},{7,3},{8,12},{9,13},{10,... | collective-permute-start | bytes 184328 | tf_op jit(solution)/shard_map/ppermute | solution.py:402
  39.5 1.2 %backward.1 = (bf16[24,32,128]{2,1,0:T(8,128)(2,1)S(1)}, bf16[24,32,128]{2,1,0:T(8,128)(2,1)S(1)}) custom-call(bf16[26,64,128]{2,1,0:T(8,128)(2,1)S(1)} %get-tuple-element.27.refs_0_, bf16[26,64,128]{2,1,0:T(8,128)(2,1)S(1)} %collective-permute-done.7.refs_1_, bf16[26,64,128]{2,1,0:T(8,128)(2,1)S(1)} %collective-permute-done.8.refs_2_, ...), custom_call_target="tpu_custom_call" | custom-call | flops 679477248 | bytes 2359296 | tf_op jit(solution)/shard_map/backward/pallas_call | solution.py:446
  40.7 1.4 %collective-permute-start.9 = (bf16[24,32,128]{2,1,0:T(8,128)(2,1)S(1)}, bf16[24,32,128]{2,1,0:T(8,128)(2,1)S(1)}, u32[]{:S(2)}, u32[]{:S(2)}) collective-permute-start(bf16[24,32,128]{2,1,0:T(8,128)(2,1)S(1)} %get-tuple-element.29), channel_id=1, source_target_pairs={{0,1},{1,0},{2,3},{3,2},{4,5},{5,4},{6,7},{7,6},{8,9},{9,8},{10,11... | collective-permute-start | bytes 589832 | tf_op jit(solution)/shard_map/ppermute | solution.py:323
  42.1 0.9 %collective-permute-done.15 = bf16[48,640]{1,0:T(8,128)(2,1)S(1)} collective-permute-done((bf16[48,640]{1,0:T(8,128)(2,1)S(1)}, bf16[48,640]{1,0:T(8,128)(2,1)S(1)}, u32[]{:S(2)}, u32[]{:S(2)}) %collective-permute-start.15) | collective-permute-done | bytes 61472 | tf_op jit(solution)/shard_map/ppermute | solution.py:402
  43.1 1.2 %unpack_activated.1 = bf16[32,48,128]{2,1,0:T(8,128)(2,1)} custom-call(bf16[24,32,128]{2,1,0:T(8,128)(2,1)S(1)} %get-tuple-element.25.refs_0_, bf16[24,32,128]{2,1,0:T(8,128)(2,1)S(1)} %collective-permute-done.6.refs_1_), custom_call_target="tpu_custom_call" | custom-call | bytes 786432 | tf_op jit(solution)/shard_map/unpack_activated/pallas_call | solution.py:430
  44.4 0.9 %finish.1 = (f32[27,32,64]{2,1,0:T(8,128)}, f32[1,32]{1,0:T(1,128)}) custom-call(f32[48,640]{1,0:T(8,128)S(1)} %convert_add_fusion.mine, f32[48,640]{1,0:T(8,128)S(1)} %collective-permute-done.16.other), custom_call_target="tpu_custom_call" | custom-call | bytes 1048576 | tf_op jit(solution)/shard_map/finish/pallas_call | solution.py:461
  45.3 1.7 %collective-permute-done.9.refs_1_ = bf16[24,32,128]{2,1,0:T(8,128)(2,1)S(1)} collective-permute-done((bf16[24,32,128]{2,1,0:T(8,128)(2,1)S(1)}, bf16[24,32,128]{2,1,0:T(8,128)(2,1)S(1)}, u32[]{:S(2)}, u32[]{:S(2)}) %collective-permute-start.9) | collective-permute-done | bytes 196640 | tf_op jit(solution)/shard_map/ppermute | solution.py:323
  47.0 1.2 %unpack_input_grad.1 = bf16[32,48,128]{2,1,0:T(8,128)(2,1)} custom-call(bf16[24,32,128]{2,1,0:T(8,128)(2,1)S(1)} %get-tuple-element.28.refs_0_, bf16[24,32,128]{2,1,0:T(8,128)(2,1)S(1)} %collective-permute-done.9.refs_1_), custom_call_target="tpu_custom_call" | custom-call | bytes 786432 | tf_op jit(solution)/shard_map/unpack_input_grad/pallas_call | solution.py:430
  (31 shorter events, 4.3 us)
Async XLA Ops:
  0.6 1.0 %copy-start = (bf16[32,1,48,128]{3,2,1,0:T(8,128)(2,1)S(1)}, bf16[32,1,48,128]{3,2,1,0:T(8,128)(2,1)}, u32[]{:S(2)}) copy-start(bf16[32,1,48,128]{3,2,1,0:T(8,128)(2,1)} %param.4) | copy-start | bytes 1179652
  1.6 7.0 %copy-start.1 = (bf16[32,1,48,128]{3,2,1,0:T(8,128)(2,1)S(1)}, bf16[32,1,48,128]{3,2,1,0:T(8,128)(2,1)}, u32[]{:S(2)}) copy-start(bf16[32,1,48,128]{3,2,1,0:T(8,128)(2,1)} %param.7) | copy-start | bytes 1179652
  1.9 9.2 %collective-permute-start = (bf16[28,32,128]{2,1,0:T(8,128)(2,1)S(1)}, bf16[28,32,128]{2,1,0:T(8,128)(2,1)S(1)}, u32[]{:S(2)}, u32[]{:S(2)}) collective-permute-start(bf16[28,32,128]{2,1,0:T(8,128)(2,1)S(1)} %get-tuple-element.20), channel_id=1, source_target_pairs={{0,1},{1,0},{2,3},{3,2},{4,5},{5,4},{6,7},{7,6},{8,9},{9,8},{10,11... | collective-permute-start | bytes 688136 | tf_op jit(solution)/shard_map/ppermute | solution.py:323
  5.0 8.1 %collective-permute-start.1 = (bf16[28,32,128]{2,1,0:T(8,128)(2,1)S(1)}, bf16[28,32,128]{2,1,0:T(8,128)(2,1)S(1)}, u32[]{:S(2)}, u32[]{:S(2)}) collective-permute-start(bf16[28,32,128]{2,1,0:T(8,128)(2,1)S(1)} %get-tuple-element.19.refs_0_), channel_id=1, source_target_pairs={{2,4},{3,5},{6,8},{7,9},{10,12},{11,13},{14,16},{15,17},{18,20},{1... | collective-permute-start | bytes 688136 | tf_op jit(solution)/shard_map/ppermute | solution.py:331
  8.7 0.7 %copy-start.3 = (f32[32]{0:T(128)S(1)}, f32[32]{0:T(128)}, u32[]{:S(2)}) copy-start(f32[32]{0:T(128)} %param.6) | copy-start | bytes 388
  9.3 0.9 %copy-start.2 = (bf16[32,64,3,3,3]{1,0,4,3,2:T(8,128)(2,1)S(1)}, bf16[32,64,3,3,3]{1,0,4,3,2:T(8,128)(2,1)}, u32[]{:S(2)}) copy-start(bf16[32,64,3,3,3]{1,0,4,3,2:T(8,128)(2,1)} %param.5) | copy-start | bytes 331780
  10.6 7.8 %collective-permute-start.5 = (bf16[41,32,128]{2,1,0:T(8,128)(2,1)S(1)}, bf16[41,32,128]{2,1,0:T(8,128)(2,1)S(1)}, u32[]{:S(2)}, u32[]{:S(2)}) collective-permute-start(bf16[41,32,128]{2,1,0:T(8,128)(2,1)S(1)} %get-tuple-element.24), channel_id=1, source_target_pairs={{0,1},{1,0},{2,3},{3,2},{4,5},{5,4},{6,7},{7,6},{8,9},{9,8},{10,11... | collective-permute-start | bytes 1007624 | tf_op jit(solution)/shard_map/ppermute | solution.py:323
  11.2 5.7 %collective-permute-start.2 = (bf16[28,32,128]{2,1,0:T(8,128)(2,1)S(1)}, bf16[28,32,128]{2,1,0:T(8,128)(2,1)S(1)}, u32[]{:S(2)}, u32[]{:S(2)}) collective-permute-start(bf16[28,32,128]{2,1,0:T(8,128)(2,1)S(1)} %get-tuple-element.19.refs_0_), channel_id=1, source_target_pairs={{0,2},{2,0},{4,6},{6,4},{8,10},{10,8},{12,14},{14,12},{16,18},{18,... | collective-permute-start | bytes 688136 | tf_op jit(solution)/shard_map/ppermute | solution.py:327
  13.1 8.1 %collective-permute-start.4 = (bf16[28,32,128]{2,1,0:T(8,128)(2,1)S(1)}, bf16[28,32,128]{2,1,0:T(8,128)(2,1)S(1)}, u32[]{:S(2)}, u32[]{:S(2)}) collective-permute-start(bf16[28,32,128]{2,1,0:T(8,128)(2,1)S(1)} %collective-permute-done.refs_1_), channel_id=1, source_target_pairs={{2,4},{3,5},{6,8},{7,9},{10,12},{11,13},{14,16},{15,17},{18,20},{1... | collective-permute-start | bytes 688136 | tf_op jit(solution)/shard_map/ppermute | solution.py:331
  16.8 4.4 %collective-permute-start.3 = (bf16[28,32,128]{2,1,0:T(8,128)(2,1)S(1)}, bf16[28,32,128]{2,1,0:T(8,128)(2,1)S(1)}, u32[]{:S(2)}, u32[]{:S(2)}) collective-permute-start(bf16[28,32,128]{2,1,0:T(8,128)(2,1)S(1)} %collective-permute-done.refs_1_), channel_id=1, source_target_pairs={{0,2},{2,0},{4,6},{6,4},{8,10},{10,8},{12,14},{14,12},{16,18},{18,... | collective-permute-start | bytes 688136 | tf_op jit(solution)/shard_map/ppermute | solution.py:327
  24.0 1.4 %collective-permute-start.10 = (bf16[2,48,640]{2,1,0:T(8,128)(2,1)S(1)}, bf16[2,48,640]{2,1,0:T(8,128)(2,1)S(1)}, u32[]{:S(2)}, u32[]{:S(2)}) collective-permute-start(bf16[2,48,640]{2,1,0:T(8,128)(2,1)S(1)} %get-tuple-element.31), channel_id=1, source_target_pairs={{0,2},{2,0},{4,6},{6,4},{8,10},{10,8},{12,14},{14,12},{16,18},{18,... | collective-permute-start | bytes 368648 | tf_op jit(solution)/shard_map/ppermute | solution.py:327
  25.5 4.9 %collective-permute-start.12 = (bf16[48,640]{1,0:T(8,128)(2,1)S(1)}, bf16[48,640]{1,0:T(8,128)(2,1)S(1)}, u32[]{:S(2)}, u32[]{:S(2)}) collective-permute-start(bf16[48,640]{1,0:T(8,128)(2,1)S(1)} %get-tuple-element.38), channel_id=1, source_target_pairs={{0,8},{1,9},{2,10},{3,11},{4,12},{5,13},{6,14},{7,15},{8,0},{9,1},... | collective-permute-start | bytes 184328 | tf_op jit(solution)/shard_map/ppermute | solution.py:402
  25.6 5.3 %collective-permute-start.13 = (bf16[48,640]{1,0:T(8,128)(2,1)S(1)}, bf16[48,640]{1,0:T(8,128)(2,1)S(1)}, u32[]{:S(2)}, u32[]{:S(2)}) collective-permute-start(bf16[48,640]{1,0:T(8,128)(2,1)S(1)} %get-tuple-element.39), channel_id=1, source_target_pairs={{0,9},{1,8},{2,11},{3,10},{4,13},{5,12},{6,15},{7,14},{8,1},{9,0},... | collective-permute-start | bytes 184328 | tf_op jit(solution)/shard_map/ppermute | solution.py:402
  27.2 4.8 %collective-permute-start.11 = (bf16[48,640]{1,0:T(8,128)(2,1)S(1)}, bf16[48,640]{1,0:T(8,128)(2,1)S(1)}, u32[]{:S(2)}, u32[]{:S(2)}) collective-permute-start(bf16[48,640]{1,0:T(8,128)(2,1)S(1)} %get-tuple-element.39), channel_id=1, source_target_pairs={{0,1},{1,0},{2,3},{3,2},{4,5},{5,4},{6,7},{7,6},{8,9},{9,8},{10,11... | collective-permute-start | bytes 184328 | tf_op jit(solution)/shard_map/ppermute | solution.py:402
  29.1 10.5 %collective-permute-start.8 = (bf16[26,64,128]{2,1,0:T(8,128)(2,1)S(1)}, bf16[26,64,128]{2,1,0:T(8,128)(2,1)S(1)}, u32[]{:S(2)}, u32[]{:S(2)}) collective-permute-start(bf16[26,64,128]{2,1,0:T(8,128)(2,1)S(1)} %get-tuple-element.27.refs_0_), channel_id=1, source_target_pairs={{2,4},{3,5},{6,8},{7,9},{10,12},{11,13},{14,16},{15,17},{18,20},{1... | collective-permute-start | bytes 1277960 | tf_op jit(solution)/shard_map/ppermute | solution.py:331
  29.3 10.3 %collective-permute-start.7 = (bf16[26,64,128]{2,1,0:T(8,128)(2,1)S(1)}, bf16[26,64,128]{2,1,0:T(8,128)(2,1)S(1)}, u32[]{:S(2)}, u32[]{:S(2)}) collective-permute-start(bf16[26,64,128]{2,1,0:T(8,128)(2,1)S(1)} %get-tuple-element.27.refs_0_), channel_id=1, source_target_pairs={{0,2},{2,0},{4,6},{6,4},{8,10},{10,8},{12,14},{14,12},{16,18},{18,... | collective-permute-start | bytes 1277960 | tf_op jit(solution)/shard_map/ppermute | solution.py:327
  32.0 6.7 %collective-permute-start.14 = (bf16[48,640]{1,0:T(8,128)(2,1)S(1)}, bf16[48,640]{1,0:T(8,128)(2,1)S(1)}, u32[]{:S(2)}, u32[]{:S(2)}) collective-permute-start(bf16[48,640]{1,0:T(8,128)(2,1)S(1)} %add_convert_fusion.2), channel_id=1, source_target_pairs={{0,16},{1,17},{2,18},{3,19},{4,20},{5,21},{6,22},{7,23},{8,24},{9,... | collective-permute-start | bytes 184328 | tf_op jit(solution)/shard_map/ppermute | solution.py:402
  34.8 8.3 %collective-permute-start.6 = (bf16[24,32,128]{2,1,0:T(8,128)(2,1)S(1)}, bf16[24,32,128]{2,1,0:T(8,128)(2,1)S(1)}, u32[]{:S(2)}, u32[]{:S(2)}) collective-permute-start(bf16[24,32,128]{2,1,0:T(8,128)(2,1)S(1)} %get-tuple-element.26), channel_id=1, source_target_pairs={{0,1},{1,0},{2,3},{3,2},{4,5},{5,4},{6,7},{7,6},{8,9},{9,8},{10,11... | collective-permute-start | bytes 589832 | tf_op jit(solution)/shard_map/ppermute | solution.py:323
  38.7 4.3 %collective-permute-start.15 = (bf16[48,640]{1,0:T(8,128)(2,1)S(1)}, bf16[48,640]{1,0:T(8,128)(2,1)S(1)}, u32[]{:S(2)}, u32[]{:S(2)}) collective-permute-start(bf16[48,640]{1,0:T(8,128)(2,1)S(1)} %add_convert_fusion.1), channel_id=1, source_target_pairs={{0,4},{1,5},{2,6},{3,7},{4,0},{5,1},{6,2},{7,3},{8,12},{9,13},{10,... | collective-permute-start | bytes 184328 | tf_op jit(solution)/shard_map/ppermute | solution.py:402
  40.7 6.3 %collective-permute-start.9 = (bf16[24,32,128]{2,1,0:T(8,128)(2,1)S(1)}, bf16[24,32,128]{2,1,0:T(8,128)(2,1)S(1)}, u32[]{:S(2)}, u32[]{:S(2)}) collective-permute-start(bf16[24,32,128]{2,1,0:T(8,128)(2,1)S(1)} %get-tuple-element.29), channel_id=1, source_target_pairs={{0,1},{1,0},{2,3},{3,2},{4,5},{5,4},{6,7},{7,6},{8,9},{9,8},{10,11... | collective-permute-start | bytes 589832 | tf_op jit(solution)/shard_map/ppermute | solution.py:323
  43.0 1.4 %collective-permute-start.16 = (f32[48,640]{1,0:T(8,128)S(1)}, f32[48,640]{1,0:T(8,128)S(1)}, u32[]{:S(2)}, u32[]{:S(2)}) collective-permute-start(f32[48,640]{1,0:T(8,128)S(1)} %convert_add_fusion.mine), channel_id=1, source_target_pairs={{0,2},{2,0},{4,6},{6,4},{8,10},{10,8},{12,14},{14,12},{16,18},{18,... | collective-permute-start | bytes 368648 | tf_op jit(solution)/shard_map/ppermute | solution.py:327

commit v5 on v4

--- a/solution.py
+++ b/solution.py
@@ -256,17 +256,17 @@
     out, staged, flat, sems = refs[nchan:]
     share = out.shape[0]
     part = lax.axis_index("chan")
-    size = rows * share
+    pitch = share + 8
     for k in range(nchan):
         q = lax.rem(part + nchan - k, nchan)
-        flat[pl.ds(pl.multiple_of(q * size, 8), size)] = (
-            blocks[k][...].astype(f32).reshape(size, 128)
-        )
+        for row in range(rows):
+            at = pl.multiple_of(q * (rows * pitch) + row * pitch, 8)
+            flat[pl.ds(at, share)] = blocks[k][row].astype(f32)
     copies = []
     for n in range(4):
         group = pl.ds(n * (share // 4), share // 4)
         for ch in range(n * (share // 4), (n + 1) * (share // 4)):
-            staged[ch] = flat[pl.ds(ch, height, stride=share)].astype(bf16)
+            staged[ch] = flat[pl.ds(ch, height, stride=pitch)].astype(bf16)
         copies.append(pltpu.make_async_copy(staged.at[group], out.at[group], sems.at[n]))
         copies[-1].start()
     for copy in copies:
@@ -432,7 +432,7 @@
             shape(share, height, width),
             [
                 pltpu.VMEM((share, height, width), bf16),
-                pltpu.VMEM((height * share, 128), f32),
+                pltpu.VMEM((height * (share + 8), 128), f32),
                 pltpu.SemaphoreType.DMA((4,)),
             ],
             0,

time: 48.4 us -> 48.1 us (level)
  Pallas kernels: 8.24 us -> 7.62 us
    pallas_call x2, Pallas kernels: 2.36 us -> 1.74 us  [unpack(): call(functools.partial(unpack_body, nchan, rows, height), shape(share, he...]
where the time goes in v5:
time: 48.1 us; the launch traced here: 47.9 us
  starting transfers between devices  20.4 us (42%)
  waiting for transfers between devices  16.5 us (34%)
  Pallas kernels  7.62 us (16%)
  local copies, waits for them, and re-layouts  2.59 us (5%)
  between operations  0.74 us (2%)
    ppermute x3, starting transfers between devices, to_pair(): return lax.ppermute(x, ('space', 'chan'), perm)  7.61 us
    ppermute x5, starting transfers between devices, from_hop(): lax.ppermute(blocks[k], ('space', 'chan'), [(i * nchan + c, (i ^ hop) * n...  6.75 us
    ppermute x5, waiting for transfers between devices, from_hop(): lax.ppermute(blocks[k], ('space', 'chan'), [(i * nchan + c, (i ^ hop) * n...  6.66 us
    ppermute x4, starting transfers between devices, over_chan(): got.append(lax.ppermute(blocks[k - 1], 'chan', perm))  5.81 us
    ppermute x3, waiting for transfers between devices, to_pair(): return lax.ppermute(x, ('space', 'chan'), perm)  4.83 us
    ppermute x4, waiting for transfers between devices, over_chan(): got.append(lax.ppermute(blocks[k - 1], 'chan', perm))  3.2 us
    pallas_call x1, Pallas kernels, shards(): call(functools.partial(forward_body, nchan, rows, step), [a_shape] * ncha...  2.78 us
    unnamed x8, local copies, waits for them, and re-layouts  2.58 us
  transfers between devices with their start and end apart: 17, of which 11 were waited for; matrix products, arithmetic and copies ran while one was open for 0% of the time, Pallas kernels for 8%

profile of v5, /device:TPU:0, one launch (start us, length us, event | category | flops | bytes accessed | tf_op | source)
XLA Modules:
  0.0 47.9 jit_solution(5847566661494978396)
XLA Ops:
  0.6 1.0 %copy-done = bf16[32,1,48,128]{3,2,1,0:T(8,128)(2,1)S(1)} copy-done((bf16[32,1,48,128]{3,2,1,0:T(8,128)(2,1)S(1)}, bf16[32,1,48,128]{3,2,1,0:T(8,128)(2,1)}, u32[]{:S(2)}) %copy-start) | copy-done | bytes 393240
  1.9 3.0 %collective-permute-start = (bf16[28,32,128]{2,1,0:T(8,128)(2,1)S(1)}, bf16[28,32,128]{2,1,0:T(8,128)(2,1)S(1)}, u32[]{:S(2)}, u32[]{:S(2)}) collective-permute-start(bf16[28,32,128]{2,1,0:T(8,128)(2,1)S(1)} %get-tuple-element.20), channel_id=1, source_target_pairs={{0,1},{1,0},{2,3},{3,2},{4,5},{5,4},{6,7},{7,6},{8,9},{9,8},{10,11... | collective-permute-start | bytes 688136 | tf_op jit(solution)/shard_map/ppermute | solution.py:323
  5.0 3.7 %collective-permute-start.1 = (bf16[28,32,128]{2,1,0:T(8,128)(2,1)S(1)}, bf16[28,32,128]{2,1,0:T(8,128)(2,1)S(1)}, u32[]{:S(2)}, u32[]{:S(2)}) collective-permute-start(bf16[28,32,128]{2,1,0:T(8,128)(2,1)S(1)} %get-tuple-element.19.refs_0_), channel_id=1, source_target_pairs={{2,4},{3,5},{6,8},{7,9},{10,12},{11,13},{14,16},{15,17},{18,20},{1... | collective-permute-start | bytes 688136 | tf_op jit(solution)/shard_map/ppermute | solution.py:331
  9.3 0.9 %copy-done.2 = bf16[32,64,3,3,3]{1,0,4,3,2:T(8,128)(2,1)S(1)} copy-done((bf16[32,64,3,3,3]{1,0,4,3,2:T(8,128)(2,1)S(1)}, bf16[32,64,3,3,3]{1,0,4,3,2:T(8,128)(2,1)}, u32[]{:S(2)}) %copy-start.2) | copy-done | bytes 110616
  11.2 1.9 %collective-permute-done.1.refs_4_ = bf16[28,32,128]{2,1,0:T(8,128)(2,1)S(1)} collective-permute-done((bf16[28,32,128]{2,1,0:T(8,128)(2,1)S(1)}, bf16[28,32,128]{2,1,0:T(8,128)(2,1)S(1)}, u32[]{:S(2)}, u32[]{:S(2)}) %collective-permute-start.1) | collective-permute-done | bytes 229408 | tf_op jit(solution)/shard_map/ppermute | solution.py:331
  13.1 3.7 %collective-permute-start.4 = (bf16[28,32,128]{2,1,0:T(8,128)(2,1)S(1)}, bf16[28,32,128]{2,1,0:T(8,128)(2,1)S(1)}, u32[]{:S(2)}, u32[]{:S(2)}) collective-permute-start(bf16[28,32,128]{2,1,0:T(8,128)(2,1)S(1)} %collective-permute-done.refs_1_), channel_id=1, source_target_pairs={{2,4},{3,5},{6,8},{7,9},{10,12},{11,13},{14,16},{15,17},{18,20},{1... | collective-permute-start | bytes 688136 | tf_op jit(solution)/shard_map/ppermute | solution.py:331
  16.8 1.5 %collective-permute-done.5.refs_7_.refs_1_ = bf16[41,32,128]{2,1,0:T(8,128)(2,1)S(1)} collective-permute-done((bf16[41,32,128]{2,1,0:T(8,128)(2,1)S(1)}, bf16[41,32,128]{2,1,0:T(8,128)(2,1)S(1)}, u32[]{:S(2)}, u32[]{:S(2)}) %collective-permute-start.5) | collective-permute-done | bytes 335904 | tf_op jit(solution)/shard_map/ppermute | solution.py:323
  18.4 2.9 %collective-permute-done.4.refs_5_ = bf16[28,32,128]{2,1,0:T(8,128)(2,1)S(1)} collective-permute-done((bf16[28,32,128]{2,1,0:T(8,128)(2,1)S(1)}, bf16[28,32,128]{2,1,0:T(8,128)(2,1)S(1)}, u32[]{:S(2)}, u32[]{:S(2)}) %collective-permute-start.4) | collective-permute-done | bytes 229408 | tf_op jit(solution)/shard_map/ppermute | solution.py:331
  21.3 2.8 %forward.1 = (bf16[24,32,128]{2,1,0:T(8,128)(2,1)S(1)}, bf16[24,32,128]{2,1,0:T(8,128)(2,1)S(1)}, bf16[26,64,128]{2,1,0:T(8,128)(2,1)S(1)}, f32[2,48,640]{2,1,0:T(8,128)S(1)}, bf16[2,48,640]{2,1,0:T(8,128)(2,1)S(1)}) custom-call(bf16[28,32,128]{2,1,0:T(8,128)(2,1)S(1)} %get-tuple-element.19.refs_0_, bf16[28,32,128]{2,1,0:T(8,128)(2,1)S(1)} %collective-permute-done.refs_1_, ...), custom_call_target="tpu_custom_call" | custom-call | flops 1358954496 | bytes 3145728 | tf_op jit(solution)/shard_map/forward/pallas_call | solution.py:379
  24.1 1.3 %collective-permute-done.10 = bf16[2,48,640]{2,1,0:T(8,128)(2,1)S(1)} collective-permute-done((bf16[2,48,640]{2,1,0:T(8,128)(2,1)S(1)}, bf16[2,48,640]{2,1,0:T(8,128)(2,1)S(1)}, u32[]{:S(2)}, u32[]{:S(2)}) %collective-permute-start.10) | collective-permute-done | bytes 122912 | tf_op jit(solution)/shard_map/ppermute | solution.py:327
  25.6 1.7 %collective-permute-start.13 = (bf16[48,640]{1,0:T(8,128)(2,1)S(1)}, bf16[48,640]{1,0:T(8,128)(2,1)S(1)}, u32[]{:S(2)}, u32[]{:S(2)}) collective-permute-start(bf16[48,640]{1,0:T(8,128)(2,1)S(1)} %get-tuple-element.39), channel_id=1, source_target_pairs={{0,9},{1,8},{2,11},{3,10},{4,13},{5,12},{6,15},{7,14},{8,1},{9,0},... | collective-permute-start | bytes 184328 | tf_op jit(solution)/shard_map/ppermute | solution.py:402
  27.2 1.8 %collective-permute-start.11 = (bf16[48,640]{1,0:T(8,128)(2,1)S(1)}, bf16[48,640]{1,0:T(8,128)(2,1)S(1)}, u32[]{:S(2)}, u32[]{:S(2)}) collective-permute-start(bf16[48,640]{1,0:T(8,128)(2,1)S(1)} %get-tuple-element.39), channel_id=1, source_target_pairs={{0,1},{1,0},{2,3},{3,2},{4,5},{5,4},{6,7},{7,6},{8,9},{9,8},{10,11... | collective-permute-start | bytes 184328 | tf_op jit(solution)/shard_map/ppermute | solution.py:402
  29.3 1.0 %collective-permute-done.12 = bf16[48,640]{1,0:T(8,128)(2,1)S(1)} collective-permute-done((bf16[48,640]{1,0:T(8,128)(2,1)S(1)}, bf16[48,640]{1,0:T(8,128)(2,1)S(1)}, u32[]{:S(2)}, u32[]{:S(2)}) %collective-permute-start.12) | collective-permute-done | bytes 61472 | tf_op jit(solution)/shard_map/ppermute | solution.py:402
  30.8 1.1 %collective-permute-done.11 = bf16[48,640]{1,0:T(8,128)(2,1)S(1)} collective-permute-done((bf16[48,640]{1,0:T(8,128)(2,1)S(1)}, bf16[48,640]{1,0:T(8,128)(2,1)S(1)}, u32[]{:S(2)}, u32[]{:S(2)}) %collective-permute-start.11) | collective-permute-done | bytes 61472 | tf_op jit(solution)/shard_map/ppermute | solution.py:402
  32.0 2.4 %collective-permute-start.14 = (bf16[48,640]{1,0:T(8,128)(2,1)S(1)}, bf16[48,640]{1,0:T(8,128)(2,1)S(1)}, u32[]{:S(2)}, u32[]{:S(2)}) collective-permute-start(bf16[48,640]{1,0:T(8,128)(2,1)S(1)} %add_convert_fusion.2), channel_id=1, source_target_pairs={{0,16},{1,17},{2,18},{3,19},{4,20},{5,21},{6,22},{7,23},{8,24},{9,... | collective-permute-start | bytes 184328 | tf_op jit(solution)/shard_map/ppermute | solution.py:402
  35.6 3.1 %collective-permute-done.14 = bf16[48,640]{1,0:T(8,128)(2,1)S(1)} collective-permute-done((bf16[48,640]{1,0:T(8,128)(2,1)S(1)}, bf16[48,640]{1,0:T(8,128)(2,1)S(1)}, u32[]{:S(2)}, u32[]{:S(2)}) %collective-permute-start.14) | collective-permute-done | bytes 61472 | tf_op jit(solution)/shard_map/ppermute | solution.py:402
  38.7 0.8 %collective-permute-start.15 = (bf16[48,640]{1,0:T(8,128)(2,1)S(1)}, bf16[48,640]{1,0:T(8,128)(2,1)S(1)}, u32[]{:S(2)}, u32[]{:S(2)}) collective-permute-start(bf16[48,640]{1,0:T(8,128)(2,1)S(1)} %add_convert_fusion.1), channel_id=1, source_target_pairs={{0,4},{1,5},{2,6},{3,7},{4,0},{5,1},{6,2},{7,3},{8,12},{9,13},{10,... | collective-permute-start | bytes 184328 | tf_op jit(solution)/shard_map/ppermute | solution.py:402
  39.5 1.2 %backward.1 = (bf16[24,32,128]{2,1,0:T(8,128)(2,1)S(1)}, bf16[24,32,128]{2,1,0:T(8,128)(2,1)S(1)}) custom-call(bf16[26,64,128]{2,1,0:T(8,128)(2,1)S(1)} %get-tuple-element.27.refs_0_, bf16[26,64,128]{2,1,0:T(8,128)(2,1)S(1)} %collective-permute-done.7.refs_1_, bf16[26,64,128]{2,1,0:T(8,128)(2,1)S(1)} %collective-permute-done.8.refs_2_, ...), custom_call_target="tpu_custom_call" | custom-call | flops 679477248 | bytes 2359296 | tf_op jit(solution)/shard_map/backward/pallas_call | solution.py:446
  40.7 1.4 %collective-permute-start.9 = (bf16[24,32,128]{2,1,0:T(8,128)(2,1)S(1)}, bf16[24,32,128]{2,1,0:T(8,128)(2,1)S(1)}, u32[]{:S(2)}, u32[]{:S(2)}) collective-permute-start(bf16[24,32,128]{2,1,0:T(8,128)(2,1)S(1)} %get-tuple-element.29), channel_id=1, source_target_pairs={{0,1},{1,0},{2,3},{3,2},{4,5},{5,4},{6,7},{7,6},{8,9},{9,8},{10,11... | collective-permute-start | bytes 589832 | tf_op jit(solution)/shard_map/ppermute | solution.py:323
  42.1 0.9 %collective-permute-done.15 = bf16[48,640]{1,0:T(8,128)(2,1)S(1)} collective-permute-done((bf16[48,640]{1,0:T(8,128)(2,1)S(1)}, bf16[48,640]{1,0:T(8,128)(2,1)S(1)}, u32[]{:S(2)}, u32[]{:S(2)}) %collective-permute-start.15) | collective-permute-done | bytes 61472 | tf_op jit(solution)/shard_map/ppermute | solution.py:402
  43.1 0.9 %unpack_activated.1 = bf16[32,48,128]{2,1,0:T(8,128)(2,1)} custom-call(bf16[24,32,128]{2,1,0:T(8,128)(2,1)S(1)} %get-tuple-element.25.refs_0_, bf16[24,32,128]{2,1,0:T(8,128)(2,1)S(1)} %collective-permute-done.6.refs_1_), custom_call_target="tpu_custom_call" | custom-call | bytes 786432 | tf_op jit(solution)/shard_map/unpack_activated/pallas_call | solution.py:430
  44.4 0.9 %finish.1 = (f32[27,32,64]{2,1,0:T(8,128)}, f32[1,32]{1,0:T(1,128)}) custom-call(f32[48,640]{1,0:T(8,128)S(1)} %convert_add_fusion.mine, f32[48,640]{1,0:T(8,128)S(1)} %collective-permute-done.16.other), custom_call_target="tpu_custom_call" | custom-call | bytes 1048576 | tf_op jit(solution)/shard_map/finish/pallas_call | solution.py:461
  45.3 1.7 %collective-permute-done.9.refs_1_ = bf16[24,32,128]{2,1,0:T(8,128)(2,1)S(1)} collective-permute-done((bf16[24,32,128]{2,1,0:T(8,128)(2,1)S(1)}, bf16[24,32,128]{2,1,0:T(8,128)(2,1)S(1)}, u32[]{:S(2)}, u32[]{:S(2)}) %collective-permute-start.9) | collective-permute-done | bytes 196640 | tf_op jit(solution)/shard_map/ppermute | solution.py:323
  47.0 0.9 %unpack_input_grad.1 = bf16[32,48,128]{2,1,0:T(8,128)(2,1)} custom-call(bf16[24,32,128]{2,1,0:T(8,128)(2,1)S(1)} %get-tuple-element.28.refs_0_, bf16[24,32,128]{2,1,0:T(8,128)(2,1)S(1)} %collective-permute-done.9.refs_1_), custom_call_target="tpu_custom_call" | custom-call | bytes 786432 | tf_op jit(solution)/shard_map/unpack_input_grad/pallas_call | solution.py:430
  (31 shorter events, 4.6 us)
Async XLA Ops:
  0.6 1.0 %copy-start = (bf16[32,1,48,128]{3,2,1,0:T(8,128)(2,1)S(1)}, bf16[32,1,48,128]{3,2,1,0:T(8,128)(2,1)}, u32[]{:S(2)}) copy-start(bf16[32,1,48,128]{3,2,1,0:T(8,128)(2,1)} %param.4) | copy-start | bytes 1179652
  1.6 7.0 %copy-start.1 = (bf16[32,1,48,128]{3,2,1,0:T(8,128)(2,1)S(1)}, bf16[32,1,48,128]{3,2,1,0:T(8,128)(2,1)}, u32[]{:S(2)}) copy-start(bf16[32,1,48,128]{3,2,1,0:T(8,128)(2,1)} %param.7) | copy-start | bytes 1179652
  1.9 9.2 %collective-permute-start = (bf16[28,32,128]{2,1,0:T(8,128)(2,1)S(1)}, bf16[28,32,128]{2,1,0:T(8,128)(2,1)S(1)}, u32[]{:S(2)}, u32[]{:S(2)}) collective-permute-start(bf16[28,32,128]{2,1,0:T(8,128)(2,1)S(1)} %get-tuple-element.20), channel_id=1, source_target_pairs={{0,1},{1,0},{2,3},{3,2},{4,5},{5,4},{6,7},{7,6},{8,9},{9,8},{10,11... | collective-permute-start | bytes 688136 | tf_op jit(solution)/shard_map/ppermute | solution.py:323
  5.0 8.1 %collective-permute-start.1 = (bf16[28,32,128]{2,1,0:T(8,128)(2,1)S(1)}, bf16[28,32,128]{2,1,0:T(8,128)(2,1)S(1)}, u32[]{:S(2)}, u32[]{:S(2)}) collective-permute-start(bf16[28,32,128]{2,1,0:T(8,128)(2,1)S(1)} %get-tuple-element.19.refs_0_), channel_id=1, source_target_pairs={{2,4},{3,5},{6,8},{7,9},{10,12},{11,13},{14,16},{15,17},{18,20},{1... | collective-permute-start | bytes 688136 | tf_op jit(solution)/shard_map/ppermute | solution.py:331
  8.7 0.7 %copy-start.3 = (f32[32]{0:T(128)S(1)}, f32[32]{0:T(128)}, u32[]{:S(2)}) copy-start(f32[32]{0:T(128)} %param.6) | copy-start | bytes 388
  9.3 0.9 %copy-start.2 = (bf16[32,64,3,3,3]{1,0,4,3,2:T(8,128)(2,1)S(1)}, bf16[32,64,3,3,3]{1,0,4,3,2:T(8,128)(2,1)}, u32[]{:S(2)}) copy-start(bf16[32,64,3,3,3]{1,0,4,3,2:T(8,128)(2,1)} %param.5) | copy-start | bytes 331780
  10.6 7.8 %collective-permute-start.5 = (bf16[41,32,128]{2,1,0:T(8,128)(2,1)S(1)}, bf16[41,32,128]{2,1,0:T(8,128)(2,1)S(1)}, u32[]{:S(2)}, u32[]{:S(2)}) collective-permute-start(bf16[41,32,128]{2,1,0:T(8,128)(2,1)S(1)} %get-tuple-element.24), channel_id=1, source_target_pairs={{0,1},{1,0},{2,3},{3,2},{4,5},{5,4},{6,7},{7,6},{8,9},{9,8},{10,11... | collective-permute-start | bytes 1007624 | tf_op jit(solution)/shard_map/ppermute | solution.py:323
  11.2 5.7 %collective-permute-start.2 = (bf16[28,32,128]{2,1,0:T(8,128)(2,1)S(1)}, bf16[28,32,128]{2,1,0:T(8,128)(2,1)S(1)}, u32[]{:S(2)}, u32[]{:S(2)}) collective-permute-start(bf16[28,32,128]{2,1,0:T(8,128)(2,1)S(1)} %get-tuple-element.19.refs_0_), channel_id=1, source_target_pairs={{0,2},{2,0},{4,6},{6,4},{8,10},{10,8},{12,14},{14,12},{16,18},{18,... | collective-permute-start | bytes 688136 | tf_op jit(solution)/shard_map/ppermute | solution.py:327
  13.1 8.1 %collective-permute-start.4 = (bf16[28,32,128]{2,1,0:T(8,128)(2,1)S(1)}, bf16[28,32,128]{2,1,0:T(8,128)(2,1)S(1)}, u32[]{:S(2)}, u32[]{:S(2)}) collective-permute-start(bf16[28,32,128]{2,1,0:T(8,128)(2,1)S(1)} %collective-permute-done.refs_1_), channel_id=1, source_target_pairs={{2,4},{3,5},{6,8},{7,9},{10,12},{11,13},{14,16},{15,17},{18,20},{1... | collective-permute-start | bytes 688136 | tf_op jit(solution)/shard_map/ppermute | solution.py:331
  16.8 4.4 %collective-permute-start.3 = (bf16[28,32,128]{2,1,0:T(8,128)(2,1)S(1)}, bf16[28,32,128]{2,1,0:T(8,128)(2,1)S(1)}, u32[]{:S(2)}, u32[]{:S(2)}) collective-permute-start(bf16[28,32,128]{2,1,0:T(8,128)(2,1)S(1)} %collective-permute-done.refs_1_), channel_id=1, source_target_pairs={{0,2},{2,0},{4,6},{6,4},{8,10},{10,8},{12,14},{14,12},{16,18},{18,... | collective-permute-start | bytes 688136 | tf_op jit(solution)/shard_map/ppermute | solution.py:327
  24.0 1.4 %collective-permute-start.10 = (bf16[2,48,640]{2,1,0:T(8,128)(2,1)S(1)}, bf16[2,48,640]{2,1,0:T(8,128)(2,1)S(1)}, u32[]{:S(2)}, u32[]{:S(2)}) collective-permute-start(bf16[2,48,640]{2,1,0:T(8,128)(2,1)S(1)} %get-tuple-element.31), channel_id=1, source_target_pairs={{0,2},{2,0},{4,6},{6,4},{8,10},{10,8},{12,14},{14,12},{16,18},{18,... | collective-permute-start | bytes 368648 | tf_op jit(solution)/shard_map/ppermute | solution.py:327
  25.5 4.9 %collective-permute-start.12 = (bf16[48,640]{1,0:T(8,128)(2,1)S(1)}, bf16[48,640]{1,0:T(8,128)(2,1)S(1)}, u32[]{:S(2)}, u32[]{:S(2)}) collective-permute-start(bf16[48,640]{1,0:T(8,128)(2,1)S(1)} %get-tuple-element.38), channel_id=1, source_target_pairs={{0,8},{1,9},{2,10},{3,11},{4,12},{5,13},{6,14},{7,15},{8,0},{9,1},... | collective-permute-start | bytes 184328 | tf_op jit(solution)/shard_map/ppermute | solution.py:402
  25.6 5.3 %collective-permute-start.13 = (bf16[48,640]{1,0:T(8,128)(2,1)S(1)}, bf16[48,640]{1,0:T(8,128)(2,1)S(1)}, u32[]{:S(2)}, u32[]{:S(2)}) collective-permute-start(bf16[48,640]{1,0:T(8,128)(2,1)S(1)} %get-tuple-element.39), channel_id=1, source_target_pairs={{0,9},{1,8},{2,11},{3,10},{4,13},{5,12},{6,15},{7,14},{8,1},{9,0},... | collective-permute-start | bytes 184328 | tf_op jit(solution)/shard_map/ppermute | solution.py:402
  27.2 4.8 %collective-permute-start.11 = (bf16[48,640]{1,0:T(8,128)(2,1)S(1)}, bf16[48,640]{1,0:T(8,128)(2,1)S(1)}, u32[]{:S(2)}, u32[]{:S(2)}) collective-permute-start(bf16[48,640]{1,0:T(8,128)(2,1)S(1)} %get-tuple-element.39), channel_id=1, source_target_pairs={{0,1},{1,0},{2,3},{3,2},{4,5},{5,4},{6,7},{7,6},{8,9},{9,8},{10,11... | collective-permute-start | bytes 184328 | tf_op jit(solution)/shard_map/ppermute | solution.py:402
  29.1 10.5 %collective-permute-start.8 = (bf16[26,64,128]{2,1,0:T(8,128)(2,1)S(1)}, bf16[26,64,128]{2,1,0:T(8,128)(2,1)S(1)}, u32[]{:S(2)}, u32[]{:S(2)}) collective-permute-start(bf16[26,64,128]{2,1,0:T(8,128)(2,1)S(1)} %get-tuple-element.27.refs_0_), channel_id=1, source_target_pairs={{2,4},{3,5},{6,8},{7,9},{10,12},{11,13},{14,16},{15,17},{18,20},{1... | collective-permute-start | bytes 1277960 | tf_op jit(solution)/shard_map/ppermute | solution.py:331
  29.3 10.3 %collective-permute-start.7 = (bf16[26,64,128]{2,1,0:T(8,128)(2,1)S(1)}, bf16[26,64,128]{2,1,0:T(8,128)(2,1)S(1)}, u32[]{:S(2)}, u32[]{:S(2)}) collective-permute-start(bf16[26,64,128]{2,1,0:T(8,128)(2,1)S(1)} %get-tuple-element.27.refs_0_), channel_id=1, source_target_pairs={{0,2},{2,0},{4,6},{6,4},{8,10},{10,8},{12,14},{14,12},{16,18},{18,... | collective-permute-start | bytes 1277960 | tf_op jit(solution)/shard_map/ppermute | solution.py:327
  32.0 6.7 %collective-permute-start.14 = (bf16[48,640]{1,0:T(8,128)(2,1)S(1)}, bf16[48,640]{1,0:T(8,128)(2,1)S(1)}, u32[]{:S(2)}, u32[]{:S(2)}) collective-permute-start(bf16[48,640]{1,0:T(8,128)(2,1)S(1)} %add_convert_fusion.2), channel_id=1, source_target_pairs={{0,16},{1,17},{2,18},{3,19},{4,20},{5,21},{6,22},{7,23},{8,24},{9,... | collective-permute-start | bytes 184328 | tf_op jit(solution)/shard_map/ppermute | solution.py:402
  34.8 8.3 %collective-permute-start.6 = (bf16[24,32,128]{2,1,0:T(8,128)(2,1)S(1)}, bf16[24,32,128]{2,1,0:T(8,128)(2,1)S(1)}, u32[]{:S(2)}, u32[]{:S(2)}) collective-permute-start(bf16[24,32,128]{2,1,0:T(8,128)(2,1)S(1)} %get-tuple-element.26), channel_id=1, source_target_pairs={{0,1},{1,0},{2,3},{3,2},{4,5},{5,4},{6,7},{7,6},{8,9},{9,8},{10,11... | collective-permute-start | bytes 589832 | tf_op jit(solution)/shard_map/ppermute | solution.py:323
  38.7 4.3 %collective-permute-start.15 = (bf16[48,640]{1,0:T(8,128)(2,1)S(1)}, bf16[48,640]{1,0:T(8,128)(2,1)S(1)}, u32[]{:S(2)}, u32[]{:S(2)}) collective-permute-start(bf16[48,640]{1,0:T(8,128)(2,1)S(1)} %add_convert_fusion.1), channel_id=1, source_target_pairs={{0,4},{1,5},{2,6},{3,7},{4,0},{5,1},{6,2},{7,3},{8,12},{9,13},{10,... | collective-permute-start | bytes 184328 | tf_op jit(solution)/shard_map/ppermute | solution.py:402
  40.7 6.3 %collective-permute-start.9 = (bf16[24,32,128]{2,1,0:T(8,128)(2,1)S(1)}, bf16[24,32,128]{2,1,0:T(8,128)(2,1)S(1)}, u32[]{:S(2)}, u32[]{:S(2)}) collective-permute-start(bf16[24,32,128]{2,1,0:T(8,128)(2,1)S(1)} %get-tuple-element.29), channel_id=1, source_target_pairs={{0,1},{1,0},{2,3},{3,2},{4,5},{5,4},{6,7},{7,6},{8,9},{9,8},{10,11... | collective-permute-start | bytes 589832 | tf_op jit(solution)/shard_map/ppermute | solution.py:323
  43.0 1.4 %collective-permute-start.16 = (f32[48,640]{1,0:T(8,128)S(1)}, f32[48,640]{1,0:T(8,128)S(1)}, u32[]{:S(2)}, u32[]{:S(2)}) collective-permute-start(f32[48,640]{1,0:T(8,128)S(1)} %convert_add_fusion.mine), channel_id=1, source_target_pairs={{0,2},{2,0},{4,6},{6,4},{8,10},{10,8},{12,14},{14,12},{16,18},{18,... | collective-permute-start | bytes 368648 | tf_op jit(solution)/shard_map/ppermute | solution.py:327

commit v6 on v5

--- a/solution.py
+++ b/solution.py
@@ -39,11 +39,13 @@
 def rows_first(src, flat, dst, rim):
     share, height, _ = src.shape
     zero = jnp.zeros((rim, share, 128), bf16)
-    flat[...] = src[...].astype(f32).reshape(share * height, 128)
+    pitch = height + 8
+    for ch in range(share):
+        flat[ch * pitch : ch * pitch + height] = src[ch].astype(f32)
     dst[0:rim] = zero
     dst[height + rim : height + 2 * rim] = zero
     for h in range(height):
-        dst[h + rim] = flat[pl.ds(h, share, stride=height)].astype(bf16)
+        dst[h + rim] = flat[pl.ds(h, share, stride=pitch)].astype(bf16)
 
 
 def pack_volume_body(nchan, rows, *refs):
@@ -338,7 +340,7 @@
         functools.partial(pack_volume_body, nchan, rows),
         [v_shape] * nchan,
         [
-            pltpu.VMEM((share * height, width), f32),
+            pltpu.VMEM((share * (height + 8), width), f32),
             pltpu.VMEM((height + 4, share, width), bf16),
         ],
         0,
@@ -351,7 +353,7 @@
         functools.partial(pack_rest_body, nchan, rows),
         [u_shape] * nchan,
         [
-            pltpu.VMEM((share * height, width), f32),
+            pltpu.VMEM((share * (height + 8), width), f32),
             pltpu.VMEM((height + 2, share, width), bf16),
         ],
         0,

time: 48.1 us -> 48 us (level)
  transfers between devices with their start and end apart: 17 -> 17, of which waited for: 11 -> 11; matrix products, arithmetic and copies ran while one was open for 0% -> 0% of each run, Pallas kernels for 8% -> 7%
where the time goes in v6:
time: 48 us; the launch traced here: 47.8 us
  starting transfers between devices  20.4 us (42%)
  waiting for transfers between devices  16.6 us (35%)
  Pallas kernels  7.43 us (15%)
  local copies, waits for them, and re-layouts  2.59 us (5%)
  between operations  0.74 us (2%)
    ppermute x3, starting transfers between devices, to_pair(): return lax.ppermute(x, ('space', 'chan'), perm)  7.61 us
    ppermute x5, starting transfers between devices, from_hop(): lax.ppermute(blocks[k], ('space', 'chan'), [(i * nchan + c, (i ^ hop) * n...  6.75 us
    ppermute x5, waiting for transfers between devices, from_hop(): lax.ppermute(blocks[k], ('space', 'chan'), [(i * nchan + c, (i ^ hop) * n...  6.66 us
    ppermute x4, starting transfers between devices, over_chan(): got.append(lax.ppermute(blocks[k - 1], 'chan', perm))  5.81 us
    ppermute x3, waiting for transfers between devices, to_pair(): return lax.ppermute(x, ('space', 'chan'), perm)  5.03 us
    ppermute x4, waiting for transfers between devices, over_chan(): got.append(lax.ppermute(blocks[k - 1], 'chan', perm))  3.1 us
    pallas_call x1, Pallas kernels, shards(): call(functools.partial(forward_body, nchan, rows, step), [a_shape] * ncha...  2.78 us
    unnamed x8, local copies, waits for them, and re-layouts  2.58 us
  transfers between devices with their start and end apart: 17, of which 11 were waited for; matrix products, arithmetic and copies ran while one was open for 0% of the time, Pallas kernels for 7%

profile of v6, /device:TPU:0, one launch (start us, length us, event | category | flops | bytes accessed | tf_op | source)
XLA Modules:
  0.0 47.8 jit_solution(2351709903575788087)
XLA Ops:
  0.6 1.0 %copy-done = bf16[32,1,48,128]{3,2,1,0:T(8,128)(2,1)S(1)} copy-done((bf16[32,1,48,128]{3,2,1,0:T(8,128)(2,1)S(1)}, bf16[32,1,48,128]{3,2,1,0:T(8,128)(2,1)}, u32[]{:S(2)}) %copy-start) | copy-done | bytes 393240
  1.8 3.0 %collective-permute-start = (bf16[28,32,128]{2,1,0:T(8,128)(2,1)S(1)}, bf16[28,32,128]{2,1,0:T(8,128)(2,1)S(1)}, u32[]{:S(2)}, u32[]{:S(2)}) collective-permute-start(bf16[28,32,128]{2,1,0:T(8,128)(2,1)S(1)} %get-tuple-element.20), channel_id=1, source_target_pairs={{0,1},{1,0},{2,3},{3,2},{4,5},{5,4},{6,7},{7,6},{8,9},{9,8},{10,11... | collective-permute-start | bytes 688136 | tf_op jit(solution)/shard_map/ppermute | solution.py:325
  4.9 3.7 %collective-permute-start.1 = (bf16[28,32,128]{2,1,0:T(8,128)(2,1)S(1)}, bf16[28,32,128]{2,1,0:T(8,128)(2,1)S(1)}, u32[]{:S(2)}, u32[]{:S(2)}) collective-permute-start(bf16[28,32,128]{2,1,0:T(8,128)(2,1)S(1)} %get-tuple-element.19.refs_0_), channel_id=1, source_target_pairs={{2,4},{3,5},{6,8},{7,9},{10,12},{11,13},{14,16},{15,17},{18,20},{1... | collective-permute-start | bytes 688136 | tf_op jit(solution)/shard_map/ppermute | solution.py:333
  9.2 0.9 %copy-done.2 = bf16[32,64,3,3,3]{1,0,4,3,2:T(8,128)(2,1)S(1)} copy-done((bf16[32,64,3,3,3]{1,0,4,3,2:T(8,128)(2,1)S(1)}, bf16[32,64,3,3,3]{1,0,4,3,2:T(8,128)(2,1)}, u32[]{:S(2)}) %copy-start.2) | copy-done | bytes 110616
  11.0 2.0 %collective-permute-done.1.refs_4_ = bf16[28,32,128]{2,1,0:T(8,128)(2,1)S(1)} collective-permute-done((bf16[28,32,128]{2,1,0:T(8,128)(2,1)S(1)}, bf16[28,32,128]{2,1,0:T(8,128)(2,1)S(1)}, u32[]{:S(2)}, u32[]{:S(2)}) %collective-permute-start.1) | collective-permute-done | bytes 229408 | tf_op jit(solution)/shard_map/ppermute | solution.py:333
  13.0 3.7 %collective-permute-start.4 = (bf16[28,32,128]{2,1,0:T(8,128)(2,1)S(1)}, bf16[28,32,128]{2,1,0:T(8,128)(2,1)S(1)}, u32[]{:S(2)}, u32[]{:S(2)}) collective-permute-start(bf16[28,32,128]{2,1,0:T(8,128)(2,1)S(1)} %collective-permute-done.refs_1_), channel_id=1, source_target_pairs={{2,4},{3,5},{6,8},{7,9},{10,12},{11,13},{14,16},{15,17},{18,20},{1... | collective-permute-start | bytes 688136 | tf_op jit(solution)/shard_map/ppermute | solution.py:333
  16.7 1.4 %collective-permute-done.5.refs_7_.refs_1_ = bf16[41,32,128]{2,1,0:T(8,128)(2,1)S(1)} collective-permute-done((bf16[41,32,128]{2,1,0:T(8,128)(2,1)S(1)}, bf16[41,32,128]{2,1,0:T(8,128)(2,1)S(1)}, u32[]{:S(2)}, u32[]{:S(2)}) %collective-permute-start.5) | collective-permute-done | bytes 335904 | tf_op jit(solution)/shard_map/ppermute | solution.py:325
  18.2 3.0 %collective-permute-done.4.refs_5_ = bf16[28,32,128]{2,1,0:T(8,128)(2,1)S(1)} collective-permute-done((bf16[28,32,128]{2,1,0:T(8,128)(2,1)S(1)}, bf16[28,32,128]{2,1,0:T(8,128)(2,1)S(1)}, u32[]{:S(2)}, u32[]{:S(2)}) %collective-permute-start.4) | collective-permute-done | bytes 229408 | tf_op jit(solution)/shard_map/ppermute | solution.py:333
  21.2 2.8 %forward.1 = (bf16[24,32,128]{2,1,0:T(8,128)(2,1)S(1)}, bf16[24,32,128]{2,1,0:T(8,128)(2,1)S(1)}, bf16[26,64,128]{2,1,0:T(8,128)(2,1)S(1)}, f32[2,48,640]{2,1,0:T(8,128)S(1)}, bf16[2,48,640]{2,1,0:T(8,128)(2,1)S(1)}) custom-call(bf16[28,32,128]{2,1,0:T(8,128)(2,1)S(1)} %get-tuple-element.19.refs_0_, bf16[28,32,128]{2,1,0:T(8,128)(2,1)S(1)} %collective-permute-done.refs_1_, ...), custom_call_target="tpu_custom_call" | custom-call | flops 1358954496 | bytes 3145728 | tf_op jit(solution)/shard_map/forward/pallas_call | solution.py:381
  24.0 1.3 %collective-permute-done.10 = bf16[2,48,640]{2,1,0:T(8,128)(2,1)S(1)} collective-permute-done((bf16[2,48,640]{2,1,0:T(8,128)(2,1)S(1)}, bf16[2,48,640]{2,1,0:T(8,128)(2,1)S(1)}, u32[]{:S(2)}, u32[]{:S(2)}) %collective-permute-start.10) | collective-permute-done | bytes 122912 | tf_op jit(solution)/shard_map/ppermute | solution.py:329
  25.5 1.7 %collective-permute-start.13 = (bf16[48,640]{1,0:T(8,128)(2,1)S(1)}, bf16[48,640]{1,0:T(8,128)(2,1)S(1)}, u32[]{:S(2)}, u32[]{:S(2)}) collective-permute-start(bf16[48,640]{1,0:T(8,128)(2,1)S(1)} %get-tuple-element.39), channel_id=1, source_target_pairs={{0,9},{1,8},{2,11},{3,10},{4,13},{5,12},{6,15},{7,14},{8,1},{9,0},... | collective-permute-start | bytes 184328 | tf_op jit(solution)/shard_map/ppermute | solution.py:404
  27.1 1.8 %collective-permute-start.11 = (bf16[48,640]{1,0:T(8,128)(2,1)S(1)}, bf16[48,640]{1,0:T(8,128)(2,1)S(1)}, u32[]{:S(2)}, u32[]{:S(2)}) collective-permute-start(bf16[48,640]{1,0:T(8,128)(2,1)S(1)} %get-tuple-element.39), channel_id=1, source_target_pairs={{0,1},{1,0},{2,3},{3,2},{4,5},{5,4},{6,7},{7,6},{8,9},{9,8},{10,11... | collective-permute-start | bytes 184328 | tf_op jit(solution)/shard_map/ppermute | solution.py:404
  29.2 1.0 %collective-permute-done.12 = bf16[48,640]{1,0:T(8,128)(2,1)S(1)} collective-permute-done((bf16[48,640]{1,0:T(8,128)(2,1)S(1)}, bf16[48,640]{1,0:T(8,128)(2,1)S(1)}, u32[]{:S(2)}, u32[]{:S(2)}) %collective-permute-start.12) | collective-permute-done | bytes 61472 | tf_op jit(solution)/shard_map/ppermute | solution.py:404
  30.8 1.1 %collective-permute-done.11 = bf16[48,640]{1,0:T(8,128)(2,1)S(1)} collective-permute-done((bf16[48,640]{1,0:T(8,128)(2,1)S(1)}, bf16[48,640]{1,0:T(8,128)(2,1)S(1)}, u32[]{:S(2)}, u32[]{:S(2)}) %collective-permute-start.11) | collective-permute-done | bytes 61472 | tf_op jit(solution)/shard_map/ppermute | solution.py:404
  31.9 2.4 %collective-permute-start.14 = (bf16[48,640]{1,0:T(8,128)(2,1)S(1)}, bf16[48,640]{1,0:T(8,128)(2,1)S(1)}, u32[]{:S(2)}, u32[]{:S(2)}) collective-permute-start(bf16[48,640]{1,0:T(8,128)(2,1)S(1)} %add_convert_fusion.2), channel_id=1, source_target_pairs={{0,16},{1,17},{2,18},{3,19},{4,20},{5,21},{6,22},{7,23},{8,24},{9,... | collective-permute-start | bytes 184328 | tf_op jit(solution)/shard_map/ppermute | solution.py:404
  35.5 3.1 %collective-permute-done.14 = bf16[48,640]{1,0:T(8,128)(2,1)S(1)} collective-permute-done((bf16[48,640]{1,0:T(8,128)(2,1)S(1)}, bf16[48,640]{1,0:T(8,128)(2,1)S(1)}, u32[]{:S(2)}, u32[]{:S(2)}) %collective-permute-start.14) | collective-permute-done | bytes 61472 | tf_op jit(solution)/shard_map/ppermute | solution.py:404
  38.6 0.8 %collective-permute-start.15 = (bf16[48,640]{1,0:T(8,128)(2,1)S(1)}, bf16[48,640]{1,0:T(8,128)(2,1)S(1)}, u32[]{:S(2)}, u32[]{:S(2)}) collective-permute-start(bf16[48,640]{1,0:T(8,128)(2,1)S(1)} %add_convert_fusion.1), channel_id=1, source_target_pairs={{0,4},{1,5},{2,6},{3,7},{4,0},{5,1},{6,2},{7,3},{8,12},{9,13},{10,... | collective-permute-start | bytes 184328 | tf_op jit(solution)/shard_map/ppermute | solution.py:404
  39.5 1.2 %backward.1 = (bf16[24,32,128]{2,1,0:T(8,128)(2,1)S(1)}, bf16[24,32,128]{2,1,0:T(8,128)(2,1)S(1)}) custom-call(bf16[26,64,128]{2,1,0:T(8,128)(2,1)S(1)} %get-tuple-element.27.refs_0_, bf16[26,64,128]{2,1,0:T(8,128)(2,1)S(1)} %collective-permute-done.7.refs_1_, bf16[26,64,128]{2,1,0:T(8,128)(2,1)S(1)} %collective-permute-done.8.refs_2_, ...), custom_call_target="tpu_custom_call" | custom-call | flops 679477248 | bytes 2359296 | tf_op jit(solution)/shard_map/backward/pallas_call | solution.py:448
  40.6 1.4 %collective-permute-start.9 = (bf16[24,32,128]{2,1,0:T(8,128)(2,1)S(1)}, bf16[24,32,128]{2,1,0:T(8,128)(2,1)S(1)}, u32[]{:S(2)}, u32[]{:S(2)}) collective-permute-start(bf16[24,32,128]{2,1,0:T(8,128)(2,1)S(1)} %get-tuple-element.29), channel_id=1, source_target_pairs={{0,1},{1,0},{2,3},{3,2},{4,5},{5,4},{6,7},{7,6},{8,9},{9,8},{10,11... | collective-permute-start | bytes 589832 | tf_op jit(solution)/shard_map/ppermute | solution.py:325
  42.0 0.9 %collective-permute-done.15 = bf16[48,640]{1,0:T(8,128)(2,1)S(1)} collective-permute-done((bf16[48,640]{1,0:T(8,128)(2,1)S(1)}, bf16[48,640]{1,0:T(8,128)(2,1)S(1)}, u32[]{:S(2)}, u32[]{:S(2)}) %collective-permute-start.15) | collective-permute-done | bytes 61472 | tf_op jit(solution)/shard_map/ppermute | solution.py:404
  43.0 0.9 %unpack_activated.1 = bf16[32,48,128]{2,1,0:T(8,128)(2,1)} custom-call(bf16[24,32,128]{2,1,0:T(8,128)(2,1)S(1)} %get-tuple-element.25.refs_0_, bf16[24,32,128]{2,1,0:T(8,128)(2,1)S(1)} %collective-permute-done.6.refs_1_), custom_call_target="tpu_custom_call" | custom-call | bytes 786432 | tf_op jit(solution)/shard_map/unpack_activated/pallas_call | solution.py:432
  44.3 0.9 %finish.1 = (f32[27,32,64]{2,1,0:T(8,128)}, f32[1,32]{1,0:T(1,128)}) custom-call(f32[48,640]{1,0:T(8,128)S(1)} %convert_add_fusion.mine, f32[48,640]{1,0:T(8,128)S(1)} %collective-permute-done.16.other), custom_call_target="tpu_custom_call" | custom-call | bytes 1048576 | tf_op jit(solution)/shard_map/finish/pallas_call | solution.py:463
  45.3 1.7 %collective-permute-done.9.refs_1_ = bf16[24,32,128]{2,1,0:T(8,128)(2,1)S(1)} collective-permute-done((bf16[24,32,128]{2,1,0:T(8,128)(2,1)S(1)}, bf16[24,32,128]{2,1,0:T(8,128)(2,1)S(1)}, u32[]{:S(2)}, u32[]{:S(2)}) %collective-permute-start.9) | collective-permute-done | bytes 196640 | tf_op jit(solution)/shard_map/ppermute | solution.py:325
  46.9 0.9 %unpack_input_grad.1 = bf16[32,48,128]{2,1,0:T(8,128)(2,1)} custom-call(bf16[24,32,128]{2,1,0:T(8,128)(2,1)S(1)} %get-tuple-element.28.refs_0_, bf16[24,32,128]{2,1,0:T(8,128)(2,1)S(1)} %collective-permute-done.9.refs_1_), custom_call_target="tpu_custom_call" | custom-call | bytes 786432 | tf_op jit(solution)/shard_map/unpack_input_grad/pallas_call | solution.py:432
  (31 shorter events, 4.4 us)
Async XLA Ops:
  0.6 1.0 %copy-start = (bf16[32,1,48,128]{3,2,1,0:T(8,128)(2,1)S(1)}, bf16[32,1,48,128]{3,2,1,0:T(8,128)(2,1)}, u32[]{:S(2)}) copy-start(bf16[32,1,48,128]{3,2,1,0:T(8,128)(2,1)} %param.4) | copy-start | bytes 1179652
  1.6 6.9 %copy-start.1 = (bf16[32,1,48,128]{3,2,1,0:T(8,128)(2,1)S(1)}, bf16[32,1,48,128]{3,2,1,0:T(8,128)(2,1)}, u32[]{:S(2)}) copy-start(bf16[32,1,48,128]{3,2,1,0:T(8,128)(2,1)} %param.7) | copy-start | bytes 1179652
  1.8 9.1 %collective-permute-start = (bf16[28,32,128]{2,1,0:T(8,128)(2,1)S(1)}, bf16[28,32,128]{2,1,0:T(8,128)(2,1)S(1)}, u32[]{:S(2)}, u32[]{:S(2)}) collective-permute-start(bf16[28,32,128]{2,1,0:T(8,128)(2,1)S(1)} %get-tuple-element.20), channel_id=1, source_target_pairs={{0,1},{1,0},{2,3},{3,2},{4,5},{5,4},{6,7},{7,6},{8,9},{9,8},{10,11... | collective-permute-start | bytes 688136 | tf_op jit(solution)/shard_map/ppermute | solution.py:325
  4.9 8.1 %collective-permute-start.1 = (bf16[28,32,128]{2,1,0:T(8,128)(2,1)S(1)}, bf16[28,32,128]{2,1,0:T(8,128)(2,1)S(1)}, u32[]{:S(2)}, u32[]{:S(2)}) collective-permute-start(bf16[28,32,128]{2,1,0:T(8,128)(2,1)S(1)} %get-tuple-element.19.refs_0_), channel_id=1, source_target_pairs={{2,4},{3,5},{6,8},{7,9},{10,12},{11,13},{14,16},{15,17},{18,20},{1... | collective-permute-start | bytes 688136 | tf_op jit(solution)/shard_map/ppermute | solution.py:333
  8.6 0.7 %copy-start.3 = (f32[32]{0:T(128)S(1)}, f32[32]{0:T(128)}, u32[]{:S(2)}) copy-start(f32[32]{0:T(128)} %param.6) | copy-start | bytes 388
  9.2 0.9 %copy-start.2 = (bf16[32,64,3,3,3]{1,0,4,3,2:T(8,128)(2,1)S(1)}, bf16[32,64,3,3,3]{1,0,4,3,2:T(8,128)(2,1)}, u32[]{:S(2)}) copy-start(bf16[32,64,3,3,3]{1,0,4,3,2:T(8,128)(2,1)} %param.5) | copy-start | bytes 331780
  10.4 7.8 %collective-permute-start.5 = (bf16[41,32,128]{2,1,0:T(8,128)(2,1)S(1)}, bf16[41,32,128]{2,1,0:T(8,128)(2,1)S(1)}, u32[]{:S(2)}, u32[]{:S(2)}) collective-permute-start(bf16[41,32,128]{2,1,0:T(8,128)(2,1)S(1)} %get-tuple-element.24), channel_id=1, source_target_pairs={{0,1},{1,0},{2,3},{3,2},{4,5},{5,4},{6,7},{7,6},{8,9},{9,8},{10,11... | collective-permute-start | bytes 1007624 | tf_op jit(solution)/shard_map/ppermute | solution.py:325
  11.0 5.8 %collective-permute-start.2 = (bf16[28,32,128]{2,1,0:T(8,128)(2,1)S(1)}, bf16[28,32,128]{2,1,0:T(8,128)(2,1)S(1)}, u32[]{:S(2)}, u32[]{:S(2)}) collective-permute-start(bf16[28,32,128]{2,1,0:T(8,128)(2,1)S(1)} %get-tuple-element.19.refs_0_), channel_id=1, source_target_pairs={{0,2},{2,0},{4,6},{6,4},{8,10},{10,8},{12,14},{14,12},{16,18},{18,... | collective-permute-start | bytes 688136 | tf_op jit(solution)/shard_map/ppermute | solution.py:329
  13.0 8.1 %collective-permute-start.4 = (bf16[28,32,128]{2,1,0:T(8,128)(2,1)S(1)}, bf16[28,32,128]{2,1,0:T(8,128)(2,1)S(1)}, u32[]{:S(2)}, u32[]{:S(2)}) collective-permute-start(bf16[28,32,128]{2,1,0:T(8,128)(2,1)S(1)} %collective-permute-done.refs_1_), channel_id=1, source_target_pairs={{2,4},{3,5},{6,8},{7,9},{10,12},{11,13},{14,16},{15,17},{18,20},{1... | collective-permute-start | bytes 688136 | tf_op jit(solution)/shard_map/ppermute | solution.py:333
  16.7 4.4 %collective-permute-start.3 = (bf16[28,32,128]{2,1,0:T(8,128)(2,1)S(1)}, bf16[28,32,128]{2,1,0:T(8,128)(2,1)S(1)}, u32[]{:S(2)}, u32[]{:S(2)}) collective-permute-start(bf16[28,32,128]{2,1,0:T(8,128)(2,1)S(1)} %collective-permute-done.refs_1_), channel_id=1, source_target_pairs={{0,2},{2,0},{4,6},{6,4},{8,10},{10,8},{12,14},{14,12},{16,18},{18,... | collective-permute-start | bytes 688136 | tf_op jit(solution)/shard_map/ppermute | solution.py:329
  24.0 1.4 %collective-permute-start.10 = (bf16[2,48,640]{2,1,0:T(8,128)(2,1)S(1)}, bf16[2,48,640]{2,1,0:T(8,128)(2,1)S(1)}, u32[]{:S(2)}, u32[]{:S(2)}) collective-permute-start(bf16[2,48,640]{2,1,0:T(8,128)(2,1)S(1)} %get-tuple-element.31), channel_id=1, source_target_pairs={{0,2},{2,0},{4,6},{6,4},{8,10},{10,8},{12,14},{14,12},{16,18},{18,... | collective-permute-start | bytes 368648 | tf_op jit(solution)/shard_map/ppermute | solution.py:329
  25.4 4.9 %collective-permute-start.12 = (bf16[48,640]{1,0:T(8,128)(2,1)S(1)}, bf16[48,640]{1,0:T(8,128)(2,1)S(1)}, u32[]{:S(2)}, u32[]{:S(2)}) collective-permute-start(bf16[48,640]{1,0:T(8,128)(2,1)S(1)} %get-tuple-element.38), channel_id=1, source_target_pairs={{0,8},{1,9},{2,10},{3,11},{4,12},{5,13},{6,14},{7,15},{8,0},{9,1},... | collective-permute-start | bytes 184328 | tf_op jit(solution)/shard_map/ppermute | solution.py:404
  25.5 5.3 %collective-permute-start.13 = (bf16[48,640]{1,0:T(8,128)(2,1)S(1)}, bf16[48,640]{1,0:T(8,128)(2,1)S(1)}, u32[]{:S(2)}, u32[]{:S(2)}) collective-permute-start(bf16[48,640]{1,0:T(8,128)(2,1)S(1)} %get-tuple-element.39), channel_id=1, source_target_pairs={{0,9},{1,8},{2,11},{3,10},{4,13},{5,12},{6,15},{7,14},{8,1},{9,0},... | collective-permute-start | bytes 184328 | tf_op jit(solution)/shard_map/ppermute | solution.py:404
  27.1 4.8 %collective-permute-start.11 = (bf16[48,640]{1,0:T(8,128)(2,1)S(1)}, bf16[48,640]{1,0:T(8,128)(2,1)S(1)}, u32[]{:S(2)}, u32[]{:S(2)}) collective-permute-start(bf16[48,640]{1,0:T(8,128)(2,1)S(1)} %get-tuple-element.39), channel_id=1, source_target_pairs={{0,1},{1,0},{2,3},{3,2},{4,5},{5,4},{6,7},{7,6},{8,9},{9,8},{10,11... | collective-permute-start | bytes 184328 | tf_op jit(solution)/shard_map/ppermute | solution.py:404
  29.0 10.5 %collective-permute-start.8 = (bf16[26,64,128]{2,1,0:T(8,128)(2,1)S(1)}, bf16[26,64,128]{2,1,0:T(8,128)(2,1)S(1)}, u32[]{:S(2)}, u32[]{:S(2)}) collective-permute-start(bf16[26,64,128]{2,1,0:T(8,128)(2,1)S(1)} %get-tuple-element.27.refs_0_), channel_id=1, source_target_pairs={{2,4},{3,5},{6,8},{7,9},{10,12},{11,13},{14,16},{15,17},{18,20},{1... | collective-permute-start | bytes 1277960 | tf_op jit(solution)/shard_map/ppermute | solution.py:333
  29.2 10.3 %collective-permute-start.7 = (bf16[26,64,128]{2,1,0:T(8,128)(2,1)S(1)}, bf16[26,64,128]{2,1,0:T(8,128)(2,1)S(1)}, u32[]{:S(2)}, u32[]{:S(2)}) collective-permute-start(bf16[26,64,128]{2,1,0:T(8,128)(2,1)S(1)} %get-tuple-element.27.refs_0_), channel_id=1, source_target_pairs={{0,2},{2,0},{4,6},{6,4},{8,10},{10,8},{12,14},{14,12},{16,18},{18,... | collective-permute-start | bytes 1277960 | tf_op jit(solution)/shard_map/ppermute | solution.py:329
  31.9 6.7 %collective-permute-start.14 = (bf16[48,640]{1,0:T(8,128)(2,1)S(1)}, bf16[48,640]{1,0:T(8,128)(2,1)S(1)}, u32[]{:S(2)}, u32[]{:S(2)}) collective-permute-start(bf16[48,640]{1,0:T(8,128)(2,1)S(1)} %add_convert_fusion.2), channel_id=1, source_target_pairs={{0,16},{1,17},{2,18},{3,19},{4,20},{5,21},{6,22},{7,23},{8,24},{9,... | collective-permute-start | bytes 184328 | tf_op jit(solution)/shard_map/ppermute | solution.py:404
  34.7 8.3 %collective-permute-start.6 = (bf16[24,32,128]{2,1,0:T(8,128)(2,1)S(1)}, bf16[24,32,128]{2,1,0:T(8,128)(2,1)S(1)}, u32[]{:S(2)}, u32[]{:S(2)}) collective-permute-start(bf16[24,32,128]{2,1,0:T(8,128)(2,1)S(1)} %get-tuple-element.26), channel_id=1, source_target_pairs={{0,1},{1,0},{2,3},{3,2},{4,5},{5,4},{6,7},{7,6},{8,9},{9,8},{10,11... | collective-permute-start | bytes 589832 | tf_op jit(solution)/shard_map/ppermute | solution.py:325
  38.6 4.3 %collective-permute-start.15 = (bf16[48,640]{1,0:T(8,128)(2,1)S(1)}, bf16[48,640]{1,0:T(8,128)(2,1)S(1)}, u32[]{:S(2)}, u32[]{:S(2)}) collective-permute-start(bf16[48,640]{1,0:T(8,128)(2,1)S(1)} %add_convert_fusion.1), channel_id=1, source_target_pairs={{0,4},{1,5},{2,6},{3,7},{4,0},{5,1},{6,2},{7,3},{8,12},{9,13},{10,... | collective-permute-start | bytes 184328 | tf_op jit(solution)/shard_map/ppermute | solution.py:404
  40.6 6.3 %collective-permute-start.9 = (bf16[24,32,128]{2,1,0:T(8,128)(2,1)S(1)}, bf16[24,32,128]{2,1,0:T(8,128)(2,1)S(1)}, u32[]{:S(2)}, u32[]{:S(2)}) collective-permute-start(bf16[24,32,128]{2,1,0:T(8,128)(2,1)S(1)} %get-tuple-element.29), channel_id=1, source_target_pairs={{0,1},{1,0},{2,3},{3,2},{4,5},{5,4},{6,7},{7,6},{8,9},{9,8},{10,11... | collective-permute-start | bytes 589832 | tf_op jit(solution)/shard_map/ppermute | solution.py:325
  42.9 1.4 %collective-permute-start.16 = (f32[48,640]{1,0:T(8,128)S(1)}, f32[48,640]{1,0:T(8,128)S(1)}, u32[]{:S(2)}, u32[]{:S(2)}) collective-permute-start(f32[48,640]{1,0:T(8,128)S(1)} %convert_add_fusion.mine), channel_id=1, source_target_pairs={{0,2},{2,0},{4,6},{6,4},{8,10},{10,8},{12,14},{14,12},{16,18},{18,... | collective-permute-start | bytes 368648 | tf_op jit(solution)/shard_map/ppermute | solution.py:329

commit v7 on v6

--- a/solution.py
+++ b/solution.py
@@ -425,7 +425,7 @@
             sums = [a + b for a, b in zip(sums[0::2], sums[1::2])]
         return sums[0]
 
-    near = 4 if nspace > 4 else 2
+    near = 2
     total = from_hops(sent, (near,))
 
     def unpack(blocks, name):
@@ -455,7 +455,7 @@
     )(delta, d_sib, d_pair, w_backward)
     ig_got = over_chan(ig[1:])
     hops = [1 << n for n in range(1, nspace.bit_length() - 1) if 1 << n != near]
-    for hop in hops[1:] + hops[:1]:
+    for hop in hops:
         total = from_hops([total.astype(bf16)], (hop,))
     summed = to_sib(total)
 

time: 48 us -> 48 us (level)
    ppermute x5, starting transfers between devices: 6.75 us -> 7.34 us  [from_hop(): lax.ppermute(blocks[k], ('space', 'chan'), [(i * nchan + c, (i ^ hop) * n...]
where the time goes in v7:
time: 48 us; the launch traced here: 47.8 us
  starting transfers between devices  20.7 us (43%)
  waiting for transfers between devices  16.2 us (34%)
  Pallas kernels  7.43 us (15%)
  local copies, waits for them, and re-layouts  2.59 us (5%)
  between operations  0.74 us (2%)
    ppermute x3, starting transfers between devices, to_pair(): return lax.ppermute(x, ('space', 'chan'), perm)  7.61 us
    ppermute x5, starting transfers between devices, from_hop(): lax.ppermute(blocks[k], ('space', 'chan'), [(i * nchan + c, (i ^ hop) * n...  7.34 us
    ppermute x5, waiting for transfers between devices, from_hop(): lax.ppermute(blocks[k], ('space', 'chan'), [(i * nchan + c, (i ^ hop) * n...  6.24 us
    ppermute x4, starting transfers between devices, over_chan(): got.append(lax.ppermute(blocks[k - 1], 'chan', perm))  5.54 us
    ppermute x3, waiting for transfers between devices, to_pair(): return lax.ppermute(x, ('space', 'chan'), perm)  5.03 us
    ppermute x4, waiting for transfers between devices, over_chan(): got.append(lax.ppermute(blocks[k - 1], 'chan', perm))  3.21 us
    pallas_call x1, Pallas kernels, shards(): call(functools.partial(forward_body, nchan, rows, step), [a_shape] * ncha...  2.78 us
    unnamed x8, local copies, waits for them, and re-layouts  2.58 us
  transfers between devices with their start and end apart: 17, of which 11 were waited for; matrix products, arithmetic and copies ran while one was open for 0% of the time, Pallas kernels for 7%

profile of v7, /device:TPU:0, one launch (start us, length us, event | category | flops | bytes accessed | tf_op | source)
XLA Modules:
  0.0 47.8 jit_solution(697498751124766071)
XLA Ops:
  0.6 1.0 %copy-done = bf16[32,1,48,128]{3,2,1,0:T(8,128)(2,1)S(1)} copy-done((bf16[32,1,48,128]{3,2,1,0:T(8,128)(2,1)S(1)}, bf16[32,1,48,128]{3,2,1,0:T(8,128)(2,1)}, u32[]{:S(2)}) %copy-start) | copy-done | bytes 393240
  1.8 3.0 %collective-permute-start = (bf16[28,32,128]{2,1,0:T(8,128)(2,1)S(1)}, bf16[28,32,128]{2,1,0:T(8,128)(2,1)S(1)}, u32[]{:S(2)}, u32[]{:S(2)}) collective-permute-start(bf16[28,32,128]{2,1,0:T(8,128)(2,1)S(1)} %get-tuple-element.20), channel_id=1, source_target_pairs={{0,1},{1,0},{2,3},{3,2},{4,5},{5,4},{6,7},{7,6},{8,9},{9,8},{10,11... | collective-permute-start | bytes 688136 | tf_op jit(solution)/shard_map/ppermute | solution.py:325
  4.9 3.7 %collective-permute-start.1 = (bf16[28,32,128]{2,1,0:T(8,128)(2,1)S(1)}, bf16[28,32,128]{2,1,0:T(8,128)(2,1)S(1)}, u32[]{:S(2)}, u32[]{:S(2)}) collective-permute-start(bf16[28,32,128]{2,1,0:T(8,128)(2,1)S(1)} %get-tuple-element.19.refs_0_), channel_id=1, source_target_pairs={{2,4},{3,5},{6,8},{7,9},{10,12},{11,13},{14,16},{15,17},{18,20},{1... | collective-permute-start | bytes 688136 | tf_op jit(solution)/shard_map/ppermute | solution.py:333
  9.2 0.9 %copy-done.2 = bf16[32,64,3,3,3]{1,0,4,3,2:T(8,128)(2,1)S(1)} copy-done((bf16[32,64,3,3,3]{1,0,4,3,2:T(8,128)(2,1)S(1)}, bf16[32,64,3,3,3]{1,0,4,3,2:T(8,128)(2,1)}, u32[]{:S(2)}) %copy-start.2) | copy-done | bytes 110616
  11.0 2.0 %collective-permute-done.1.refs_4_ = bf16[28,32,128]{2,1,0:T(8,128)(2,1)S(1)} collective-permute-done((bf16[28,32,128]{2,1,0:T(8,128)(2,1)S(1)}, bf16[28,32,128]{2,1,0:T(8,128)(2,1)S(1)}, u32[]{:S(2)}, u32[]{:S(2)}) %collective-permute-start.1) | collective-permute-done | bytes 229408 | tf_op jit(solution)/shard_map/ppermute | solution.py:333
  13.0 3.7 %collective-permute-start.4 = (bf16[28,32,128]{2,1,0:T(8,128)(2,1)S(1)}, bf16[28,32,128]{2,1,0:T(8,128)(2,1)S(1)}, u32[]{:S(2)}, u32[]{:S(2)}) collective-permute-start(bf16[28,32,128]{2,1,0:T(8,128)(2,1)S(1)} %collective-permute-done.refs_1_), channel_id=1, source_target_pairs={{2,4},{3,5},{6,8},{7,9},{10,12},{11,13},{14,16},{15,17},{18,20},{1... | collective-permute-start | bytes 688136 | tf_op jit(solution)/shard_map/ppermute | solution.py:333
  16.7 1.4 %collective-permute-done.5.refs_7_.refs_1_ = bf16[41,32,128]{2,1,0:T(8,128)(2,1)S(1)} collective-permute-done((bf16[41,32,128]{2,1,0:T(8,128)(2,1)S(1)}, bf16[41,32,128]{2,1,0:T(8,128)(2,1)S(1)}, u32[]{:S(2)}, u32[]{:S(2)}) %collective-permute-start.5) | collective-permute-done | bytes 335904 | tf_op jit(solution)/shard_map/ppermute | solution.py:325
  18.2 3.0 %collective-permute-done.4.refs_5_ = bf16[28,32,128]{2,1,0:T(8,128)(2,1)S(1)} collective-permute-done((bf16[28,32,128]{2,1,0:T(8,128)(2,1)S(1)}, bf16[28,32,128]{2,1,0:T(8,128)(2,1)S(1)}, u32[]{:S(2)}, u32[]{:S(2)}) %collective-permute-start.4) | collective-permute-done | bytes 229408 | tf_op jit(solution)/shard_map/ppermute | solution.py:333
  21.2 2.8 %forward.1 = (bf16[24,32,128]{2,1,0:T(8,128)(2,1)S(1)}, bf16[24,32,128]{2,1,0:T(8,128)(2,1)S(1)}, bf16[26,64,128]{2,1,0:T(8,128)(2,1)S(1)}, f32[2,48,640]{2,1,0:T(8,128)S(1)}, bf16[2,48,640]{2,1,0:T(8,128)(2,1)S(1)}) custom-call(bf16[28,32,128]{2,1,0:T(8,128)(2,1)S(1)} %get-tuple-element.19.refs_0_, bf16[28,32,128]{2,1,0:T(8,128)(2,1)S(1)} %collective-permute-done.refs_1_, ...), custom_call_target="tpu_custom_call" | custom-call | flops 1358954496 | bytes 3145728 | tf_op jit(solution)/shard_map/forward/pallas_call | solution.py:381
  24.0 1.3 %collective-permute-done.10 = bf16[2,48,640]{2,1,0:T(8,128)(2,1)S(1)} collective-permute-done((bf16[2,48,640]{2,1,0:T(8,128)(2,1)S(1)}, bf16[2,48,640]{2,1,0:T(8,128)(2,1)S(1)}, u32[]{:S(2)}, u32[]{:S(2)}) %collective-permute-start.10) | collective-permute-done | bytes 122912 | tf_op jit(solution)/shard_map/ppermute | solution.py:329
  25.6 1.5 %collective-permute-start.13 = (bf16[48,640]{1,0:T(8,128)(2,1)S(1)}, bf16[48,640]{1,0:T(8,128)(2,1)S(1)}, u32[]{:S(2)}, u32[]{:S(2)}) collective-permute-start(bf16[48,640]{1,0:T(8,128)(2,1)S(1)} %get-tuple-element.39), channel_id=1, source_target_pairs={{0,5},{1,4},{2,7},{3,6},{4,1},{5,0},{6,3},{7,2},{8,13},{9,12},{10,... | collective-permute-start | bytes 184328 | tf_op jit(solution)/shard_map/ppermute | solution.py:404
  27.1 1.8 %collective-permute-start.11 = (bf16[48,640]{1,0:T(8,128)(2,1)S(1)}, bf16[48,640]{1,0:T(8,128)(2,1)S(1)}, u32[]{:S(2)}, u32[]{:S(2)}) collective-permute-start(bf16[48,640]{1,0:T(8,128)(2,1)S(1)} %get-tuple-element.39), channel_id=1, source_target_pairs={{0,1},{1,0},{2,3},{3,2},{4,5},{5,4},{6,7},{7,6},{8,9},{9,8},{10,11... | collective-permute-start | bytes 184328 | tf_op jit(solution)/shard_map/ppermute | solution.py:404
  29.2 1.0 %collective-permute-done.12 = bf16[48,640]{1,0:T(8,128)(2,1)S(1)} collective-permute-done((bf16[48,640]{1,0:T(8,128)(2,1)S(1)}, bf16[48,640]{1,0:T(8,128)(2,1)S(1)}, u32[]{:S(2)}, u32[]{:S(2)}) %collective-permute-start.12) | collective-permute-done | bytes 61472 | tf_op jit(solution)/shard_map/ppermute | solution.py:404
  30.8 1.1 %collective-permute-done.11 = bf16[48,640]{1,0:T(8,128)(2,1)S(1)} collective-permute-done((bf16[48,640]{1,0:T(8,128)(2,1)S(1)}, bf16[48,640]{1,0:T(8,128)(2,1)S(1)}, u32[]{:S(2)}, u32[]{:S(2)}) %collective-permute-start.11) | collective-permute-done | bytes 61472 | tf_op jit(solution)/shard_map/ppermute | solution.py:404
  31.9 1.4 %collective-permute-start.14 = (bf16[48,640]{1,0:T(8,128)(2,1)S(1)}, bf16[48,640]{1,0:T(8,128)(2,1)S(1)}, u32[]{:S(2)}, u32[]{:S(2)}) collective-permute-start(bf16[48,640]{1,0:T(8,128)(2,1)S(1)} %add_convert_fusion.2), channel_id=1, source_target_pairs={{0,8},{1,9},{2,10},{3,11},{4,12},{5,13},{6,14},{7,15},{8,0},{9,1},... | collective-permute-start | bytes 184328 | tf_op jit(solution)/shard_map/ppermute | solution.py:404
  34.5 2.7 %collective-permute-done.14 = bf16[48,640]{1,0:T(8,128)(2,1)S(1)} collective-permute-done((bf16[48,640]{1,0:T(8,128)(2,1)S(1)}, bf16[48,640]{1,0:T(8,128)(2,1)S(1)}, u32[]{:S(2)}, u32[]{:S(2)}) %collective-permute-start.14) | collective-permute-done | bytes 61472 | tf_op jit(solution)/shard_map/ppermute | solution.py:404
  37.2 2.4 %collective-permute-start.15 = (bf16[48,640]{1,0:T(8,128)(2,1)S(1)}, bf16[48,640]{1,0:T(8,128)(2,1)S(1)}, u32[]{:S(2)}, u32[]{:S(2)}) collective-permute-start(bf16[48,640]{1,0:T(8,128)(2,1)S(1)} %add_convert_fusion.1), channel_id=1, source_target_pairs={{0,16},{1,17},{2,18},{3,19},{4,20},{5,21},{6,22},{7,23},{8,24},{9,... | collective-permute-start | bytes 184328 | tf_op jit(solution)/shard_map/ppermute | solution.py:404
  39.6 1.2 %backward.1 = (bf16[24,32,128]{2,1,0:T(8,128)(2,1)S(1)}, bf16[24,32,128]{2,1,0:T(8,128)(2,1)S(1)}) custom-call(bf16[26,64,128]{2,1,0:T(8,128)(2,1)S(1)} %get-tuple-element.27.refs_0_, bf16[26,64,128]{2,1,0:T(8,128)(2,1)S(1)} %collective-permute-done.7.refs_1_, bf16[26,64,128]{2,1,0:T(8,128)(2,1)S(1)} %collective-permute-done.8.refs_2_, ...), custom_call_target="tpu_custom_call" | custom-call | flops 679477248 | bytes 2359296 | tf_op jit(solution)/shard_map/backward/pallas_call | solution.py:448
  40.8 1.1 %collective-permute-start.9 = (bf16[24,32,128]{2,1,0:T(8,128)(2,1)S(1)}, bf16[24,32,128]{2,1,0:T(8,128)(2,1)S(1)}, u32[]{:S(2)}, u32[]{:S(2)}) collective-permute-start(bf16[24,32,128]{2,1,0:T(8,128)(2,1)S(1)} %get-tuple-element.29), channel_id=1, source_target_pairs={{0,1},{1,0},{2,3},{3,2},{4,5},{5,4},{6,7},{7,6},{8,9},{9,8},{10,11... | collective-permute-start | bytes 589832 | tf_op jit(solution)/shard_map/ppermute | solution.py:325
  41.9 0.9 %collective-permute-done.15 = bf16[48,640]{1,0:T(8,128)(2,1)S(1)} collective-permute-done((bf16[48,640]{1,0:T(8,128)(2,1)S(1)}, bf16[48,640]{1,0:T(8,128)(2,1)S(1)}, u32[]{:S(2)}, u32[]{:S(2)}) %collective-permute-start.15) | collective-permute-done | bytes 61472 | tf_op jit(solution)/shard_map/ppermute | solution.py:404
  42.9 0.9 %unpack_activated.1 = bf16[32,48,128]{2,1,0:T(8,128)(2,1)} custom-call(bf16[24,32,128]{2,1,0:T(8,128)(2,1)S(1)} %get-tuple-element.25.refs_0_, bf16[24,32,128]{2,1,0:T(8,128)(2,1)S(1)} %collective-permute-done.6.refs_1_), custom_call_target="tpu_custom_call" | custom-call | bytes 786432 | tf_op jit(solution)/shard_map/unpack_activated/pallas_call | solution.py:432
  44.2 0.9 %finish.1 = (f32[27,32,64]{2,1,0:T(8,128)}, f32[1,32]{1,0:T(1,128)}) custom-call(f32[48,640]{1,0:T(8,128)S(1)} %convert_add_fusion.mine, f32[48,640]{1,0:T(8,128)S(1)} %collective-permute-done.16.other), custom_call_target="tpu_custom_call" | custom-call | bytes 1048576 | tf_op jit(solution)/shard_map/finish/pallas_call | solution.py:463
  45.1 1.8 %collective-permute-done.9.refs_1_ = bf16[24,32,128]{2,1,0:T(8,128)(2,1)S(1)} collective-permute-done((bf16[24,32,128]{2,1,0:T(8,128)(2,1)S(1)}, bf16[24,32,128]{2,1,0:T(8,128)(2,1)S(1)}, u32[]{:S(2)}, u32[]{:S(2)}) %collective-permute-start.9) | collective-permute-done | bytes 196640 | tf_op jit(solution)/shard_map/ppermute | solution.py:325
  46.9 0.9 %unpack_input_grad.1 = bf16[32,48,128]{2,1,0:T(8,128)(2,1)} custom-call(bf16[24,32,128]{2,1,0:T(8,128)(2,1)S(1)} %get-tuple-element.28.refs_0_, bf16[24,32,128]{2,1,0:T(8,128)(2,1)S(1)} %collective-permute-done.9.refs_1_), custom_call_target="tpu_custom_call" | custom-call | bytes 786432 | tf_op jit(solution)/shard_map/unpack_input_grad/pallas_call | solution.py:432
  (31 shorter events, 4.6 us)
Async XLA Ops:
  0.6 1.0 %copy-start = (bf16[32,1,48,128]{3,2,1,0:T(8,128)(2,1)S(1)}, bf16[32,1,48,128]{3,2,1,0:T(8,128)(2,1)}, u32[]{:S(2)}) copy-start(bf16[32,1,48,128]{3,2,1,0:T(8,128)(2,1)} %param.4) | copy-start | bytes 1179652
  1.6 6.9 %copy-start.1 = (bf16[32,1,48,128]{3,2,1,0:T(8,128)(2,1)S(1)}, bf16[32,1,48,128]{3,2,1,0:T(8,128)(2,1)}, u32[]{:S(2)}) copy-start(bf16[32,1,48,128]{3,2,1,0:T(8,128)(2,1)} %param.7) | copy-start | bytes 1179652
  1.8 9.1 %collective-permute-start = (bf16[28,32,128]{2,1,0:T(8,128)(2,1)S(1)}, bf16[28,32,128]{2,1,0:T(8,128)(2,1)S(1)}, u32[]{:S(2)}, u32[]{:S(2)}) collective-permute-start(bf16[28,32,128]{2,1,0:T(8,128)(2,1)S(1)} %get-tuple-element.20), channel_id=1, source_target_pairs={{0,1},{1,0},{2,3},{3,2},{4,5},{5,4},{6,7},{7,6},{8,9},{9,8},{10,11... | collective-permute-start | bytes 688136 | tf_op jit(solution)/shard_map/ppermute | solution.py:325
  4.9 8.1 %collective-permute-start.1 = (bf16[28,32,128]{2,1,0:T(8,128)(2,1)S(1)}, bf16[28,32,128]{2,1,0:T(8,128)(2,1)S(1)}, u32[]{:S(2)}, u32[]{:S(2)}) collective-permute-start(bf16[28,32,128]{2,1,0:T(8,128)(2,1)S(1)} %get-tuple-element.19.refs_0_), channel_id=1, source_target_pairs={{2,4},{3,5},{6,8},{7,9},{10,12},{11,13},{14,16},{15,17},{18,20},{1... | collective-permute-start | bytes 688136 | tf_op jit(solution)/shard_map/ppermute | solution.py:333
  8.6 0.7 %copy-start.3 = (f32[32]{0:T(128)S(1)}, f32[32]{0:T(128)}, u32[]{:S(2)}) copy-start(f32[32]{0:T(128)} %param.6) | copy-start | bytes 388
  9.2 0.9 %copy-start.2 = (bf16[32,64,3,3,3]{1,0,4,3,2:T(8,128)(2,1)S(1)}, bf16[32,64,3,3,3]{1,0,4,3,2:T(8,128)(2,1)}, u32[]{:S(2)}) copy-start(bf16[32,64,3,3,3]{1,0,4,3,2:T(8,128)(2,1)} %param.5) | copy-start | bytes 331780
  10.4 7.8 %collective-permute-start.5 = (bf16[41,32,128]{2,1,0:T(8,128)(2,1)S(1)}, bf16[41,32,128]{2,1,0:T(8,128)(2,1)S(1)}, u32[]{:S(2)}, u32[]{:S(2)}) collective-permute-start(bf16[41,32,128]{2,1,0:T(8,128)(2,1)S(1)} %get-tuple-element.24), channel_id=1, source_target_pairs={{0,1},{1,0},{2,3},{3,2},{4,5},{5,4},{6,7},{7,6},{8,9},{9,8},{10,11... | collective-permute-start | bytes 1007624 | tf_op jit(solution)/shard_map/ppermute | solution.py:325
  11.0 5.8 %collective-permute-start.2 = (bf16[28,32,128]{2,1,0:T(8,128)(2,1)S(1)}, bf16[28,32,128]{2,1,0:T(8,128)(2,1)S(1)}, u32[]{:S(2)}, u32[]{:S(2)}) collective-permute-start(bf16[28,32,128]{2,1,0:T(8,128)(2,1)S(1)} %get-tuple-element.19.refs_0_), channel_id=1, source_target_pairs={{0,2},{2,0},{4,6},{6,4},{8,10},{10,8},{12,14},{14,12},{16,18},{18,... | collective-permute-start | bytes 688136 | tf_op jit(solution)/shard_map/ppermute | solution.py:329
  13.0 8.1 %collective-permute-start.4 = (bf16[28,32,128]{2,1,0:T(8,128)(2,1)S(1)}, bf16[28,32,128]{2,1,0:T(8,128)(2,1)S(1)}, u32[]{:S(2)}, u32[]{:S(2)}) collective-permute-start(bf16[28,32,128]{2,1,0:T(8,128)(2,1)S(1)} %collective-permute-done.refs_1_), channel_id=1, source_target_pairs={{2,4},{3,5},{6,8},{7,9},{10,12},{11,13},{14,16},{15,17},{18,20},{1... | collective-permute-start | bytes 688136 | tf_op jit(solution)/shard_map/ppermute | solution.py:333
  16.7 4.4 %collective-permute-start.3 = (bf16[28,32,128]{2,1,0:T(8,128)(2,1)S(1)}, bf16[28,32,128]{2,1,0:T(8,128)(2,1)S(1)}, u32[]{:S(2)}, u32[]{:S(2)}) collective-permute-start(bf16[28,32,128]{2,1,0:T(8,128)(2,1)S(1)} %collective-permute-done.refs_1_), channel_id=1, source_target_pairs={{0,2},{2,0},{4,6},{6,4},{8,10},{10,8},{12,14},{14,12},{16,18},{18,... | collective-permute-start | bytes 688136 | tf_op jit(solution)/shard_map/ppermute | solution.py:329
  24.0 1.4 %collective-permute-start.10 = (bf16[2,48,640]{2,1,0:T(8,128)(2,1)S(1)}, bf16[2,48,640]{2,1,0:T(8,128)(2,1)S(1)}, u32[]{:S(2)}, u32[]{:S(2)}) collective-permute-start(bf16[2,48,640]{2,1,0:T(8,128)(2,1)S(1)} %get-tuple-element.31), channel_id=1, source_target_pairs={{0,2},{2,0},{4,6},{6,4},{8,10},{10,8},{12,14},{14,12},{16,18},{18,... | collective-permute-start | bytes 368648 | tf_op jit(solution)/shard_map/ppermute | solution.py:329
  25.4 4.8 %collective-permute-start.12 = (bf16[48,640]{1,0:T(8,128)(2,1)S(1)}, bf16[48,640]{1,0:T(8,128)(2,1)S(1)}, u32[]{:S(2)}, u32[]{:S(2)}) collective-permute-start(bf16[48,640]{1,0:T(8,128)(2,1)S(1)} %get-tuple-element.38), channel_id=1, source_target_pairs={{0,4},{1,5},{2,6},{3,7},{4,0},{5,1},{6,2},{7,3},{8,12},{9,13},{10,... | collective-permute-start | bytes 184328 | tf_op jit(solution)/shard_map/ppermute | solution.py:404
  25.6 5.2 %collective-permute-start.13 = (bf16[48,640]{1,0:T(8,128)(2,1)S(1)}, bf16[48,640]{1,0:T(8,128)(2,1)S(1)}, u32[]{:S(2)}, u32[]{:S(2)}) collective-permute-start(bf16[48,640]{1,0:T(8,128)(2,1)S(1)} %get-tuple-element.39), channel_id=1, source_target_pairs={{0,5},{1,4},{2,7},{3,6},{4,1},{5,0},{6,3},{7,2},{8,13},{9,12},{10,... | collective-permute-start | bytes 184328 | tf_op jit(solution)/shard_map/ppermute | solution.py:404
  27.1 4.8 %collective-permute-start.11 = (bf16[48,640]{1,0:T(8,128)(2,1)S(1)}, bf16[48,640]{1,0:T(8,128)(2,1)S(1)}, u32[]{:S(2)}, u32[]{:S(2)}) collective-permute-start(bf16[48,640]{1,0:T(8,128)(2,1)S(1)} %get-tuple-element.39), channel_id=1, source_target_pairs={{0,1},{1,0},{2,3},{3,2},{4,5},{5,4},{6,7},{7,6},{8,9},{9,8},{10,11... | collective-permute-start | bytes 184328 | tf_op jit(solution)/shard_map/ppermute | solution.py:404
  29.0 10.7 %collective-permute-start.8 = (bf16[26,64,128]{2,1,0:T(8,128)(2,1)S(1)}, bf16[26,64,128]{2,1,0:T(8,128)(2,1)S(1)}, u32[]{:S(2)}, u32[]{:S(2)}) collective-permute-start(bf16[26,64,128]{2,1,0:T(8,128)(2,1)S(1)} %get-tuple-element.27.refs_0_), channel_id=1, source_target_pairs={{2,4},{3,5},{6,8},{7,9},{10,12},{11,13},{14,16},{15,17},{18,20},{1... | collective-permute-start | bytes 1277960 | tf_op jit(solution)/shard_map/ppermute | solution.py:333
  29.2 10.5 %collective-permute-start.7 = (bf16[26,64,128]{2,1,0:T(8,128)(2,1)S(1)}, bf16[26,64,128]{2,1,0:T(8,128)(2,1)S(1)}, u32[]{:S(2)}, u32[]{:S(2)}) collective-permute-start(bf16[26,64,128]{2,1,0:T(8,128)(2,1)S(1)} %get-tuple-element.27.refs_0_), channel_id=1, source_target_pairs={{0,2},{2,0},{4,6},{6,4},{8,10},{10,8},{12,14},{14,12},{16,18},{18,... | collective-permute-start | bytes 1277960 | tf_op jit(solution)/shard_map/ppermute | solution.py:329
  31.9 5.2 %collective-permute-start.14 = (bf16[48,640]{1,0:T(8,128)(2,1)S(1)}, bf16[48,640]{1,0:T(8,128)(2,1)S(1)}, u32[]{:S(2)}, u32[]{:S(2)}) collective-permute-start(bf16[48,640]{1,0:T(8,128)(2,1)S(1)} %add_convert_fusion.2), channel_id=1, source_target_pairs={{0,8},{1,9},{2,10},{3,11},{4,12},{5,13},{6,14},{7,15},{8,0},{9,1},... | collective-permute-start | bytes 184328 | tf_op jit(solution)/shard_map/ppermute | solution.py:404
  33.7 9.3 %collective-permute-start.6 = (bf16[24,32,128]{2,1,0:T(8,128)(2,1)S(1)}, bf16[24,32,128]{2,1,0:T(8,128)(2,1)S(1)}, u32[]{:S(2)}, u32[]{:S(2)}) collective-permute-start(bf16[24,32,128]{2,1,0:T(8,128)(2,1)S(1)} %get-tuple-element.26), channel_id=1, source_target_pairs={{0,1},{1,0},{2,3},{3,2},{4,5},{5,4},{6,7},{7,6},{8,9},{9,8},{10,11... | collective-permute-start | bytes 589832 | tf_op jit(solution)/shard_map/ppermute | solution.py:325
  37.2 5.6 %collective-permute-start.15 = (bf16[48,640]{1,0:T(8,128)(2,1)S(1)}, bf16[48,640]{1,0:T(8,128)(2,1)S(1)}, u32[]{:S(2)}, u32[]{:S(2)}) collective-permute-start(bf16[48,640]{1,0:T(8,128)(2,1)S(1)} %add_convert_fusion.1), channel_id=1, source_target_pairs={{0,16},{1,17},{2,18},{3,19},{4,20},{5,21},{6,22},{7,23},{8,24},{9,... | collective-permute-start | bytes 184328 | tf_op jit(solution)/shard_map/ppermute | solution.py:404
  40.8 6.1 %collective-permute-start.9 = (bf16[24,32,128]{2,1,0:T(8,128)(2,1)S(1)}, bf16[24,32,128]{2,1,0:T(8,128)(2,1)S(1)}, u32[]{:S(2)}, u32[]{:S(2)}) collective-permute-start(bf16[24,32,128]{2,1,0:T(8,128)(2,1)S(1)} %get-tuple-element.29), channel_id=1, source_target_pairs={{0,1},{1,0},{2,3},{3,2},{4,5},{5,4},{6,7},{7,6},{8,9},{9,8},{10,11... | collective-permute-start | bytes 589832 | tf_op jit(solution)/shard_map/ppermute | solution.py:325
  42.8 1.4 %collective-permute-start.16 = (f32[48,640]{1,0:T(8,128)S(1)}, f32[48,640]{1,0:T(8,128)S(1)}, u32[]{:S(2)}, u32[]{:S(2)}) collective-permute-start(f32[48,640]{1,0:T(8,128)S(1)} %convert_add_fusion.mine), channel_id=1, source_target_pairs={{0,2},{2,0},{4,6},{6,4},{8,10},{10,8},{12,14},{14,12},{16,18},{18,... | collective-permute-start | bytes 368648 | tf_op jit(solution)/shard_map/ppermute | solution.py:329
